TPU v7x, 32 devices: a whole 2x2x4 slice. The times are simulated.
32 devices in a mesh: rep: 16 (over z, x, core), shard: 2 (over y).
Axes of the slice: x: 2, y: 2, z: 4, core: 2. Of those that a mesh axis runs over, the one named last changes fastest.
Arguments:
- tokens: bfloat16 [4096, 1024], P(('rep', 'shard')), may hold values from -6 to 6
- cotangent: bfloat16 [4096, 1024], P(('rep', 'shard')), may hold values from -6 to 6
- lengths: int32 [32], P(('rep', 'shard')), may hold values from 16 to 128, as said below
- qkv_weight: bfloat16 [1024, 3072], P('shard'), may hold values from -0.1875 to 0.1875
- qkv_bias: bfloat16 [3072], P('shard'), may hold values from -1 to 1
- dense_weight: bfloat16 [1024, 1024], P('shard'), may hold values from -1 to 1
- dense_bias: bfloat16 [1024], P('shard'), may hold values from -1 to 1
- in_weight: bfloat16 [1024, 4096], P('shard'), may hold values from -0.1875 to 0.1875
- in_bias: bfloat16 [4096], P('shard'), may hold values from -1 to 1
- out_weight: bfloat16 [4096, 1024], P('shard'), may hold values from -0.09375 to 0.09375
- out_bias: bfloat16 [1024], P('shard'), may hold values from -1 to 1
- norm1_gain: bfloat16 [1024], P('shard'), may hold values from 0.5 to 1.5
- norm1_bias: bfloat16 [1024], P('shard'), may hold values from -1 to 1
- norm2_gain: bfloat16 [1024], P('shard'), may hold values from 0.5 to 1.5
- norm2_bias: bfloat16 [1024], P('shard'), may hold values from -1 to 1
Outputs:
- result: bfloat16 [4096, 1024], P(('rep', 'shard'))
- grad_tokens: bfloat16 [4096, 1024], P(('rep', 'shard'))
- grad_qkv_weight: float32 [1024, 3072], P('shard')
- grad_qkv_bias: float32 [3072], P('shard')
- grad_dense_weight: float32 [1024, 1024], P('shard')
- grad_dense_bias: float32 [1024], P('shard')
- grad_in_weight: float32 [1024, 4096], P('shard')
- grad_in_bias: float32 [4096], P('shard')
- grad_out_weight: float32 [4096, 1024], P('shard')
- grad_out_bias: float32 [1024], P('shard')
- grad_norm1_gain: float32 [1024], P('shard')
- grad_norm1_bias: float32 [1024], P('shard')
- grad_norm2_gain: float32 [1024], P('shard')
- grad_norm2_bias: float32 [1024], P('shard')
Inputs may be any that keep to these rules, and one draw needn't show every extreme that they name: `lengths`: each device's sequence has a length of its own; in every draw some device's sequence fills all 128 slots.
All inputs are finite; a program needn't handle non-finite values.
Results may differ from a plain program's by a relative error of at most 0.0084.
Values may be sent and summed in bfloat16 or wider, within the bound.
No kernel may reach another device: no remote copies, remote signals or barrier semaphores. Data moves between devices by JAX's collectives and lax.ppermute only.
A program may use at most 192 MiB of HBM per device.

v0:
```python
import jax
import jax.numpy as jnp
import numpy as np
from jax import lax
from jax.experimental import pallas as pl
from jax.experimental.pallas import tpu as pltpu
from jax.sharding import PartitionSpec as P

HEAD_DIM = 64
ROT = 16
F32 = jnp.float32
BF16 = jnp.bfloat16
EXTRA = 16


def rotary(values, turn):
    seq_rows = values.shape[-2]
    half = ROT // 2
    inverse = 10000.0 ** (-(2.0 * jnp.arange(half).astype(F32)) / ROT)
    angles = jnp.arange(seq_rows).astype(F32)[:, None] * inverse[None, :]
    cosine = jnp.cos(angles)
    sine = jnp.sin(angles) * turn
    first = values[..., :half]
    second = values[..., half:ROT]
    return jnp.concatenate(
        [first * cosine - second * sine, second * cosine + first * sine, values[..., ROT:]],
        axis=-1,
    )


def dot(left, right):
    return jnp.dot(left, right, preferred_element_type=F32)


def dot_nt(left, right):
    return lax.dot_general(left, right, (((1,), (1,)), ((), ())), preferred_element_type=F32)


def dot_tn(left, right):
    return lax.dot_general(left, right, (((0,), (0,)), ((), ())), preferred_element_type=F32)


def plan(mesh_shape, heads):
    shards, reps = mesh_shape["shard"], mesh_shape["rep"]
    split = 1
    while split < 4 and reps % (2 * split) == 0 and heads % (2 * split * shards) == 0:
        split *= 2
    return shards, reps, split


def make(mesh):
    def on_device(
        tokens,
        cotangent,
        lengths,
        qkv_weight,
        qkv_bias,
        dense_weight,
        dense_bias,
        in_weight,
        in_bias,
        out_weight,
        out_bias,
        norm1_gain,
        norm1_bias,
        norm2_gain,
        norm2_bias,
    ):
        seq_rows, width = tokens.shape
        heads = width // HEAD_DIM
        shards, reps, split = plan(dict(mesh.shape), heads)
        lines = reps // split
        group = shards * split
        owned = width // shards
        hidden = in_weight.shape[1]
        part_f = hidden // group
        part_h = width // group
        own_heads = part_h // HEAD_DIM
        shard = lax.axis_index("shard")
        rep = lax.axis_index("rep")
        slot = lax.rem(rep, split)
        line = rep // split
        block = shard * split + slot
        bits = []
        bit = split // 2
        while bit:
            bits.append(bit)
            bit //= 2

        def swap_rep(values, bit):
            return lax.ppermute(values, "rep", [(i, i ^ bit) for i in range(reps)])

        def swap_shard(values):
            return lax.ppermute(values, "shard", [(0, 1), (1, 0)])

        def gather_shard(values):
            if shards == 1:
                return values
            if shards == 2:
                return jnp.concatenate([values, swap_shard(values)], axis=0)
            return lax.all_gather(values, "shard", axis=0, tiled=True)

        def gather_rep(values):
            for bit in bits:
                values = jnp.concatenate([values, swap_rep(values, bit)], axis=0)
            return values

        def scatter_sum(values):
            for bit in reversed(bits):
                half = values.shape[0] // 2
                values = values[:half] + swap_rep(values[half:].astype(BF16), bit).astype(F32)
            if shards == 2:
                half = values.shape[0] // 2
                values = values[:half] + swap_shard(values[half:].astype(BF16)).astype(F32)
            elif shards > 2:
                values = lax.psum_scatter(
                    values.astype(BF16), "shard", scatter_dimension=0, tiled=True
                ).astype(F32)
            return values

        def ordered(mine, other, flag, axis):
            first = jnp.where(flag, other, mine)
            second = jnp.where(flag, mine, other)
            return jnp.concatenate([first, second], axis=axis)

        def columns_of(weight, parts, size):
            rows = weight.shape[0]
            cut = weight.reshape(rows, parts, group, size)

            def piece(at):
                return lax.dynamic_slice_in_dim(cut, at, 1, 2).reshape(rows, parts * size)

            if shards == 1:
                return piece(block)
            if shards == 2:
                other = swap_shard(piece((1 - shard) * split + slot))
                return ordered(piece(block), other, shard == 1, 0)
            picked = jnp.stack([piece(s * split + slot) for s in range(shards)], axis=0)
            return lax.all_to_all(picked, "shard", 0, 0, tiled=True).reshape(
                rows * shards, parts * size
            )

        def rows_exchange(grad):
            if shards == 1:
                return [grad]
            if shards == 2:
                mine = lax.dynamic_slice_in_dim(grad, shard * owned, owned, 0)
                other = swap_shard(lax.dynamic_slice_in_dim(grad, (1 - shard) * owned, owned, 0))
                return [jnp.where(shard == 1, other, mine), jnp.where(shard == 1, mine, other)]
            got = lax.all_to_all(grad, "shard", 0, 0, tiled=True)
            return [got[s * owned : (s + 1) * owned] for s in range(shards)]

        length = lengths[0]
        live = (jnp.arange(seq_rows) < length).astype(F32)[:, None]
        branch = (live * cotangent.astype(F32)).astype(BF16)
        halves = [dense_bias, out_bias, norm1_gain, norm1_bias, norm2_gain, norm2_bias]
        params = jnp.concatenate([qkv_bias] + halves)
        params = jnp.pad(params, (0, 8 * width - params.shape[0])).reshape(8, width)
        length_rows = jnp.broadcast_to(length.astype(BF16), (EXTRA - 8, width))
        packed = jnp.concatenate([tokens, params, length_rows], axis=0)
        packed = gather_shard(packed)
        branch_all = gather_shard(branch)
        in_w = columns_of(in_weight, 1, part_f)
        packed_all = gather_rep(packed).reshape(group, seq_rows + EXTRA, width)
        branch_all = gather_rep(branch_all)
        qkv_w = columns_of(qkv_weight, 3, part_h)

        by_shard = packed.reshape(shards, seq_rows + EXTRA, width)[:, seq_rows : seq_rows + 8]
        by_shard = by_shard.reshape(shards, 8 * width)
        if shards == 2:
            by_shard = jnp.where(shard == 1, by_shard[::-1], by_shard)

        def whole(at, size):
            return by_shard[:, at : at + size].reshape(shards * size).astype(F32)

        qkv_b = whole(0, 3 * owned)
        at = 3 * owned
        full = []
        for _ in halves:
            full.append(whole(at, owned))
            at += owned
        dense_b, out_b, gain_one, shift_one, gain_two, shift_two = full
        all_lengths = packed_all[:, seq_rows + 8, 0].astype(jnp.int32)
        rows = group * seq_rows
        values = packed_all[:, :seq_rows].reshape(rows, width).astype(F32)

        centre = values - jnp.mean(values, axis=-1, keepdims=True)
        spread = jnp.mean(centre * centre, axis=-1, keepdims=True)
        root = lax.rsqrt(spread + 1e-05)
        xhat = centre * root
        normed = (xhat * gain_one + shift_one).astype(BF16)
        normed_two = (xhat * gain_two + shift_two).astype(BF16)

        out_w = lax.dynamic_slice_in_dim(out_weight, slot * part_f, part_f, 0)
        in_b = lax.dynamic_slice_in_dim(in_bias, slot * part_f, part_f, 0).astype(F32)
        before = dot(normed_two, in_w) + in_b
        cdf = 0.5 * (1.0 + lax.erf(before * (0.5**0.5)))
        active = (before * cdf).astype(BF16)
        slope = cdf + before * jnp.exp(-0.5 * before * before) * 0.3989422804014327
        grad_before = (dot_nt(branch_all, out_w) * slope).astype(BF16)
        grad_out_w = dot_tn(active, branch_all).astype(BF16)
        grad_in_w = dot_tn(normed_two, grad_before).astype(BF16)
        grad_two = dot_nt(grad_before, in_w)

        scaling = HEAD_DIM ** (-0.5)
        bias = lax.dynamic_slice_in_dim(qkv_b.reshape(3, group, part_h), block, 1, 1)
        joint = dot(normed, qkv_w) + bias.reshape(3 * part_h)
        split_joint = joint.reshape(group, seq_rows, 3, own_heads, HEAD_DIM).transpose(2, 0, 3, 1, 4)
        query = rotary(split_joint[0], 1.0).astype(BF16)
        keys = rotary(split_joint[1], 1.0).astype(BF16)
        vals = split_joint[2].astype(BF16)
        position = jnp.arange(seq_rows)
        allowed = (position[None, :] <= position[:, None])[None] & (
            position[None, None, :] < all_lengths[:, None, None]
        )
        scores = jnp.einsum("bhpd,bhqd->bhpq", query, keys, preferred_element_type=F32) * scaling
        scores = jnp.where(allowed[:, None], scores, -1e30)
        raised = jnp.exp(scores - jnp.max(scores, axis=-1, keepdims=True))
        exact = raised / jnp.sum(raised, axis=-1, keepdims=True)
        probs = exact.astype(BF16)
        context = jnp.einsum("bhpq,bhqd->bhpd", probs, vals, preferred_element_type=F32)
        context = context.astype(BF16).transpose(0, 2, 1, 3).reshape(rows, part_h)
        dense_w = lax.dynamic_slice_in_dim(dense_weight, slot * part_h, part_h, 0)
        mixed = scatter_sum(dot(active, out_w) + dot(context, dense_w))
        result = (tokens.astype(F32) + live * (mixed + dense_b + out_b)).astype(BF16)

        grad_context = dot_nt(branch_all, dense_w).astype(BF16)
        grad_dense_w = dot_tn(context, branch_all).astype(BF16)
        grad_context = grad_context.reshape(group, seq_rows, own_heads, HEAD_DIM).transpose(0, 2, 1, 3)
        grad_probs = jnp.einsum(
            "bhpd,bhqd->bhpq", grad_context, vals, preferred_element_type=F32
        )
        grad_vals = jnp.einsum("bhpq,bhpd->bhqd", probs, grad_context, preferred_element_type=F32)
        grad_scores = (
            exact * (grad_probs - jnp.sum(grad_probs * exact, axis=-1, keepdims=True))
        ).astype(BF16)
        grad_query = jnp.einsum("bhpq,bhqd->bhpd", grad_scores, keys, preferred_element_type=F32)
        grad_keys = jnp.einsum("bhpq,bhpd->bhqd", grad_scores, query, preferred_element_type=F32)
        grad_joint = jnp.stack(
            [rotary(grad_query * scaling, -1.0), rotary(grad_keys * scaling, -1.0), grad_vals]
        ).astype(BF16)
        grad_joint = grad_joint.transpose(1, 3, 0, 2, 4).reshape(rows, 3 * part_h)
        grad_qkv_w = dot_tn(normed, grad_joint).astype(BF16)
        grad_one = dot_nt(grad_joint, qkv_w)

        inner = scatter_sum(grad_one * gain_one + grad_two * gain_two)
        own_xhat = xhat[:seq_rows] if shards <= 2 else None
        if own_xhat is None:
            own_xhat = lax.dynamic_slice_in_dim(xhat, shard * seq_rows, seq_rows, 0)
            own_root = lax.dynamic_slice_in_dim(root, shard * seq_rows, seq_rows, 0)
        else:
            own_root = root[:seq_rows]
        inner = (
            inner
            - jnp.mean(inner, axis=-1, keepdims=True)
            - own_xhat * jnp.mean(inner * own_xhat, axis=-1, keepdims=True)
        ) * own_root
        grad_tokens = (cotangent.astype(F32) + inner).astype(BF16)

        in_sum = jnp.sum(grad_before.astype(F32), axis=0)
        qkv_sum = jnp.sum(grad_joint.astype(F32), axis=0).reshape(3, 1, part_h)
        vectors = jnp.concatenate(
            [
                jnp.sum(grad_one * xhat, axis=0),
                jnp.sum(grad_one, axis=0),
                jnp.sum(grad_two * xhat, axis=0),
                jnp.sum(grad_two, axis=0),
                jnp.sum(branch.astype(F32), axis=0),
                lax.dynamic_update_slice_in_dim(jnp.zeros((hidden,), F32), in_sum, block * part_f, 0),
                lax.dynamic_update_slice_in_dim(
                    jnp.zeros((3, group, part_h), F32), qkv_sum, block, 1
                ).reshape(3 * width),
            ]
        )
        vectors = lax.psum(vectors, ("rep", "shard"))

        def own_part(at, size):
            piece = size // shards
            return lax.dynamic_slice_in_dim(vectors, at + shard * piece, piece, 0)

        in_parts = rows_exchange(grad_in_w)
        qkv_parts = rows_exchange(grad_qkv_w)
        chunks = [grad_out_w] + in_parts + [grad_dense_w] + qkv_parts
        if lines == 4:
            inner_line = (line == 1) | (line == 2)

            def line_permute(values, pairs):
                return lax.ppermute(
                    values,
                    "rep",
                    [(a * split + i, b * split + i) for a, b in pairs for i in range(split)],
                )

            summed = []
            for chunk in chunks:
                got = line_permute(chunk, [(0, 1), (3, 2)])
                near = lax.optimization_barrier((chunk.astype(F32) + got.astype(F32)).astype(BF16))
                got = line_permute(near, [(1, 2), (2, 1)])
                both = lax.optimization_barrier((near.astype(F32) + got.astype(F32)).astype(BF16))
                got = line_permute(both, [(1, 0), (2, 3)])
                summed.append(jnp.where(inner_line, both, got))
        else:
            groups = [[a * split + i for a in range(lines)] for i in range(split)]
            summed = [lax.psum(c, "rep", axis_index_groups=groups) for c in chunks]

        def gather_slots(values):
            values = values[None]
            for bit in reversed(bits):
                values = ordered(values, swap_rep(values, bit), (slot & bit) != 0, 0)
            return values

        summed = [gather_slots(c) for c in summed]
        total_out = summed[0].reshape(split * part_f, width).astype(F32)
        total_in = jnp.stack(summed[1 : 1 + shards])
        total_in = total_in.transpose(2, 0, 1, 3).reshape(owned, hidden).astype(F32)
        total_dense = summed[1 + shards].reshape(split * part_h, width).astype(F32)
        total_qkv = jnp.stack(summed[2 + shards :]).reshape(shards, split, owned, 3, part_h)
        total_qkv = total_qkv.transpose(2, 3, 0, 1, 4).reshape(owned, 3 * width).astype(F32)
        at_in = 5 * width
        at_qkv = at_in + hidden
        out_sum = own_part(4 * width, width)
        return (
            result,
            grad_tokens,
            total_qkv,
            own_part(at_qkv, 3 * width),
            total_dense,
            out_sum,
            total_in,
            own_part(at_in, hidden),
            total_out,
            out_sum,
            own_part(0, width),
            own_part(width, width),
            own_part(2 * width, width),
            own_part(3 * width, width),
        )

    return on_device


GROUP = 8
SPLIT = 4
LINES = 4
TAIL = 16
ANY = pl.BlockSpec(memory_space=pl.ANY)
SCALAR = pl.BlockSpec(memory_space=pltpu.SMEM)
WHOLE = pl.BlockSpec(memory_space=pltpu.VMEM)
LIMIT = 48 * 2**20
COST = pl.CostEstimate(flops=1024, bytes_accessed=1024, transcendentals=0)


def shaped(shape, dtype=BF16):
    return jax.ShapeDtypeStruct(shape, dtype)


def call(kernel, name, ins, outs, scratch=()):
    return pl.pallas_call(
        kernel,
        out_shape=[shape for shape, _ in outs],
        in_specs=[spec for _, spec in ins],
        out_specs=[spec for _, spec in outs],
        scratch_shapes=list(scratch),
        compiler_params=pltpu.CompilerParams(vmem_limit_bytes=LIMIT),
        cost_estimate=COST,
        name=name,
    )(*[array for array, _ in ins])


class Copies:
    def __init__(self, sems):
        self.sems, self.used = sems, 0

    def start(self, source, target):
        copy = pltpu.make_async_copy(source, target, self.sems.at[self.used])
        self.used += 1
        copy.start()
        return copy


def place_of():
    shard = lax.axis_index("shard")
    slot = lax.rem(lax.axis_index("rep"), SPLIT)
    return shard, slot, shard * SPLIT + slot


def span(at, size):
    return pl.ds(pl.multiple_of(at * size, size), size)


def pack_kernel(length, tok, cot, in_bias, qb, db, ob, g1, b1, g2, b2, in_weight, qkv_weight,
                packed, total, in_b, in_give, qkv_give, tok_v, cot_v, ib_v, qb_v, *rest):
    vecs, sems = rest[:-1], rest[-1]
    shard, slot, _ = place_of()
    twin = (1 - shard) * SPLIT + slot
    rows, width = tok_v.shape
    owned = vecs[0].shape[0]
    part_f, part_h = in_give.shape[1], qkv_give.shape[1] // 3
    copies = Copies(sems)
    first = [copies.start(tok, tok_v), copies.start(cot, cot_v), copies.start(in_bias, ib_v)]
    first.append(copies.start(qb, qb_v))
    first += [copies.start(a, b) for a, b in zip((db, ob, g1, b1, g2, b2), vecs)]
    given = [copies.start(in_weight.at[:, span(twin, part_f)], in_give)]
    for i in range(3):
        cols = pl.ds(pl.multiple_of(i * width + twin * part_h, part_h), part_h)
        target = qkv_give.at[:, i * part_h : (i + 1) * part_h]
        given.append(copies.start(qkv_weight.at[:, cols], target))
    for copy in first:
        copy.wait()
    live = lax.broadcasted_iota(jnp.int32, (rows, width), 0) < length[0]
    kept = jnp.where(live, cot_v[...].astype(F32), 0.0)
    packed[rows + TAIL :, :] = kept.astype(BF16)
    total[...] = jnp.sum(kept, axis=0, keepdims=True)
    packed[0:rows, :] = tok_v[...]
    whole = qb_v[...].astype(F32).reshape(1, 3 * owned)
    lines = [whole[:, i * owned : (i + 1) * owned] for i in range(3)]
    lines += [ref[...].astype(F32).reshape(1, owned) for ref in vecs]
    lines.append(jnp.full((TAIL - 9, owned), length[0].astype(F32)))
    packed[rows : rows + TAIL, 0:owned] = jnp.concatenate(lines, axis=0).astype(BF16)
    packed[rows : rows + TAIL, owned:width] = jnp.zeros((TAIL, width - owned), BF16)
    bias = ib_v[...].astype(F32).reshape(1, SPLIT * part_f)
    in_b[...] = sum(
        jnp.where(slot == i, bias[:, i * part_f : (i + 1) * part_f], 0.0) for i in range(SPLIT)
    )
    for copy in given:
        copy.wait()


def hidden_kernel(*refs):
    pieces, refs = refs[:GROUP], refs[GROUP:]
    (in_weight, in_got, out_weight, in_b, normed_o, xhat_o, active_o, grad_o, branch_o, out_a, out_b,
     own_o, other_o, params, lens, in_sum, every, branch, tails, w_full, out_w, normed, normed_two,
     xhat, active, slope, grad_before, grad_out, own, other, sems) = refs
    shard, slot, block = place_of()
    rows = pieces[0].shape[0] - TAIL >> 1
    owned, part = in_got.shape
    copies = Copies(sems)
    edge = [copies.start(p.at[rows : rows + TAIL, :], tails.at[i]) for i, p in enumerate(pieces)]
    first = [copies.start(p.at[0:rows, :], every.at[i * rows : (i + 1) * rows, :]) for i, p in enumerate(pieces)]
    first.append(copies.start(in_weight.at[:, span(block, part)], w_full.at[span(shard, owned), :]))
    first.append(copies.start(in_got, w_full.at[span(1 - shard, owned), :]))
    late = [copies.start(p.at[rows + TAIL :, :], branch.at[i * rows : (i + 1) * rows, :]) for i, p in enumerate(pieces)]
    late.append(copies.start(out_weight.at[span(slot, part), :], out_w))
    for copy in edge:
        copy.wait()
    params[:, span(shard, owned)] = tails[0, :, 0:owned].astype(F32)
    params[:, span(1 - shard, owned)] = tails[1, :, 0:owned].astype(F32)
    for i in range(GROUP):
        lens[i * 8 : (i + 1) * 8, :] = tails[i, :, 0:128].astype(F32)[8:]
    g1, b1, g2, b2 = (params[i : i + 1, :] for i in range(5, 9))
    for copy in first:
        copy.wait()
    step = 256

    def forward(i, carry):
        at = span(i, step)
        values = every[at, :].astype(F32)
        centre = values - jnp.mean(values, axis=-1, keepdims=True)
        spread = jnp.mean(centre * centre, axis=-1, keepdims=True)
        hat = centre * lax.rsqrt(spread + 1e-05)
        xhat[at, :] = hat.astype(BF16)
        normed[at, :] = (hat * g1 + b1).astype(BF16)
        two = (hat * g2 + b2).astype(BF16)
        normed_two[at, :] = two
        before = dot(two, w_full[...]) + in_b[...]
        cdf = 0.5 * (1.0 + lax.erf(before * (0.5**0.5)))
        active[at, :] = (before * cdf).astype(BF16)
        slope[at, :] = cdf + before * jnp.exp(-0.5 * before * before) * 0.3989422804014327
        return carry

    lax.fori_loop(0, GROUP * rows // step, forward, 0)
    done = [copies.start(normed, normed_o), copies.start(xhat, xhat_o), copies.start(active, active_o)]
    for copy in late:
        copy.wait()
    done.append(copies.start(branch, branch_o))

    def out_grad(j, carry):
        grad_out[span(j, step), :] = dot_tn(active[:, span(j, step)], branch[...]).astype(BF16)
        return carry

    lax.fori_loop(0, part // step, out_grad, 0)
    done.append(copies.start(grad_out.at[0 : part // 2, :], out_a))
    done.append(copies.start(grad_out.at[part // 2 :, :], out_b))
    in_sum[...] = jnp.zeros_like(in_sum)

    def back(i, carry):
        at = span(i, step)
        grad = (dot_nt(branch[at, :], out_w[...]) * slope[at, :]).astype(BF16)
        grad_before[at, :] = grad
        in_sum[...] += jnp.sum(grad.astype(F32), axis=0, keepdims=True)
        return carry

    lax.fori_loop(0, GROUP * rows // step, back, 0)
    done.append(copies.start(grad_before, grad_o))
    for ref, target, where in ((other, other_o, 1 - shard), (own, own_o, shard)):

        def weight(j, carry, ref=ref, where=where):
            cols = span(where * (owned // step) + j, step)
            ref[span(j, step), :] = dot_tn(normed_two[:, cols], grad_before[...]).astype(BF16)
            return carry

        lax.fori_loop(0, owned // step, weight, 0)
        done.append(copies.start(ref, target))
    for copy in done:
        copy.wait()


def turn(values, tables, back):
    cosine, low, high = tables
    width = values.shape[1]
    ahead = pltpu.roll(values, width - ROT // 2, 1)
    behind = pltpu.roll(values, ROT // 2, 1)
    moved = ahead * low + behind * high
    return values * cosine - moved if back else values * cosine + moved


def attention_kernel(last, *refs):
    (normed, branch, active, grad_before, xhat, lens, qkv_weight, qkv_got, dense_weight, out_weight,
     in_weight, in_got, params, cosine, low, high), refs = refs[:16], refs[16:]
    if last:
        (joint_held, dense_held, sums_held, jsum_held, in_sum, own_sum), refs = refs[:6], refs[6:]
        both, own, other, dense_o, vectors, acc, dense, sums, jsum, *refs = refs
    else:
        both, acc, dense, sums, jsum, *refs = refs
    w_full, dense_w, out_w, in_w, sems = refs
    shard, slot, block = place_of()
    rows, width = normed.shape
    part = dense_w.shape[0]
    owned, hidden = in_got.shape
    step = pl.program_id(0)

    @pl.when(step == 0)
    def _():
        copies = Copies(sems)
        mine, theirs = span(shard, owned), span(1 - shard, owned)
        started = [copies.start(qkv_got, w_full.at[theirs, :])]
        for i in range(3):
            cols = pl.ds(pl.multiple_of(i * width + block * part, part), part)
            target = w_full.at[mine, i * part : (i + 1) * part]
            started.append(copies.start(qkv_weight.at[:, cols], target))
        started.append(copies.start(dense_weight.at[span(slot, part), :], dense_w))
        started.append(copies.start(out_weight.at[span(slot, hidden), :], out_w))
        started.append(copies.start(in_weight.at[:, span(block, hidden)], in_w.at[mine, :]))
        started.append(copies.start(in_got, in_w.at[theirs, :]))
        if last:
            pairs = ((joint_held, acc), (dense_held, dense), (sums_held, sums), (jsum_held, jsum))
            started += [copies.start(a, b) for a, b in pairs]
        else:
            for ref in (acc, dense, sums, jsum):
                ref[...] = jnp.zeros_like(ref)
        for copy in started:
            copy.wait()

    scaling = HEAD_DIM**-0.5
    biases = []
    for i in range(3):
        at = i * width + block * part
        inside = lax.rem(at, 3 * owned)
        col = at // (3 * owned) * owned + lax.rem(inside, owned)
        cols = pl.ds(pl.multiple_of(col, part), part)
        biases.append(
            sum(jnp.where(inside // owned == r, params[r : r + 1, cols], 0.0) for r in range(3))
        )
    joint = dot(normed[...], w_full[...]) + jnp.concatenate(biases, axis=1)
    grad_context = dot_nt(branch[...], dense_w[...]).astype(BF16)
    seq = cosine.shape[0]
    tables = (cosine[...], low[...], high[...])
    at_p = lax.broadcasted_iota(jnp.int32, (seq, seq), 0)
    at_q = lax.broadcasted_iota(jnp.int32, (seq, seq), 1)
    contexts, grads = [], []
    for one in range(rows // seq):
        at = slice(one * seq, (one + 1) * seq)
        query = turn(joint[at, 0:part], tables, False).astype(BF16)
        keys = turn(joint[at, part : 2 * part], tables, False).astype(BF16)
        vals = joint[at, 2 * part :].astype(BF16)
        allowed = (at_q <= at_p) & (at_q.astype(F32) < lens[8 * one + 7 : 8 * one + 8, :])
        ctxs, queries, keyss, valss = [], [], [], []
        for head in range(part // HEAD_DIM):
            cols = slice(head * HEAD_DIM, (head + 1) * HEAD_DIM)
            q, k, v, gc = query[:, cols], keys[:, cols], vals[:, cols], grad_context[at, cols]
            scores = jnp.where(allowed, dot_nt(q, k) * scaling, -1e30)
            raised = jnp.exp(scores - jnp.max(scores, axis=-1, keepdims=True))
            exact = raised / jnp.sum(raised, axis=-1, keepdims=True)
            probs = exact.astype(BF16)
            ctxs.append(dot(probs, v))
            grad_probs = dot_nt(gc, v)
            valss.append(dot_tn(probs, gc))
            grad_scores = exact * (grad_probs - jnp.sum(grad_probs * exact, axis=-1, keepdims=True))
            grad_scores = grad_scores.astype(BF16)
            queries.append(dot(grad_scores, k) * scaling)
            keyss.append(dot_tn(grad_scores, q) * scaling)
        contexts.append(jnp.concatenate(ctxs, axis=1).astype(BF16))
        grad_query = turn(jnp.concatenate(queries, axis=1), tables, True)
        grad_keys = turn(jnp.concatenate(keyss, axis=1), tables, True)
        grads.append(jnp.concatenate([grad_query, grad_keys] + valss, axis=1).astype(BF16))
    ctx = jnp.concatenate(contexts, axis=0)
    grad = jnp.concatenate(grads, axis=0)
    jsum[...] += jnp.sum(grad.astype(F32), axis=0, keepdims=True)
    acc[...] += dot_tn(normed[...], grad)
    dense[...] += dot_tn(ctx, branch[...])
    both[:, 0:width] = (dot(active[...], out_w[...]) + dot(ctx, dense_w[...])).astype(BF16)
    hat = xhat[...].astype(F32)
    one = dot_nt(grad, w_full[...])
    sums[0:1, :] += jnp.sum(one * hat, axis=0, keepdims=True)
    sums[1:2, :] += jnp.sum(one, axis=0, keepdims=True)
    two = dot_nt(grad_before[...], in_w[...])
    sums[2:3, :] += jnp.sum(two * hat, axis=0, keepdims=True)
    sums[3:4, :] += jnp.sum(two, axis=0, keepdims=True)
    both[:, width:] = (one * params[5:6, :] + two * params[7:8, :]).astype(BF16)
    if not last:
        return

    @pl.when(step == pl.num_programs(0) - 1)
    def _():
        own[...] = acc[span(shard, owned), :].astype(BF16)
        other[...] = acc[span(1 - shard, owned), :].astype(BF16)
        dense_o[...] = dense[...].astype(BF16)
        vectors[...] = jnp.zeros_like(vectors)
        vectors[0:4, :] = sums[0:4, :]
        vectors[4:5, :] = own_sum[...]
        per_row = width // hidden
        vectors[pl.ds(5 + block // per_row, 1), span(lax.rem(block, per_row), hidden)] = in_sum[...]
        for i in range(3):
            row = 5 + GROUP // per_row + i
            vectors[row : row + 1, span(block, part)] = jsum[:, i * part : (i + 1) * part]


def attention(first, blocks, whole, tables, seq_rows, sizes, held=None):
    width, part, hidden = sizes
    rows, steps = 2 * seq_rows, 2
    owned = width // 2
    last = held is not None

    def block(array, height):
        return pl.BlockSpec((height, array.shape[1]), lambda i: (i + first, 0))

    def full(shape):
        return pl.BlockSpec(shape, lambda i: (0, 0))

    sums = [(width, 3 * part), (part, width), (8, width), (1, 3 * part)]
    out = [(shaped((steps * rows, 2 * width)), pl.BlockSpec((rows, 2 * width), lambda i: (i, 0)))]
    if last:
        shapes = [(owned, 3 * part), (owned, 3 * part), (part, width)]
        out += [(shaped(s), full(s)) for s in shapes]
        out.append((shaped((TAIL, width), F32), full((TAIL, width))))
    else:
        out += [(shaped(s, F32), full(s)) for s in sums]
    args = [*blocks, *whole, *tables] + list(held or ())
    specs = [block(a, h) for a, h in zip(blocks, [rows] * 5 + [16])]
    specs += [ANY] * 6 + [full(whole[6].shape)] + [full(t.shape) for t in tables]
    if last:
        specs += [ANY] * 4 + [full(a.shape) for a in held[4:]]
    scratch = [pltpu.VMEM(s, F32) for s in sums] if last else []
    scratch += [pltpu.VMEM(s, BF16) for s in ((width, 3 * part), (part, width), (hidden, width), (width, hidden))]
    return pl.pallas_call(
        lambda *refs: attention_kernel(last, *refs),
        grid=(steps,),
        out_shape=[shape for shape, _ in out],
        in_specs=specs,
        out_specs=[spec for _, spec in out],
        scratch_shapes=scratch + [pltpu.SemaphoreType.DMA((12,))],
        compiler_params=pltpu.CompilerParams(vmem_limit_bytes=LIMIT),
        cost_estimate=COST,
        name="attention",
    )(*args)


def placed(held, pieces, shape, size, where, parts=1):
    count = len(pieces)
    per = shape[1] // max(parts, 1)

    def kernel(*refs):
        ins, (out, raw, wide, sems) = refs[:count], refs[-4:]
        shard, slot, _ = place_of()
        copies = Copies(sems)
        loads = [copies.start(ref, raw.at[j]) for j, ref in enumerate(ins)]
        stores = []
        for j in range(count):
            loads[j].wait()
            wide[j] = raw[j].astype(F32)
            at = where(slot ^ (0, 2, 1, 3)[j], shard)
            if parts == 0:
                stores.append(copies.start(wide.at[j], out.at[span(at, size), :]))
            for i in range(parts):
                cols = pl.ds(pl.multiple_of(i * per + at * size, size), size)
                source = wide.at[j, :, i * size : (i + 1) * size]
                stores.append(copies.start(source, out.at[:, cols]))
        for copy in stores:
            copy.wait()

    args = list(pieces) + ([] if held is None else [held])
    return pl.pallas_call(
        kernel,
        in_specs=[ANY] * len(args),
        out_specs=ANY,
        out_shape=shaped(shape, F32),
        scratch_shapes=[
            pltpu.VMEM((count,) + pieces[0].shape, BF16),
            pltpu.VMEM((count,) + pieces[0].shape, F32),
            pltpu.SemaphoreType.DMA((count * (1 + max(parts, 1)),)),
        ],
        input_output_aliases={} if held is None else {count: 0},
        compiler_params=pltpu.CompilerParams(vmem_limit_bytes=LIMIT),
        cost_estimate=COST,
        name="place",
    )(*args)


def finish_kernel(length, tok, cot, own, got, params, result, grad_tokens):
    rows, width = tok.shape
    live = lax.broadcasted_iota(jnp.int32, (rows, width), 0) < length[0]
    values = tok[...].astype(F32)
    mixed = own[:, 0:width] + got[:, 0:width].astype(F32) + params[3:4, :] + params[4:5, :]
    result[...] = (values + jnp.where(live, mixed, 0.0)).astype(BF16)
    centre = values - jnp.mean(values, axis=-1, keepdims=True)
    root = lax.rsqrt(jnp.mean(centre * centre, axis=-1, keepdims=True) + 1e-05)
    hat = centre * root
    inner = own[:, width:] + got[:, width:].astype(F32)
    inner = inner - jnp.mean(inner, axis=-1, keepdims=True) - hat * jnp.mean(inner * hat, axis=-1, keepdims=True)
    grad_tokens[...] = (cot[...].astype(F32) + inner * root).astype(BF16)


def turn_tables(seq_rows, columns):
    half = ROT // 2
    inverse = np.float32(10000.0) ** (-(2.0 * np.arange(half, dtype=np.float32)) / np.float32(ROT))
    angles = np.arange(seq_rows, dtype=np.float32)[:, None] * inverse.astype(np.float32)[None, :]
    cosine = np.ones((seq_rows, HEAD_DIM), np.float32)
    low = np.zeros((seq_rows, HEAD_DIM), np.float32)
    high = np.zeros((seq_rows, HEAD_DIM), np.float32)
    cosine[:, :half] = cosine[:, half:ROT] = np.cos(angles)
    low[:, :half] = -np.sin(angles)
    high[:, half:ROT] = np.sin(angles)
    return [jnp.asarray(np.tile(t, (1, columns // HEAD_DIM))) for t in (cosine, low, high)]


def make_pairs(mesh):
    reps = mesh.shape["rep"]

    def swap_rep(values, bit):
        return lax.ppermute(values, "rep", [(i, i ^ bit) for i in range(reps)])

    def swap_shard(values):
        return lax.ppermute(values, "shard", [(0, 1), (1, 0)])

    def line_permute(values, pairs):
        pairs = [(a * SPLIT + i, b * SPLIT + i) for a, b in pairs for i in range(SPLIT)]
        return lax.ppermute(values, "rep", pairs)

    def added(left, right):
        return (left.astype(F32) + right.astype(F32)).astype(BF16)

    def after(value, other):
        return lax.optimization_barrier((value, other))[0]

    def on_device(
        tokens, cotangent, lengths, qkv_weight, qkv_bias, dense_weight, dense_bias, in_weight,
        in_bias, out_weight, out_bias, norm1_gain, norm1_bias, norm2_gain, norm2_bias,
    ):
        seq_rows, width = tokens.shape
        owned = width // 2
        hidden = in_weight.shape[1]
        part_f, part_h = hidden // GROUP, width // GROUP
        rows = GROUP * seq_rows
        line = lax.axis_index("rep") // SPLIT

        halves = [qkv_bias, dense_bias, out_bias, norm1_gain, norm1_bias, norm2_gain, norm2_bias]
        packed, branch_sum, in_b, in_give, qkv_give = call(
            pack_kernel,
            "pack",
            [(lengths, SCALAR)]
            + [(a, ANY) for a in [tokens, cotangent, in_bias, *halves, in_weight, qkv_weight]],
            [
                (shaped((2 * seq_rows + TAIL, width)), WHOLE),
                (shaped((1, width), F32), WHOLE),
                (shaped((1, part_f), F32), WHOLE),
                (shaped((owned, part_f)), ANY),
                (shaped((owned, 3 * part_h)), ANY),
            ],
            [pltpu.VMEM((seq_rows, width), BF16)] * 2
            + [pltpu.VMEM(v.shape, BF16) for v in [in_bias, *halves]]
            + [pltpu.SemaphoreType.DMA((14,))],
        )
        beside = swap_rep(packed, 2)
        across = swap_shard(packed)
        beyond = swap_rep(after(across, beside), 2)
        pieces = [packed, across, beside, beyond]
        pieces += [swap_rep(v, 1) for v in pieces]
        in_got = swap_shard(in_give)
        qkv_got = swap_shard(qkv_give)

        normed, xhat, active, grad_before, branch, out_a, out_b, in_mine, in_theirs, params, lens, in_sum = call(
            hidden_kernel,
            "hidden",
            [(p, ANY) for p in pieces]
            + [(in_weight, ANY), (in_got, ANY), (out_weight, ANY), (in_b, WHOLE)],
            [
                (shaped((rows, width)), ANY),
                (shaped((rows, width)), ANY),
                (shaped((rows, part_f)), ANY),
                (shaped((rows, part_f)), ANY),
                (shaped((rows, width)), ANY),
                (shaped((part_f // 2, width)), ANY),
                (shaped((part_f // 2, width)), ANY),
                (shaped((owned, part_f)), ANY),
                (shaped((owned, part_f)), ANY),
                (shaped((TAIL, width), F32), WHOLE),
                (shaped((GROUP * 8, 128), F32), WHOLE),
                (shaped((1, part_f), F32), WHOLE),
            ],
            [
                pltpu.VMEM((rows, width), BF16),
                pltpu.VMEM((rows, width), BF16),
                pltpu.VMEM((GROUP, TAIL, width), BF16),
                pltpu.VMEM((width, part_f), BF16),
                pltpu.VMEM((part_f, width), BF16),
                pltpu.VMEM((rows, width), BF16),
                pltpu.VMEM((rows, width), BF16),
                pltpu.VMEM((rows, width), BF16),
                pltpu.VMEM((rows, part_f), BF16),
                pltpu.VMEM((rows, part_f), F32),
                pltpu.VMEM((rows, part_f), BF16),
                pltpu.VMEM((part_f, width), BF16),
                pltpu.VMEM((owned, part_f), BF16),
                pltpu.VMEM((owned, part_f), BF16),
                pltpu.SemaphoreType.DMA((3 * GROUP + 3 + 9,)),
            ],
        )
        in_other = swap_shard(in_theirs)

        blocks = [normed, branch, active, grad_before, xhat, lens]
        whole = [qkv_weight, qkv_got, dense_weight, out_weight, in_weight, in_got, params]
        tables = turn_tables(seq_rows, part_h)
        sizes = (width, part_h, part_f)
        inner_line = (line == 1) | (line == 2)
        last = [params]

        def then(value):
            return after(value, last[0])

        def did(value):
            last[0] = value
            return value

        def meet(chunk):
            got = line_permute(chunk, [(0, 1), (3, 2)])
            return did(lax.optimization_barrier(added(then(chunk), got)))

        def cross(near):
            got = line_permute(near, [(1, 2), (2, 1)])
            return did(lax.optimization_barrier(added(then(near), got)))

        def spread(both):
            got = line_permute(both, [(1, 0), (2, 3)])
            return did(jnp.where(inner_line, then(both), got))

        def slots(chunk):
            two = [chunk, swap_rep(chunk, 2)]
            return two + [swap_rep(v, 1) for v in two]

        def place(held, pieces, *how):
            return did(placed(held, [then(pieces[0])] + pieces[1:], *how))

        far, *sums = attention(2, blocks, whole, tables, seq_rows, sizes)
        did(sums[3])
        far = swap_rep(far, 1)
        out_a = meet(out_a)
        near, qkv_mine, qkv_theirs, dense_mine, vectors = attention(
            0, [then(normed)] + blocks[1:], whole, tables, seq_rows, sizes, sums + [in_sum, branch_sum]
        )
        did(vectors)
        qkv_other = swap_shard(qkv_theirs)
        out_b = meet(out_b)
        out_a = cross(out_a)
        in_mine = meet(in_mine)
        half = 2 * seq_rows
        give = did(added(then(near[half:]), far[half:]))
        give = swap_rep(give, 2)
        vectors = did(then(vectors) + swap_rep(vectors, 1))
        out_b = cross(out_b)
        in_other = meet(in_other)
        out_a = spread(out_a)
        vectors = did(then(vectors) + swap_rep(vectors, 2))
        in_mine = cross(in_mine)
        qkv_mine = meet(qkv_mine)
        out_b = spread(out_b)
        out_a = slots(out_a)
        vectors = did(then(vectors) + swap_shard(vectors))
        dense_mine = did(jnp.concatenate([dense_mine, then(vectors).astype(BF16)], axis=0))
        in_other = cross(in_other)
        qkv_other = meet(qkv_other)
        in_mine = spread(in_mine)
        out_b = slots(out_b)
        half_f = (hidden // 2, width)
        total_out = place(None, out_a, half_f, part_f // 2, lambda slot, shard: 2 * slot, 0)
        qkv_mine = cross(qkv_mine)
        dense_mine = meet(dense_mine)
        in_other = spread(in_other)
        in_mine = slots(in_mine)
        keep = did(then(near[:half]).astype(F32) + far[:half].astype(F32) + give.astype(F32))
        give = swap_shard(keep[seq_rows:].astype(BF16))
        total_out = place(total_out, out_b, half_f, part_f // 2, lambda slot, shard: 2 * slot + 1, 0)
        qkv_other = cross(qkv_other)
        qkv_mine = spread(qkv_mine)
        in_other = slots(in_other)
        here = lambda slot, shard: shard * SPLIT + slot
        there = lambda slot, shard: (1 - shard) * SPLIT + slot
        dense_mine = cross(dense_mine)
        total_in = place(None, in_mine, (owned, hidden), part_f, here, 1)
        qkv_other = spread(qkv_other)
        qkv_mine = slots(qkv_mine)
        dense_mine = spread(dense_mine)
        qkv_other = slots(qkv_other)
        dense_four = slots(dense_mine[:part_h])
        total_in = place(total_in, in_other, (owned, hidden), part_f, there, 1)
        result, grad_tokens = call(
            finish_kernel,
            "finish",
            [(then(lengths), SCALAR)]
            + [(a, WHOLE) for a in (tokens, cotangent, keep[:seq_rows], give, params)],
            [(shaped((seq_rows, width)), WHOLE)] * 2,
        )
        did(result)
        total_qkv = place(None, qkv_mine, (owned, 3 * width), part_h, here, 3)
        vectors = did(then(dense_mine)[part_h:].astype(F32))
        total_qkv = place(total_qkv, qkv_other, (owned, 3 * width), part_h, there, 3)
        total_dense = place(None, dense_four, (owned, width), part_h, lambda slot, shard: slot, 0)
        shard = lax.axis_index("shard")

        def own_part(first, count):
            piece = vectors[first : first + count].reshape(-1)
            return lax.dynamic_slice_in_dim(piece, shard * (piece.shape[0] // 2), piece.shape[0] // 2, 0)

        hidden_rows = hidden // width
        out_sum = own_part(4, 1)
        return (
            result,
            grad_tokens,
            total_qkv,
            own_part(5 + hidden_rows, 3),
            total_dense,
            out_sum,
            total_in,
            own_part(5, hidden_rows),
            total_out,
            out_sum,
            own_part(0, 1),
            own_part(1, 1),
            own_part(2, 1),
            own_part(3, 1),
        )

    return on_device


def solution(mesh):
    rows = P(("rep", "shard"), None)
    vector = P("shard")
    matrix = P("shard", None)
    weights = (matrix, vector)
    in_specs = (rows, rows, P(("rep", "shard"))) + 4 * weights + 4 * (vector,)
    out_specs = (rows, rows) + 4 * weights + 4 * (vector,)
    paired = mesh.shape["shard"] == 2 and mesh.shape["rep"] == SPLIT * LINES
    body = make_pairs(mesh) if paired else make(mesh)
    return jax.shard_map(body, mesh=mesh, in_specs=in_specs, out_specs=out_specs, check_vma=False)
```

profile of v0, /device:TPU:9, one launch (start us, length us, event | category | flops | bytes accessed | tf_op | source)
XLA Modules:
  0.0 249.9 jit_solution(6603349298583431445)
XLA Ops:
  14.3 11.0 %collective-permute-done.refs_1_ = bf16[272,1024]{1,0:T(8,128)(2,1)S(1)} collective-permute-done((bf16[272,1024]{1,0:T(8,128)(2,1)S(1)}, bf16[272,1024]{1,0:T(8,128)(2,1)S(1)}, u32[]{:S(2)}, u32[]{:S(2)}) %collective-permute-start) | collective-permute-done | bytes 557088 | tf_op jit(solution)/shard_map/ppermute | solution.py:743
  30.6 7.9 %collective-permute-done.2.refs_3_ = bf16[272,1024]{1,0:T(8,128)(2,1)S(1)} collective-permute-done((bf16[272,1024]{1,0:T(8,128)(2,1)S(1)}, bf16[272,1024]{1,0:T(8,128)(2,1)S(1)}, u32[]{:S(2)}, u32[]{:S(2)}) %collective-permute-start.2) | collective-permute-done | bytes 557088 | tf_op jit(solution)/shard_map/ppermute | solution.py:740
  43.7 11.0 %hidden.1 = (bf16[1024,1024]{1,0:T(8,128)(2,1)}, bf16[1024,1024]{1,0:T(8,128)(2,1)}, bf16[1024,512]{1,0:T(8,128)(2,1)}, bf16[1024,512]{1,0:T(8,128)(2,1)}, bf16[...) custom-call(bf16[272,1024]{1,0:T(8,128)(2,1)S(1)} %get-tuple-element, ...), custom_call_target="tpu_custom_call" | custom-call | flops 1024 | bytes 1024 | tf_op jit(solution)/shard_map/hidden/pallas_call | solution.py:358
  58.5 13.7 %attention.2 = (bf16[512,2048]{1,0:T(8,128)(2,1)}, f32[1024,384]{1,0:T(8,128)}, f32[128,1024]{1,0:T(8,128)S(1)}, f32[8,1024]{1,0:T(8,128)S(1)}, f32[1,384]{1,0:T(1,128)S(1)}) custom-call(bf16[1024,1024]{1,0:T(8,128)(2,1)} %get-tuple-element.97.refs_0_, bf16[1024,1024]{1,0:T(8,128)(2,1)} %get-tuple-element.88.refs_1_, bf16[1024,512]{1,0:T(8,128)(2,1)S(1)} %copy-done.2, ...), custom_call_target="tpu_custom_call" | custom-call | flops 1024 | bytes 1024 | tf_op jit(solution)/shard_map/attention/pallas_call | solution.py:655
  77.9 3.4 %collective-permute-start.12 = (bf16[256,1024]{1,0:T(8,128)(2,1)S(1)}, bf16[256,1024]{1,0:T(8,128)(2,1)S(1)}, u32[]{:S(2)}, u32[]{:S(2)}) collective-permute-start(bf16[256,1024]{1,0:T(8,128)(2,1)S(1)} %add_convert_fusion.8), channel_id=1, source_target_pairs={{8,16},{10,18},{12,20},{14,22},{16,8},{18,10},{20,12},{22,14},{9,1... | collective-permute-start | bytes 1572872 | tf_op jit(solution)/shard_map/ppermute | solution.py:747
  83.6 14.1 %attention.3 = (bf16[512,2048]{1,0:T(8,128)(2,1)}, bf16[512,384]{1,0:T(8,128)(2,1)S(1)}, bf16[512,384]{1,0:T(8,128)(2,1)S(1)}, bf16[128,1024]{1,0:T(8,128)(2,1)S(1)}, f32[16,1024]{1,0:T(8,128)S(1)}) custom-call(bf16[1024,1024]{1,0:T(8,128)(2,1)} %get-tuple-element.97.refs_0_, bf16[1024,1024]{1,0:T(8,128)(2,1)} %get-tuple-element.88.refs_1_, ...), custom_call_target="tpu_custom_call" | custom-call | flops 1024 | bytes 1024 | tf_op jit(solution)/shard_map/attention/pallas_call | solution.py:655
  107.2 5.5 %collective-permute-done.25 = bf16[512,384]{1,0:T(8,128)(2,1)S(1)} collective-permute-done((bf16[512,384]{1,0:T(8,128)(2,1)S(1)}, bf16[512,384]{1,0:T(8,128)(2,1)S(1)}, u32[]{:S(2)}, u32[]{:S(2)}) %collective-permute-start.25) | collective-permute-done | bytes 393248 | tf_op jit(solution)/shard_map/ppermute | solution.py:743
  116.9 4.1 %collective-permute-start.18 = (bf16[256,1024]{1,0:T(8,128)(2,1)S(1)}, bf16[256,1024]{1,0:T(8,128)(2,1)S(1)}, u32[]{:S(2)}, u32[]{:S(2)}) collective-permute-start(bf16[256,1024]{1,0:T(8,128)(2,1)S(1)} %add_convert_fusion.6), channel_id=1, source_target_pairs={{8,0},{10,2},{12,4},{14,6},{16,24},{18,26},{20,28},{22,30},{9,1},{... | collective-permute-start | bytes 1572872 | tf_op jit(solution)/shard_map/ppermute | solution.py:747
  121.1 3.2 %collective-permute-start.20 = (bf16[512,512]{1,0:T(8,128)(2,1)S(1)}, bf16[512,512]{1,0:T(8,128)(2,1)S(1)}, u32[]{:S(2)}, u32[]{:S(2)}) collective-permute-start(bf16[512,512]{1,0:T(8,128)(2,1)S(1)} %add_convert_fusion.5), channel_id=1, source_target_pairs={{8,16},{10,18},{12,20},{14,22},{16,8},{18,10},{20,12},{22,14},{9,1... | collective-permute-start | bytes 1572872 | tf_op jit(solution)/shard_map/ppermute | solution.py:747
  124.5 4.8 %collective-permute-done.17 = bf16[512,512]{1,0:T(8,128)(2,1)S(1)} collective-permute-done((bf16[512,512]{1,0:T(8,128)(2,1)S(1)}, bf16[512,512]{1,0:T(8,128)(2,1)S(1)}, u32[]{:S(2)}, u32[]{:S(2)}) %collective-permute-start.17) | collective-permute-done | bytes 524320 | tf_op jit(solution)/shard_map/ppermute | solution.py:747
  130.8 3.3 %collective-permute-start.22 = (bf16[256,1024]{1,0:T(8,128)(2,1)S(1)}, bf16[256,1024]{1,0:T(8,128)(2,1)S(1)}, u32[]{:S(2)}, u32[]{:S(2)}) collective-permute-start(bf16[256,1024]{1,0:T(8,128)(2,1)S(1)} %add_convert_fusion.4), channel_id=1, source_target_pairs={{8,0},{10,2},{12,4},{14,6},{16,24},{18,26},{20,28},{22,30},{9,1},{... | collective-permute-start | bytes 1572872 | tf_op jit(solution)/shard_map/ppermute | solution.py:747
  134.2 3.2 %collective-permute-start.24 = (bf16[512,512]{1,0:T(8,128)(2,1)S(1)}, bf16[512,512]{1,0:T(8,128)(2,1)S(1)}, u32[]{:S(2)}, u32[]{:S(2)}) collective-permute-start(bf16[512,512]{1,0:T(8,128)(2,1)S(1)} %add_convert_fusion.3), channel_id=1, source_target_pairs={{8,16},{10,18},{12,20},{14,22},{16,8},{18,10},{20,12},{22,14},{9,1... | collective-permute-start | bytes 1572872 | tf_op jit(solution)/shard_map/ppermute | solution.py:747
  138.4 4.1 %collective-permute-start.29 = (bf16[256,1024]{1,0:T(8,128)(2,1)S(1)}, bf16[256,1024]{1,0:T(8,128)(2,1)S(1)}, u32[]{:S(2)}, u32[]{:S(2)}) collective-permute-start(bf16[256,1024]{1,0:T(8,128)(2,1)S(1)} %broadcast_select_fusion.1.refs_0_), channel_id=1, source_target_pairs={{0,2},{2,0},{4,6},{6,4},{8,10},{10,8},{12,14},{14,12},{16,18},{18,... | collective-permute-start | bytes 1572872 | tf_op jit(solution)/shard_map/ppermute | solution.py:740
  146.2 3.5 %collective-permute-start.27 = (bf16[512,512]{1,0:T(8,128)(2,1)S(1)}, bf16[512,512]{1,0:T(8,128)(2,1)S(1)}, u32[]{:S(2)}, u32[]{:S(2)}) collective-permute-start(bf16[512,512]{1,0:T(8,128)(2,1)S(1)} %add_convert_fusion.2), channel_id=1, source_target_pairs={{8,0},{10,2},{12,4},{14,6},{16,24},{18,26},{20,28},{22,30},{9,1},{... | collective-permute-start | bytes 1572872 | tf_op jit(solution)/shard_map/ppermute | solution.py:747
  150.5 5.6 %collective-permute-start.30 = (bf16[256,1024]{1,0:T(8,128)(2,1)S(1)}, bf16[256,1024]{1,0:T(8,128)(2,1)S(1)}, u32[]{:S(2)}, u32[]{:S(2)}) collective-permute-start(bf16[256,1024]{1,0:T(8,128)(2,1)S(1)} %collective-permute-done.28.refs_1_), channel_id=1, source_target_pairs={{0,2},{2,0},{4,6},{6,4},{8,10},{10,8},{12,14},{14,12},{16,18},{18,... | collective-permute-start | bytes 1572872 | tf_op jit(solution)/shard_map/ppermute | solution.py:740
  156.2 3.2 %collective-permute-start.31 = (bf16[512,384]{1,0:T(8,128)(2,1)S(1)}, bf16[512,384]{1,0:T(8,128)(2,1)S(1)}, u32[]{:S(2)}, u32[]{:S(2)}) collective-permute-start(bf16[512,384]{1,0:T(8,128)(2,1)S(1)} %add_convert_fusion.12), channel_id=1, source_target_pairs={{8,16},{10,18},{12,20},{14,22},{16,8},{18,10},{20,12},{22,14},{9,1... | collective-permute-start | bytes 1179656 | tf_op jit(solution)/shard_map/ppermute | solution.py:747
  160.9 4.0 %collective-permute-start.33 = (bf16[512,512]{1,0:T(8,128)(2,1)S(1)}, bf16[512,512]{1,0:T(8,128)(2,1)S(1)}, u32[]{:S(2)}, u32[]{:S(2)}) collective-permute-start(bf16[512,512]{1,0:T(8,128)(2,1)S(1)} %add_convert_fusion.1), channel_id=1, source_target_pairs={{8,0},{10,2},{12,4},{14,6},{16,24},{18,26},{20,28},{22,30},{9,1},{... | collective-permute-start | bytes 1572872 | tf_op jit(solution)/shard_map/ppermute | solution.py:747
  170.3 3.0 %collective-permute-start.36 = (bf16[256,1024]{1,0:T(8,128)(2,1)S(1)}, bf16[256,1024]{1,0:T(8,128)(2,1)S(1)}, u32[]{:S(2)}, u32[]{:S(2)}) collective-permute-start(bf16[256,1024]{1,0:T(8,128)(2,1)S(1)} %broadcast_select_fusion.refs_0_), channel_id=1, source_target_pairs={{0,2},{2,0},{4,6},{6,4},{8,10},{10,8},{12,14},{14,12},{16,18},{18,... | collective-permute-start | bytes 1572872 | tf_op jit(solution)/shard_map/ppermute | solution.py:740
  175.8 7.7 %collective-permute-done.35.refs_1_ = bf16[256,1024]{1,0:T(8,128)(2,1)S(1)} collective-permute-done((bf16[256,1024]{1,0:T(8,128)(2,1)S(1)}, bf16[256,1024]{1,0:T(8,128)(2,1)S(1)}, u32[]{:S(2)}, u32[]{:S(2)}) %collective-permute-start.35) | collective-permute-done | bytes 524320 | tf_op jit(solution)/shard_map/ppermute | solution.py:740
  184.8 7.7 %collective-permute-start.37 = (bf16[256,1024]{1,0:T(8,128)(2,1)S(1)}, bf16[256,1024]{1,0:T(8,128)(2,1)S(1)}, u32[]{:S(2)}, u32[]{:S(2)}) collective-permute-start(bf16[256,1024]{1,0:T(8,128)(2,1)S(1)} %collective-permute-done.35.refs_1_), channel_id=1, source_target_pairs={{0,2},{2,0},{4,6},{6,4},{8,10},{10,8},{12,14},{14,12},{16,18},{18,... | collective-permute-start | bytes 1572872 | tf_op jit(solution)/shard_map/ppermute | solution.py:740
  194.4 4.3 %collective-permute-start.40 = (bf16[144,1024]{1,0:T(8,128)(2,1)S(1)}, bf16[144,1024]{1,0:T(8,128)(2,1)S(1)}, u32[]{:S(2)}, u32[]{:S(2)}) collective-permute-start(bf16[144,1024]{1,0:T(8,128)(2,1)S(1)} %add_convert_fusion.14), channel_id=1, source_target_pairs={{8,16},{10,18},{12,20},{14,22},{16,8},{18,10},{20,12},{22,14},{9,1... | collective-permute-start | bytes 884744 | tf_op jit(solution)/shard_map/ppermute | solution.py:747
  231.0 3.1 %place.10 = f32[512,4096]{1,0:T(8,128)} custom-call(bf16[512,512]{1,0:T(8,128)(2,1)S(1)} %broadcast_select_fusion.2.refs_0_, bf16[512,512]{1,0:T(8,128)(2,1)} %collective-permute-done.46.refs_1_, bf16[512,512]{1,0:T(8,128)(2,1)} %collective-permute-done.47.refs_2_, bf16[512,512]{1,0:T(8,128)(2,1)} %collective-permute-done.48.refs_3_, ...), custom_call_target="tpu_custom_call", output_to_operand_aliasing={{}: (4, {})} | custom-call | flops 1024 | bytes 1024 | tf_op jit(solution)/shard_map/place/pallas_call | solution.py:692
  234.7 2.9 %place.11.refs_4_ = f32[512,3072]{1,0:T(8,128)} custom-call(bf16[512,384]{1,0:T(8,128)(2,1)S(1)} %broadcast_select_fusion.5.refs_0_, bf16[512,384]{1,0:T(8,128)(2,1)} %collective-permute-done.50.refs_1_, bf16[512,384]{1,0:T(8,128)(2,1)} %collective-permute-done.51.refs_2_, bf16[512,384]{1,0:T(8,128)(2,1)} %collective-permute-done.52.refs_3_), custom_call_target="tpu_custom_call" | custom-call | flops 1024 | bytes 1024 | tf_op jit(solution)/shard_map/place/pallas_call | solution.py:692
  238.4 3.4 %collective-permute-done.53.refs_1_ = bf16[512,384]{1,0:T(8,128)(2,1)S(1)} collective-permute-done((bf16[512,384]{1,0:T(8,128)(2,1)S(1)}, bf16[512,384]{1,0:T(8,128)(2,1)S(1)}, u32[]{:S(2)}, u32[]{:S(2)}) %collective-permute-start.53) | collective-permute-done | bytes 393248 | tf_op jit(solution)/shard_map/ppermute | solution.py:740
  (215 shorter events, 109.9 us)
Async XLA Ops:
  41.3 14.7 %collective-permute-start.9 = (bf16[512,384]{1,0:T(8,128)(2,1)S(1)}, bf16[512,384]{1,0:T(8,128)(2,1)S(1)}, u32[]{:S(2)}, u32[]{:S(2)}) collective-permute-start(bf16[512,384]{1,0:T(8,128)(2,1)S(1)} %get-tuple-element.93), channel_id=1, source_target_pairs={{0,1},{1,0},{2,3},{3,2},{4,5},{5,4},{6,7},{7,6},{8,9},{9,8},{10,11... | collective-permute-start | bytes 1179656 | tf_op jit(solution)/shard_map/ppermute | solution.py:743
  54.7 21.8 %collective-permute-start.10 = (bf16[256,1024]{1,0:T(8,128)(2,1)}, bf16[256,1024]{1,0:T(8,128)(2,1)}, u32[]{:S(2)}, u32[]{:S(2)}) collective-permute-start(bf16[256,1024]{1,0:T(8,128)(2,1)} %get-tuple-element.96), channel_id=1, source_target_pairs={{0,8},{2,10},{4,12},{6,14},{24,16},{26,18},{28,20},{30,22},{1,9},{... | collective-permute-start | bytes 1572872 | tf_op jit(solution)/shard_map/ppermute | solution.py:747
  73.0 41.0 %collective-permute-start.14 = (bf16[512,2048]{1,0:T(8,128)(2,1)}, bf16[512,2048]{1,0:T(8,128)(2,1)}, u32[]{:S(2)}, u32[]{:S(2)}) collective-permute-start(bf16[512,2048]{1,0:T(8,128)(2,1)} %get-tuple-element.110), channel_id=1, source_target_pairs={{0,2},{2,0},{4,6},{6,4},{8,10},{10,8},{12,14},{14,12},{16,18},{18,... | collective-permute-start | bytes 6291464 | tf_op jit(solution)/shard_map/ppermute | solution.py:740
  73.4 24.3 %collective-permute-start.11 = (bf16[256,1024]{1,0:T(8,128)(2,1)}, bf16[256,1024]{1,0:T(8,128)(2,1)}, u32[]{:S(2)}, u32[]{:S(2)}) collective-permute-start(bf16[256,1024]{1,0:T(8,128)(2,1)} %get-tuple-element.104), channel_id=1, source_target_pairs={{0,8},{2,10},{4,12},{6,14},{24,16},{26,18},{28,20},{30,22},{1,9},{... | collective-permute-start | bytes 1572872 | tf_op jit(solution)/shard_map/ppermute | solution.py:747
  74.7 31.2 %collective-permute-start.8 = (bf16[512,512]{1,0:T(8,128)(2,1)}, bf16[512,512]{1,0:T(8,128)(2,1)S(1)}, u32[]{:S(2)}, u32[]{:S(2)}) collective-permute-start(bf16[512,512]{1,0:T(8,128)(2,1)} %copy-done.27), channel_id=1, source_target_pairs={{0,1},{1,0},{2,3},{3,2},{4,5},{5,4},{6,7},{7,6},{8,9},{9,8},{10,11... | collective-permute-start | bytes 1572872 | tf_op jit(solution)/shard_map/ppermute | solution.py:743
  75.2 29.0 %collective-permute-start.13 = (bf16[512,512]{1,0:T(8,128)(2,1)}, bf16[512,512]{1,0:T(8,128)(2,1)S(1)}, u32[]{:S(2)}, u32[]{:S(2)}) collective-permute-start(bf16[512,512]{1,0:T(8,128)(2,1)} %copy-done.10), channel_id=1, source_target_pairs={{0,8},{2,10},{4,12},{6,14},{24,16},{26,18},{28,20},{30,22},{1,9},{... | collective-permute-start | bytes 1572872 | tf_op jit(solution)/shard_map/ppermute | solution.py:747
  77.9 25.1 %collective-permute-start.12 = (bf16[256,1024]{1,0:T(8,128)(2,1)S(1)}, bf16[256,1024]{1,0:T(8,128)(2,1)S(1)}, u32[]{:S(2)}, u32[]{:S(2)}) collective-permute-start(bf16[256,1024]{1,0:T(8,128)(2,1)S(1)} %add_convert_fusion.8), channel_id=1, source_target_pairs={{8,16},{10,18},{12,20},{14,22},{16,8},{18,10},{20,12},{22,14},{9,1... | collective-permute-start | bytes 1572872 | tf_op jit(solution)/shard_map/ppermute | solution.py:747
  99.1 22.0 %collective-permute-start.16 = (bf16[256,1024]{1,0:T(8,128)(2,1)S(1)}, bf16[256,1024]{1,0:T(8,128)(2,1)S(1)}, u32[]{:S(2)}, u32[]{:S(2)}) collective-permute-start(bf16[256,1024]{1,0:T(8,128)(2,1)S(1)} %add_convert_fusion.7), channel_id=1, source_target_pairs={{8,16},{10,18},{12,20},{14,22},{16,8},{18,10},{20,12},{22,14},{9,1... | collective-permute-start | bytes 1572872 | tf_op jit(solution)/shard_map/ppermute | solution.py:747
  105.9 32.6 %collective-permute-start.21 = (bf16[512,384]{1,0:T(8,128)(2,1)S(1)}, bf16[512,384]{1,0:T(8,128)(2,1)S(1)}, u32[]{:S(2)}, u32[]{:S(2)}) collective-permute-start(bf16[512,384]{1,0:T(8,128)(2,1)S(1)} %get-tuple-element.119), channel_id=1, source_target_pairs={{0,8},{2,10},{4,12},{6,14},{24,16},{26,18},{28,20},{30,22},{1,9},{... | collective-permute-start | bytes 1179656 | tf_op jit(solution)/shard_map/ppermute | solution.py:747
  112.7 16.6 %collective-permute-start.17 = (bf16[512,512]{1,0:T(8,128)(2,1)S(1)}, bf16[512,512]{1,0:T(8,128)(2,1)S(1)}, u32[]{:S(2)}, u32[]{:S(2)}) collective-permute-start(bf16[512,512]{1,0:T(8,128)(2,1)S(1)} %collective-permute-done.8), channel_id=1, source_target_pairs={{0,8},{2,10},{4,12},{6,14},{24,16},{26,18},{28,20},{30,22},{1,9},{... | collective-permute-start | bytes 1572872 | tf_op jit(solution)/shard_map/ppermute | solution.py:747
  114.0 42.2 %collective-permute-start.26 = (bf16[512,384]{1,0:T(8,128)(2,1)S(1)}, bf16[512,384]{1,0:T(8,128)(2,1)S(1)}, u32[]{:S(2)}, u32[]{:S(2)}) collective-permute-start(bf16[512,384]{1,0:T(8,128)(2,1)S(1)} %collective-permute-done.25), channel_id=1, source_target_pairs={{0,8},{2,10},{4,12},{6,14},{24,16},{26,18},{28,20},{30,22},{1,9},{... | collective-permute-start | bytes 1179656 | tf_op jit(solution)/shard_map/ppermute | solution.py:747
  121.1 16.4 %collective-permute-start.20 = (bf16[512,512]{1,0:T(8,128)(2,1)S(1)}, bf16[512,512]{1,0:T(8,128)(2,1)S(1)}, u32[]{:S(2)}, u32[]{:S(2)}) collective-permute-start(bf16[512,512]{1,0:T(8,128)(2,1)S(1)} %add_convert_fusion.5), channel_id=1, source_target_pairs={{8,16},{10,18},{12,20},{14,22},{16,8},{18,10},{20,12},{22,14},{9,1... | collective-permute-start | bytes 1572872 | tf_op jit(solution)/shard_map/ppermute | solution.py:747
  134.2 15.6 %collective-permute-start.24 = (bf16[512,512]{1,0:T(8,128)(2,1)S(1)}, bf16[512,512]{1,0:T(8,128)(2,1)S(1)}, u32[]{:S(2)}, u32[]{:S(2)}) collective-permute-start(bf16[512,512]{1,0:T(8,128)(2,1)S(1)} %add_convert_fusion.3), channel_id=1, source_target_pairs={{8,16},{10,18},{12,20},{14,22},{16,8},{18,10},{20,12},{22,14},{9,1... | collective-permute-start | bytes 1572872 | tf_op jit(solution)/shard_map/ppermute | solution.py:747
  138.4 21.1 %collective-permute-start.29 = (bf16[256,1024]{1,0:T(8,128)(2,1)S(1)}, bf16[256,1024]{1,0:T(8,128)(2,1)S(1)}, u32[]{:S(2)}, u32[]{:S(2)}) collective-permute-start(bf16[256,1024]{1,0:T(8,128)(2,1)S(1)} %broadcast_select_fusion.1.refs_0_), channel_id=1, source_target_pairs={{0,2},{2,0},{4,6},{6,4},{8,10},{10,8},{12,14},{14,12},{16,18},{18,... | collective-permute-start | bytes 1572872 | tf_op jit(solution)/shard_map/ppermute | solution.py:740
  149.8 35.0 %collective-permute-start.34 = (bf16[256,2048]{1,0:T(8,128)(2,1)S(1)}, bf16[256,2048]{1,0:T(8,128)(2,1)S(1)}, u32[]{:S(2)}, u32[]{:S(2)}) collective-permute-start(bf16[256,2048]{1,0:T(8,128)(2,1)S(1)} %add_convert_fusion), channel_id=1, source_target_pairs={{0,4},{2,6},{4,0},{6,2},{8,12},{10,14},{12,8},{14,10},{16,20},{18,... | collective-permute-start | bytes 3145736 | tf_op jit(solution)/shard_map/ppermute | solution.py:740
  165.0 36.0 %collective-permute-start.38 = (bf16[512,384]{1,0:T(8,128)(2,1)S(1)}, bf16[512,384]{1,0:T(8,128)(2,1)S(1)}, u32[]{:S(2)}, u32[]{:S(2)}) collective-permute-start(bf16[512,384]{1,0:T(8,128)(2,1)S(1)} %add_convert_fusion.11), channel_id=1, source_target_pairs={{8,16},{10,18},{12,20},{14,22},{16,8},{18,10},{20,12},{22,14},{9,1... | collective-permute-start | bytes 1179656 | tf_op jit(solution)/shard_map/ppermute | solution.py:747
  170.3 24.0 %collective-permute-start.36 = (bf16[256,1024]{1,0:T(8,128)(2,1)S(1)}, bf16[256,1024]{1,0:T(8,128)(2,1)S(1)}, u32[]{:S(2)}, u32[]{:S(2)}) collective-permute-start(bf16[256,1024]{1,0:T(8,128)(2,1)S(1)} %broadcast_select_fusion.refs_0_), channel_id=1, source_target_pairs={{0,2},{2,0},{4,6},{6,4},{8,10},{10,8},{12,14},{14,12},{16,18},{18,... | collective-permute-start | bytes 1572872 | tf_op jit(solution)/shard_map/ppermute | solution.py:740
  175.0 26.7 %collective-permute-start.41 = (bf16[512,512]{1,0:T(8,128)(2,1)S(1)}, bf16[512,512]{1,0:T(8,128)(2,1)S(1)}, u32[]{:S(2)}, u32[]{:S(2)}) collective-permute-start(bf16[512,512]{1,0:T(8,128)(2,1)S(1)} %broadcast_select_fusion.3.refs_0_), channel_id=1, source_target_pairs={{0,4},{2,6},{4,0},{6,2},{8,12},{10,14},{12,8},{14,10},{16,20},{18,... | collective-permute-start | bytes 1572872 | tf_op jit(solution)/shard_map/ppermute | solution.py:740
  183.5 19.4 %collective-permute-start.39 = (bf16[512,384]{1,0:T(8,128)(2,1)S(1)}, bf16[512,384]{1,0:T(8,128)(2,1)S(1)}, u32[]{:S(2)}, u32[]{:S(2)}) collective-permute-start(bf16[512,384]{1,0:T(8,128)(2,1)S(1)} %add_convert_fusion.10), channel_id=1, source_target_pairs={{8,0},{10,2},{12,4},{14,6},{16,24},{18,26},{20,28},{22,30},{9,1},{... | collective-permute-start | bytes 1179656 | tf_op jit(solution)/shard_map/ppermute | solution.py:747
  205.7 16.6 %collective-permute-start.50 = (bf16[512,384]{1,0:T(8,128)(2,1)S(1)}, bf16[512,384]{1,0:T(8,128)(2,1)}, u32[]{:S(2)}, u32[]{:S(2)}) collective-permute-start(bf16[512,384]{1,0:T(8,128)(2,1)S(1)} %broadcast_select_fusion.5.refs_0_), channel_id=1, source_target_pairs={{0,4},{2,6},{4,0},{6,2},{8,12},{10,14},{12,8},{14,10},{16,20},{18,... | collective-permute-start | bytes 1179656 | tf_op jit(solution)/shard_map/ppermute | solution.py:740
  208.1 16.0 %collective-permute-start.49 = (bf16[128,2048]{1,0:T(8,128)(2,1)S(1)}, bf16[128,2048]{1,0:T(8,128)(2,1)S(1)}, u32[]{:S(2)}, u32[]{:S(2)}) collective-permute-start(bf16[128,2048]{1,0:T(8,128)(2,1)S(1)} %slice.78), channel_id=1, source_target_pairs={{0,1},{1,0},{2,3},{3,2},{4,5},{5,4},{6,7},{7,6},{8,9},{9,8},{10,11... | collective-permute-start | bytes 1572872 | tf_op jit(solution)/shard_map/ppermute | solution.py:743
  213.9 15.8 %collective-permute-start.47 = (bf16[512,512]{1,0:T(8,128)(2,1)S(1)}, bf16[512,512]{1,0:T(8,128)(2,1)}, u32[]{:S(2)}, u32[]{:S(2)}) collective-permute-start(bf16[512,512]{1,0:T(8,128)(2,1)S(1)} %broadcast_select_fusion.2.refs_0_), channel_id=1, source_target_pairs={{0,2},{2,0},{4,6},{6,4},{8,10},{10,8},{12,14},{14,12},{16,18},{18,... | collective-permute-start | bytes 1572872 | tf_op jit(solution)/shard_map/ppermute | solution.py:740
  219.2 14.9 %collective-permute-start.51 = (bf16[512,384]{1,0:T(8,128)(2,1)S(1)}, bf16[512,384]{1,0:T(8,128)(2,1)}, u32[]{:S(2)}, u32[]{:S(2)}) collective-permute-start(bf16[512,384]{1,0:T(8,128)(2,1)S(1)} %broadcast_select_fusion.5.refs_0_), channel_id=1, source_target_pairs={{0,2},{2,0},{4,6},{6,4},{8,10},{10,8},{12,14},{14,12},{16,18},{18,... | collective-permute-start | bytes 1179656 | tf_op jit(solution)/shard_map/ppermute | solution.py:740
  230.5 14.7 %collective-permute-start.54 = (bf16[512,384]{1,0:T(8,128)(2,1)S(1)}, bf16[512,384]{1,0:T(8,128)(2,1)S(1)}, u32[]{:S(2)}, u32[]{:S(2)}) collective-permute-start(bf16[512,384]{1,0:T(8,128)(2,1)S(1)} %broadcast_select_fusion.4.refs_0_), channel_id=1, source_target_pairs={{0,2},{2,0},{4,6},{6,4},{8,10},{10,8},{12,14},{14,12},{16,18},{18,... | collective-permute-start | bytes 1179656 | tf_op jit(solution)/shard_map/ppermute | solution.py:740
  (68 other events, 569.5 us)
where the time goes:
time: 251 us; the launch traced here: 250 us
  starting transfers between devices  101 us (40%)
  Pallas kernels  58 us (23%)
  waiting for transfers between devices  54.9 us (22%)
  local copies, waits for them, and re-layouts  24.4 us (10%)
  other arithmetic  8.81 us (4%)
    ppermute x21, starting transfers between devices, line_permute(): return lax.ppermute(values, 'rep', pairs)  49.5 us
    ppermute x31, starting transfers between devices, swap_rep(): return lax.ppermute(values, 'rep', [(i, i ^ bit) for i in range(reps)])  45.7 us
    pallas_call x2, Pallas kernels, attention(): pl.pallas_call(lambda *refs: attention_kernel(last, *refs), grid=(steps,)...  27.7 us
    ppermute x31, waiting for transfers between devices, swap_rep(): return lax.ppermute(values, 'rep', [(i, i ^ bit) for i in range(reps)])  25.7 us
    ppermute x7, waiting for transfers between devices, swap_shard(): return lax.ppermute(values, 'shard', [(0, 1), (1, 0)])  18.8 us
    unnamed x69, local copies, waits for them, and re-layouts  18.7 us
    pallas_call x7, Pallas kernels, placed(): pl.pallas_call(kernel, in_specs=[ANY] * len(args), out_specs=ANY, out_sha...  17 us
    pallas_call x3, Pallas kernels, call(): pl.pallas_call(kernel, out_shape=[shape for shape, _ in outs], in_specs=[...  13.3 us
  transfers between devices with their start and end apart: 59, of which 14 were waited for; matrix products, arithmetic and copies ran while one was open for 6% of the time, Pallas kernels for 22%

commit v1 on v0

--- a/solution.py
+++ b/solution.py
@@ -343,11 +343,13 @@
 SPLIT = 4
 LINES = 4
 TAIL = 16
-ANY = pl.BlockSpec(memory_space=pl.ANY)
+VECTORS = 32
+ANY = pl.BlockSpec(memory_space=pltpu.HBM)
 SCALAR = pl.BlockSpec(memory_space=pltpu.SMEM)
 WHOLE = pl.BlockSpec(memory_space=pltpu.VMEM)
-LIMIT = 48 * 2**20
-COST = pl.CostEstimate(flops=1024, bytes_accessed=1024, transcendentals=0)
+LIMIT = 63 * 2**20
+COST = pl.CostEstimate(flops=10**12, bytes_accessed=10**9, transcendentals=0)
+SMALL = pl.CostEstimate(flops=10**6, bytes_accessed=0, transcendentals=0)
 
 
 def shaped(shape, dtype=BF16):
@@ -362,7 +364,7 @@
         out_specs=[spec for _, spec in outs],
         scratch_shapes=list(scratch),
         compiler_params=pltpu.CompilerParams(vmem_limit_bytes=LIMIT),
-        cost_estimate=COST,
+        cost_estimate=COST if name == "hidden" else SMALL,
         name=name,
     )(*[array for array, _ in ins])
 
@@ -371,9 +373,12 @@
     def __init__(self, sems):
         self.sems, self.used = sems, 0
 
+    def make(self, source, target):
+        self.used += 1
+        return pltpu.make_async_copy(source, target, self.sems.at[self.used - 1])
+
     def start(self, source, target):
-        copy = pltpu.make_async_copy(source, target, self.sems.at[self.used])
-        self.used += 1
+        copy = self.make(source, target)
         copy.start()
         return copy
 
@@ -385,6 +390,8 @@
 
 
 def span(at, size):
+    if isinstance(at, int):
+        return pl.ds(at * size, size)
     return pl.ds(pl.multiple_of(at * size, size), size)
 
 
@@ -428,7 +435,7 @@
 
 def hidden_kernel(*refs):
     pieces, refs = refs[:GROUP], refs[GROUP:]
-    (in_weight, in_got, out_weight, in_b, normed_o, xhat_o, active_o, grad_o, branch_o, out_a, out_b,
+    (in_weight, in_got, out_weight, in_b, normed_o, xhat_o, active_o, grad_o, branch_o, out_o,
      own_o, other_o, params, lens, in_sum, every, branch, tails, w_full, out_w, normed, normed_two,
      xhat, active, slope, grad_before, grad_out, own, other, sems) = refs
     shard, slot, block = place_of()
@@ -468,7 +475,8 @@
         slope[at, :] = cdf + before * jnp.exp(-0.5 * before * before) * 0.3989422804014327
         return carry
 
-    lax.fori_loop(0, GROUP * rows // step, forward, 0)
+    for i in range(GROUP * rows // step):
+        forward(i, 0)
     done = [copies.start(normed, normed_o), copies.start(xhat, xhat_o), copies.start(active, active_o)]
     for copy in late:
         copy.wait()
@@ -479,8 +487,7 @@
         return carry
 
     lax.fori_loop(0, part // step, out_grad, 0)
-    done.append(copies.start(grad_out.at[0 : part // 2, :], out_a))
-    done.append(copies.start(grad_out.at[part // 2 :, :], out_b))
+    done.append(copies.start(grad_out, out_o))
     in_sum[...] = jnp.zeros_like(in_sum)
 
     def back(i, carry):
@@ -490,7 +497,8 @@
         in_sum[...] += jnp.sum(grad.astype(F32), axis=0, keepdims=True)
         return carry
 
-    lax.fori_loop(0, GROUP * rows // step, back, 0)
+    for i in range(GROUP * rows // step):
+        back(i, 0)
     done.append(copies.start(grad_before, grad_o))
     for ref, target, where in ((other, other_o, 1 - shard), (own, own_o, shard)):
 
@@ -514,41 +522,36 @@
     return values * cosine - moved if back else values * cosine + moved
 
 
-def attention_kernel(last, *refs):
-    (normed, branch, active, grad_before, xhat, lens, qkv_weight, qkv_got, dense_weight, out_weight,
-     in_weight, in_got, params, cosine, low, high), refs = refs[:16], refs[16:]
-    if last:
-        (joint_held, dense_held, sums_held, jsum_held, in_sum, own_sum), refs = refs[:6], refs[6:]
-        both, own, other, dense_o, vectors, acc, dense, sums, jsum, *refs = refs
-    else:
-        both, acc, dense, sums, jsum, *refs = refs
-    w_full, dense_w, out_w, in_w, sems = refs
+def attention_kernel(
+    normed, branch, active, grad_before, xhat, lens, qkv_weight, qkv_got, dense_weight, out_weight,
+    in_weight, in_got, params, cosine, low, high, in_sum, own_sum, far, near, mine_o, theirs_o,
+    acc, dense, sums, jsum, vectors, w_full, dense_w, out_w, in_w, sems,
+):
     shard, slot, block = place_of()
     rows, width = normed.shape
     part = dense_w.shape[0]
     owned, hidden = in_got.shape
     step = pl.program_id(0)
 
+    copies = Copies(sems)
+    mine, theirs = span(shard, owned), span(1 - shard, owned)
+    early = [copies.make(qkv_got, w_full.at[theirs, :])]
+    for i in range(3):
+        cols = pl.ds(pl.multiple_of(i * width + block * part, part), part)
+        target = w_full.at[mine, i * part : (i + 1) * part]
+        early.append(copies.make(qkv_weight.at[:, cols], target))
+    early.append(copies.make(dense_weight.at[span(slot, part), :], dense_w))
+    late = [copies.make(out_weight.at[span(slot, hidden), :], out_w)]
+    late.append(copies.make(in_weight.at[:, span(block, hidden)], in_w.at[mine, :]))
+    late.append(copies.make(in_got, in_w.at[theirs, :]))
+
     @pl.when(step == 0)
     def _():
-        copies = Copies(sems)
-        mine, theirs = span(shard, owned), span(1 - shard, owned)
-        started = [copies.start(qkv_got, w_full.at[theirs, :])]
-        for i in range(3):
-            cols = pl.ds(pl.multiple_of(i * width + block * part, part), part)
-            target = w_full.at[mine, i * part : (i + 1) * part]
-            started.append(copies.start(qkv_weight.at[:, cols], target))
-        started.append(copies.start(dense_weight.at[span(slot, part), :], dense_w))
-        started.append(copies.start(out_weight.at[span(slot, hidden), :], out_w))
-        started.append(copies.start(in_weight.at[:, span(block, hidden)], in_w.at[mine, :]))
-        started.append(copies.start(in_got, in_w.at[theirs, :]))
-        if last:
-            pairs = ((joint_held, acc), (dense_held, dense), (sums_held, sums), (jsum_held, jsum))
-            started += [copies.start(a, b) for a, b in pairs]
-        else:
-            for ref in (acc, dense, sums, jsum):
-                ref[...] = jnp.zeros_like(ref)
-        for copy in started:
+        for copy in early + late:
+            copy.start()
+        for ref in (acc, dense, sums, jsum):
+            ref[...] = jnp.zeros_like(ref)
+        for copy in early:
             copy.wait()
 
     scaling = HEAD_DIM**-0.5
@@ -567,6 +570,20 @@
     tables = (cosine[...], low[...], high[...])
     at_p = lax.broadcasted_iota(jnp.int32, (seq, seq), 0)
     at_q = lax.broadcasted_iota(jnp.int32, (seq, seq), 1)
+    head_of = lax.broadcasted_iota(jnp.int32, (seq, part), 1) // HEAD_DIM
+
+    def apart(values):
+        zero = jnp.zeros_like(values)
+        return jnp.concatenate(
+            [jnp.where(head_of == h, values, zero) for h in range(part // HEAD_DIM)], axis=0
+        )
+
+    def together(values):
+        total = values[0:seq]
+        for h in range(1, part // HEAD_DIM):
+            total = jnp.where(head_of == h, values[h * seq : (h + 1) * seq], total)
+        return total
+
     contexts, grads = [], []
     for one in range(rows // seq):
         at = slice(one * seq, (one + 1) * seq)
@@ -574,31 +591,40 @@
         keys = turn(joint[at, part : 2 * part], tables, False).astype(BF16)
         vals = joint[at, 2 * part :].astype(BF16)
         allowed = (at_q <= at_p) & (at_q.astype(F32) < lens[8 * one + 7 : 8 * one + 8, :])
-        ctxs, queries, keyss, valss = [], [], [], []
-        for head in range(part // HEAD_DIM):
-            cols = slice(head * HEAD_DIM, (head + 1) * HEAD_DIM)
-            q, k, v, gc = query[:, cols], keys[:, cols], vals[:, cols], grad_context[at, cols]
-            scores = jnp.where(allowed, dot_nt(q, k) * scaling, -1e30)
-            raised = jnp.exp(scores - jnp.max(scores, axis=-1, keepdims=True))
-            exact = raised / jnp.sum(raised, axis=-1, keepdims=True)
-            probs = exact.astype(BF16)
-            ctxs.append(dot(probs, v))
-            grad_probs = dot_nt(gc, v)
-            valss.append(dot_tn(probs, gc))
-            grad_scores = exact * (grad_probs - jnp.sum(grad_probs * exact, axis=-1, keepdims=True))
-            grad_scores = grad_scores.astype(BF16)
-            queries.append(dot(grad_scores, k) * scaling)
-            keyss.append(dot_tn(grad_scores, q) * scaling)
-        contexts.append(jnp.concatenate(ctxs, axis=1).astype(BF16))
-        grad_query = turn(jnp.concatenate(queries, axis=1), tables, True)
-        grad_keys = turn(jnp.concatenate(keyss, axis=1), tables, True)
-        grads.append(jnp.concatenate([grad_query, grad_keys] + valss, axis=1).astype(BF16))
+        gc = grad_context[at, :]
+        keys_apart, vals_apart = apart(keys), apart(vals)
+        scores = dot_nt(query, keys_apart) * scaling
+        heads = range(part // HEAD_DIM)
+        exact = []
+        for head in heads:
+            masked = jnp.where(allowed, scores[:, head * seq : (head + 1) * seq], -1e30)
+            raised = jnp.exp(masked - jnp.max(masked, axis=-1, keepdims=True))
+            exact.append(raised / jnp.sum(raised, axis=-1, keepdims=True))
+        probs = jnp.concatenate(exact, axis=1).astype(BF16)
+        contexts.append(dot(probs, vals_apart).astype(BF16))
+        grad_probs = dot_nt(gc, vals_apart)
+        grad_vals = together(dot_tn(probs, gc))
+        grad_scores = []
+        for head in heads:
+            grad = grad_probs[:, head * seq : (head + 1) * seq]
+            mean = jnp.sum(grad * exact[head], axis=-1, keepdims=True)
+            grad_scores.append((exact[head] * (grad - mean)).astype(BF16))
+        grad_scores = jnp.concatenate(grad_scores, axis=1)
+        grad_query = turn(dot(grad_scores, keys_apart) * scaling, tables, True)
+        grad_keys = turn(together(dot_tn(grad_scores, query)) * scaling, tables, True)
+        grads.append(jnp.concatenate([grad_query, grad_keys, grad_vals], axis=1).astype(BF16))
     ctx = jnp.concatenate(contexts, axis=0)
     grad = jnp.concatenate(grads, axis=0)
     jsum[...] += jnp.sum(grad.astype(F32), axis=0, keepdims=True)
     acc[...] += dot_tn(normed[...], grad)
     dense[...] += dot_tn(ctx, branch[...])
-    both[:, 0:width] = (dot(active[...], out_w[...]) + dot(ctx, dense_w[...])).astype(BF16)
+
+    @pl.when(step == 0)
+    def _():
+        for copy in late:
+            copy.wait()
+
+    mixed = (dot(active[...], out_w[...]) + dot(ctx, dense_w[...])).astype(BF16)
     hat = xhat[...].astype(F32)
     one = dot_nt(grad, w_full[...])
     sums[0:1, :] += jnp.sum(one * hat, axis=0, keepdims=True)
@@ -606,59 +632,64 @@
     two = dot_nt(grad_before[...], in_w[...])
     sums[2:3, :] += jnp.sum(two * hat, axis=0, keepdims=True)
     sums[3:4, :] += jnp.sum(two, axis=0, keepdims=True)
-    both[:, width:] = (one * params[5:6, :] + two * params[7:8, :]).astype(BF16)
-    if not last:
-        return
+    inner = (one * params[5:6, :] + two * params[7:8, :]).astype(BF16)
+    for ref, here in ((far, step < 2), (near, step >= 2)):
+
+        @pl.when(here)
+        def _(ref=ref):
+            ref[:, 0:width] = mixed
+            ref[:, width:] = inner
 
     @pl.when(step == pl.num_programs(0) - 1)
     def _():
-        own[...] = acc[span(shard, owned), :].astype(BF16)
-        other[...] = acc[span(1 - shard, owned), :].astype(BF16)
-        dense_o[...] = dense[...].astype(BF16)
+        wide = 3 * part
         vectors[...] = jnp.zeros_like(vectors)
-        vectors[0:4, :] = sums[0:4, :]
-        vectors[4:5, :] = own_sum[...]
-        per_row = width // hidden
-        vectors[pl.ds(5 + block // per_row, 1), span(lax.rem(block, per_row), hidden)] = in_sum[...]
-        for i in range(3):
-            row = 5 + GROUP // per_row + i
-            vectors[row : row + 1, span(block, part)] = jsum[:, i * part : (i + 1) * part]
-
-
-def attention(first, blocks, whole, tables, seq_rows, sizes, held=None):
+        row = 0
+        for source in [sums[i : i + 1, :] for i in range(4)] + [own_sum[...], in_sum[...], jsum[...]]:
+            for at in range(0, source.shape[1], wide):
+                piece = source[:, at : at + wide]
+                vectors[row : row + 1, 0 : piece.shape[1]] = piece
+                row += 1
+        for ref, which in ((mine_o, shard), (theirs_o, 1 - shard)):
+            ref[0:owned, 0:wide] = acc[span(which, owned), :].astype(BF16)
+            ref[owned:, 0:wide] = vectors[...].astype(BF16)
+        each = width * part // owned
+        for i in range(owned // part):
+            cols = slice(i * each, (i + 1) * each)
+            mine_o[i * part : (i + 1) * part, wide:] = dense[:, cols].astype(BF16)
+        mine_o[owned:, wide:] = jnp.zeros((VECTORS, each), BF16)
+
+
+def attention(blocks, whole, tables, small, seq_rows, sizes):
     width, part, hidden = sizes
-    rows, steps = 2 * seq_rows, 2
-    owned = width // 2
-    last = held is not None
+    rows, steps = 2 * seq_rows, 4
+    owned, wide = width // 2, 3 * part
 
     def block(array, height):
-        return pl.BlockSpec((height, array.shape[1]), lambda i: (i + first, 0))
+        return pl.BlockSpec((height, array.shape[1]), lambda i: ((i + 2) % 4, 0))
 
     def full(shape):
         return pl.BlockSpec(shape, lambda i: (0, 0))
 
-    sums = [(width, 3 * part), (part, width), (8, width), (1, 3 * part)]
-    out = [(shaped((steps * rows, 2 * width)), pl.BlockSpec((rows, 2 * width), lambda i: (i, 0)))]
-    if last:
-        shapes = [(owned, 3 * part), (owned, 3 * part), (part, width)]
-        out += [(shaped(s), full(s)) for s in shapes]
-        out.append((shaped((TAIL, width), F32), full((TAIL, width))))
-    else:
-        out += [(shaped(s, F32), full(s)) for s in sums]
-    args = [*blocks, *whole, *tables] + list(held or ())
+    outer = pl.BlockSpec((rows, 2 * width), lambda i: (jnp.minimum(i, 1), 0))
+    inner = pl.BlockSpec((rows, 2 * width), lambda i: (jnp.maximum(i - 2, 0), 0))
+    mine = (owned + VECTORS, wide + width * part // owned)
+    theirs = (owned + VECTORS, wide)
+    half = shaped((2 * rows, 2 * width))
+    args = [*blocks, *whole, *tables, *small]
     specs = [block(a, h) for a, h in zip(blocks, [rows] * 5 + [16])]
-    specs += [ANY] * 6 + [full(whole[6].shape)] + [full(t.shape) for t in tables]
-    if last:
-        specs += [ANY] * 4 + [full(a.shape) for a in held[4:]]
-    scratch = [pltpu.VMEM(s, F32) for s in sums] if last else []
-    scratch += [pltpu.VMEM(s, BF16) for s in ((width, 3 * part), (part, width), (hidden, width), (width, hidden))]
+    specs += [ANY] * 6 + [full(a.shape) for a in [whole[6], *tables, *small]]
+    sums = [(width, wide), (part, width), (8, width), (1, wide), (VECTORS, wide)]
+    weights = [(width, wide), (part, width), (hidden, width), (width, hidden)]
     return pl.pallas_call(
-        lambda *refs: attention_kernel(last, *refs),
+        attention_kernel,
         grid=(steps,),
-        out_shape=[shape for shape, _ in out],
+        out_shape=[half, half, shaped(mine), shaped(theirs)],
         in_specs=specs,
-        out_specs=[spec for _, spec in out],
-        scratch_shapes=scratch + [pltpu.SemaphoreType.DMA((12,))],
+        out_specs=[outer, inner, full(mine), full(theirs)],
+        scratch_shapes=[pltpu.VMEM(s, F32) for s in sums]
+        + [pltpu.VMEM(s, BF16) for s in weights]
+        + [pltpu.SemaphoreType.DMA((8,))],
         compiler_params=pltpu.CompilerParams(vmem_limit_bytes=LIMIT),
         cost_estimate=COST,
         name="attention",
@@ -668,12 +699,14 @@
 def placed(held, pieces, shape, size, where, parts=1):
     count = len(pieces)
     per = shape[1] // max(parts, 1)
+    height = pieces[0].shape[0] if parts else size
+    held_shape = (count, height, pieces[0].shape[1])
 
     def kernel(*refs):
         ins, (out, raw, wide, sems) = refs[:count], refs[-4:]
         shard, slot, _ = place_of()
         copies = Copies(sems)
-        loads = [copies.start(ref, raw.at[j]) for j, ref in enumerate(ins)]
+        loads = [copies.start(ref.at[0:height, :], raw.at[j]) for j, ref in enumerate(ins)]
         stores = []
         for j in range(count):
             loads[j].wait()
@@ -691,19 +724,136 @@
     args = list(pieces) + ([] if held is None else [held])
     return pl.pallas_call(
         kernel,
-        in_specs=[ANY] * len(args),
-        out_specs=ANY,
+        in_specs=[pl.BlockSpec(memory_space=pl.ANY)] * len(args),
+        out_specs=pl.BlockSpec(memory_space=pl.ANY),
         out_shape=shaped(shape, F32),
         scratch_shapes=[
-            pltpu.VMEM((count,) + pieces[0].shape, BF16),
-            pltpu.VMEM((count,) + pieces[0].shape, F32),
+            pltpu.VMEM(held_shape, BF16),
+            pltpu.VMEM(held_shape, F32),
             pltpu.SemaphoreType.DMA((count * (1 + max(parts, 1)),)),
         ],
         input_output_aliases={} if held is None else {count: 0},
-        compiler_params=pltpu.CompilerParams(vmem_limit_bytes=LIMIT),
-        cost_estimate=COST,
+        compiler_params=pltpu.CompilerParams(vmem_limit_bytes=LIMIT // 2),
+        cost_estimate=SMALL,
         name="place",
     )(*args)
+
+
+def fold(left, right, rows=None, name="fold"):
+    count = rows or left.shape[0]
+    shape = (count, left.shape[1])
+
+    def kernel(a, b, out, a_v, b_v, sems):
+        copies = Copies(sems)
+        first = copies.start(a.at[a.shape[0] - count :, :], a_v)
+        second = copies.start(b.at[b.shape[0] - count :, :], b_v)
+        first.wait()
+        second.wait()
+        a_v[...] = (a_v[...].astype(F32) + b_v[...].astype(F32)).astype(BF16)
+        copies.start(a_v, out).wait()
+
+    scratch = [pltpu.VMEM(shape, BF16)] * 2 + [pltpu.SemaphoreType.DMA((3,))]
+    return call(kernel, name, [(left, ANY), (right, ANY)], [(shaped(shape), ANY)], scratch)[0]
+
+
+def keep_sum(near, far, got):
+    count, width = got.shape[0] // 2, got.shape[1]
+
+    def kernel(a, b, c, own, give, a_v, b_v, c_v, o_v, sems):
+        copies = Copies(sems)
+        loads = [copies.start(r.at[0 : 2 * count, :], v) for r, v in ((a, a_v), (b, b_v), (c, c_v))]
+        for copy in loads:
+            copy.wait()
+        total = a_v[...].astype(F32) + b_v[...].astype(F32) + c_v[...].astype(F32)
+        o_v[...] = total[0:count, :]
+        a_v[0:count, :] = total[count:, :].astype(BF16)
+        stores = [copies.start(o_v, own), copies.start(a_v.at[0:count, :], give)]
+        for copy in stores:
+            copy.wait()
+
+    scratch = [pltpu.VMEM((2 * count, width), BF16)] * 3 + [pltpu.VMEM((count, width), F32)]
+    return call(
+        kernel,
+        "keep",
+        [(near, ANY), (far, ANY), (got, ANY)],
+        [(shaped((count, width), F32), ANY), (shaped((count, width)), ANY)],
+        scratch + [pltpu.SemaphoreType.DMA((5,))],
+    )
+
+
+def joint_kernel(*refs):
+    ins, (total, dense, raw, wide, sems) = refs[:4], refs[4:]
+    shard, slot, _ = place_of()
+    owned = total.shape[0]
+    part = dense.shape[0] // SPLIT
+    copies = Copies(sems)
+    loads = [copies.start(ref.at[0:owned, :], raw.at[j]) for j, ref in enumerate(ins)]
+    stores = []
+    for j in range(4):
+        loads[j].wait()
+        wide[j] = raw[j].astype(F32)
+        at = slot ^ (0, 2, 1, 3)[j]
+        for i in range(3):
+            where = i * (total.shape[1] // 3) + (shard * SPLIT + at) * part
+            cols = pl.ds(pl.multiple_of(where, part), part)
+            stores.append(copies.start(wide.at[j, :, i * part : (i + 1) * part], total.at[:, cols]))
+        each = raw.shape[2] - 3 * part
+        for i in range(owned // part):
+            source = wide.at[j, i * part : (i + 1) * part, 3 * part :]
+            target = dense.at[span(at, part), i * each : (i + 1) * each]
+            stores.append(copies.start(source, target))
+    for copy in stores:
+        copy.wait()
+
+
+def other_kernel(*refs):
+    own, ins, refs = refs[:4], refs[4:8], refs[9:]
+    total, qkv_o, in_o, out_o, dense_o, g1, b1, g2, b2, raw, wide, edge, flat, joint, in_b, sems = refs
+    shard, slot, _ = place_of()
+    owned = total.shape[0]
+    width = total.shape[1] // 3
+    part = raw.shape[2] // 3
+    hidden = in_o.shape[0] // SPLIT
+    copies = Copies(sems)
+    edges = [copies.start(ref.at[owned:, 0 : 3 * part], edge.at[j]) for j, ref in enumerate(own)]
+    loads = [copies.start(ref, raw.at[j]) for j, ref in enumerate(ins)]
+    stores = []
+    for j in range(4):
+        loads[j].wait()
+        wide[j] = raw[j].astype(F32)
+        at = slot ^ (0, 2, 1, 3)[j]
+        for i in range(3):
+            where = i * width + ((1 - shard) * SPLIT + at) * part
+            cols = pl.ds(pl.multiple_of(where, part), part)
+            source = wide.at[j, 0:owned, i * part : (i + 1) * part]
+            stores.append(copies.start(source, total.at[:, cols]))
+    for copy in edges:
+        copy.wait()
+    mine = [edge[j].astype(F32) for j in range(4)]
+    theirs = [wide[j, owned:, :] for j in range(4)]
+    every = sum(mine) + sum(theirs)
+    per = -(-width // (3 * part))
+    for i, vectors in enumerate(((g1,), (b1,), (g2,), (b2,), (out_o, dense_o))):
+        flat[...] = jnp.concatenate([every[i * per + k : i * per + k + 1] for k in range(per)], axis=1)[:, 0:width]
+        for ref in vectors:
+            ref[...] = flat[:, span(shard, owned)].reshape(owned)
+    row = 5 * per
+    long = -(-hidden // (3 * part))
+    for j in range(4):
+        at = slot ^ (0, 2, 1, 3)[j]
+        sums = jnp.concatenate([mine[j][row + k : row + k + 1] for k in range(long)], axis=1)
+        in_b[:, span(at, hidden)] = sums[:, 0:hidden]
+        for values, group in ((mine[j], shard), (theirs[j], 1 - shard)):
+            for i in range(3):
+                piece = values[row + long : row + long + 1, i * part : (i + 1) * part]
+                joint[i : i + 1, span(group * SPLIT + at, part)] = piece
+    thirds = [joint[i : i + 1, k * owned : (k + 1) * owned] for i in range(3) for k in range(2)]
+    for i in range(3):
+        third = jnp.where(shard == 0, thirds[i], thirds[3 + i])
+        qkv_o[i * owned : (i + 1) * owned] = third.reshape(owned)
+    in_o[...] = in_b[...].reshape(in_o.shape)
+    for copy in stores:
+        copy.wait()
 
 
 def finish_kernel(length, tok, cot, own, got, params, result, grad_tokens):
@@ -733,6 +883,15 @@
     return [jnp.asarray(np.tile(t, (1, columns // HEAD_DIM))) for t in (cosine, low, high)]
 
 
+ORDER = (
+    "far", "mob", "moa", "coa", "fold", "tja", "mia", "mib", "cob", "poa",
+    "xoa", "cia", "tjb", "pob", "keep", "xob", "cib", "mja", "pia", "xia",
+    "sob", "soa", "mjb", "pib", "xib", "loa", "cja", "sia", "lob", "pja",
+    "cjb", "xja", "sib", "pjb", "xjb", "lia", "lib", "sja", "end", "sjb",
+    "lja",
+)
+
+
 def make_pairs(mesh):
     reps = mesh.shape["rep"]
 
@@ -745,9 +904,6 @@
     def line_permute(values, pairs):
         pairs = [(a * SPLIT + i, b * SPLIT + i) for a, b in pairs for i in range(SPLIT)]
         return lax.ppermute(values, "rep", pairs)
-
-    def added(left, right):
-        return (left.astype(F32) + right.astype(F32)).astype(BF16)
 
     def after(value, other):
         return lax.optimization_barrier((value, other))[0]
@@ -761,8 +917,6 @@
         hidden = in_weight.shape[1]
         part_f, part_h = hidden // GROUP, width // GROUP
         rows = GROUP * seq_rows
-        line = lax.axis_index("rep") // SPLIT
-
         halves = [qkv_bias, dense_bias, out_bias, norm1_gain, norm1_bias, norm2_gain, norm2_bias]
         packed, branch_sum, in_b, in_give, qkv_give = call(
             pack_kernel,
@@ -773,8 +927,8 @@
                 (shaped((2 * seq_rows + TAIL, width)), WHOLE),
                 (shaped((1, width), F32), WHOLE),
                 (shaped((1, part_f), F32), WHOLE),
-                (shaped((owned, part_f)), ANY),
-                (shaped((owned, 3 * part_h)), ANY),
+                (shaped((owned, part_f)), WHOLE),
+                (shaped((owned, 3 * part_h)), WHOLE),
             ],
             [pltpu.VMEM((seq_rows, width), BF16)] * 2
             + [pltpu.VMEM(v.shape, BF16) for v in [in_bias, *halves]]
@@ -783,12 +937,12 @@
         beside = swap_rep(packed, 2)
         across = swap_shard(packed)
         beyond = swap_rep(after(across, beside), 2)
-        pieces = [packed, across, beside, beyond]
-        pieces += [swap_rep(v, 1) for v in pieces]
         in_got = swap_shard(in_give)
         qkv_got = swap_shard(qkv_give)
-
-        normed, xhat, active, grad_before, branch, out_a, out_b, in_mine, in_theirs, params, lens, in_sum = call(
+        pieces = [packed, across, beside, after(beyond, in_got)]
+        pieces += [swap_rep(v, 1) for v in pieces]
+
+        normed, xhat, active, grad_before, branch, out_all, in_mine, in_theirs, params, lens, in_sum = call(
             hidden_kernel,
             "hidden",
             [(p, ANY) for p in pieces]
@@ -799,8 +953,7 @@
                 (shaped((rows, part_f)), ANY),
                 (shaped((rows, part_f)), ANY),
                 (shaped((rows, width)), ANY),
-                (shaped((part_f // 2, width)), ANY),
-                (shaped((part_f // 2, width)), ANY),
+                (shaped((part_f, width)), ANY),
                 (shaped((owned, part_f)), ANY),
                 (shaped((owned, part_f)), ANY),
                 (shaped((TAIL, width), F32), WHOLE),
@@ -831,6 +984,7 @@
         whole = [qkv_weight, qkv_got, dense_weight, out_weight, in_weight, in_got, params]
         tables = turn_tables(seq_rows, part_h)
         sizes = (width, part_h, part_f)
+        line = lax.axis_index("rep") // SPLIT
         inner_line = (line == 1) | (line == 2)
         last = [params]
 
@@ -841,112 +995,115 @@
             last[0] = value
             return value
 
+        def added(left, right):
+            total = (left.astype(F32) + right.astype(F32)).astype(BF16)
+            return did(lax.optimization_barrier(total))
+
         def meet(chunk):
-            got = line_permute(chunk, [(0, 1), (3, 2)])
-            return did(lax.optimization_barrier(added(then(chunk), got)))
+            return added(then(chunk), line_permute(chunk, [(0, 1), (3, 2)]))
 
         def cross(near):
-            got = line_permute(near, [(1, 2), (2, 1)])
-            return did(lax.optimization_barrier(added(then(near), got)))
+            return added(then(near), line_permute(near, [(1, 2), (2, 1)]))
 
         def spread(both):
             got = line_permute(both, [(1, 0), (2, 3)])
             return did(jnp.where(inner_line, then(both), got))
 
-        def slots(chunk):
-            two = [chunk, swap_rep(chunk, 2)]
-            return two + [swap_rep(v, 1) for v in two]
-
-        def place(held, pieces, *how):
-            return did(placed(held, [then(pieces[0])] + pieces[1:], *how))
-
-        far, *sums = attention(2, blocks, whole, tables, seq_rows, sizes)
-        did(sums[3])
-        far = swap_rep(far, 1)
-        out_a = meet(out_a)
-        near, qkv_mine, qkv_theirs, dense_mine, vectors = attention(
-            0, [then(normed)] + blocks[1:], whole, tables, seq_rows, sizes, sums + [in_sum, branch_sum]
-        )
-        did(vectors)
-        qkv_other = swap_shard(qkv_theirs)
-        out_b = meet(out_b)
-        out_a = cross(out_a)
-        in_mine = meet(in_mine)
-        half = 2 * seq_rows
-        give = did(added(then(near[half:]), far[half:]))
-        give = swap_rep(give, 2)
-        vectors = did(then(vectors) + swap_rep(vectors, 1))
-        out_b = cross(out_b)
-        in_other = meet(in_other)
-        out_a = spread(out_a)
-        vectors = did(then(vectors) + swap_rep(vectors, 2))
-        in_mine = cross(in_mine)
-        qkv_mine = meet(qkv_mine)
-        out_b = spread(out_b)
-        out_a = slots(out_a)
-        vectors = did(then(vectors) + swap_shard(vectors))
-        dense_mine = did(jnp.concatenate([dense_mine, then(vectors).astype(BF16)], axis=0))
-        in_other = cross(in_other)
-        qkv_other = meet(qkv_other)
-        in_mine = spread(in_mine)
-        out_b = slots(out_b)
         half_f = (hidden // 2, width)
-        total_out = place(None, out_a, half_f, part_f // 2, lambda slot, shard: 2 * slot, 0)
-        qkv_mine = cross(qkv_mine)
-        dense_mine = meet(dense_mine)
-        in_other = spread(in_other)
-        in_mine = slots(in_mine)
-        keep = did(then(near[:half]).astype(F32) + far[:half].astype(F32) + give.astype(F32))
-        give = swap_shard(keep[seq_rows:].astype(BF16))
-        total_out = place(total_out, out_b, half_f, part_f // 2, lambda slot, shard: 2 * slot + 1, 0)
-        qkv_other = cross(qkv_other)
-        qkv_mine = spread(qkv_mine)
-        in_other = slots(in_other)
+        wide = 3 * part_h
         here = lambda slot, shard: shard * SPLIT + slot
         there = lambda slot, shard: (1 - shard) * SPLIT + slot
-        dense_mine = cross(dense_mine)
-        total_in = place(None, in_mine, (owned, hidden), part_f, here, 1)
-        qkv_other = spread(qkv_other)
-        qkv_mine = slots(qkv_mine)
-        dense_mine = spread(dense_mine)
-        qkv_other = slots(qkv_other)
-        dense_four = slots(dense_mine[:part_h])
-        total_in = place(total_in, in_other, (owned, hidden), part_f, there, 1)
-        result, grad_tokens = call(
-            finish_kernel,
-            "finish",
-            [(then(lengths), SCALAR)]
-            + [(a, WHOLE) for a in (tokens, cotangent, keep[:seq_rows], give, params)],
-            [(shaped((seq_rows, width)), WHOLE)] * 2,
+        goes = {
+            "oa": ("out", half_f, part_f // 2, lambda slot, shard: 2 * slot, 0),
+            "ob": ("out", half_f, part_f // 2, lambda slot, shard: 2 * slot + 1, 0),
+            "ia": ("in", (owned, hidden), part_f, here, 1),
+            "ib": ("in", (owned, hidden), part_f, there, 1),
+        }
+        totals = {"out": None, "in": None}
+
+        far, near, joint_a, joint_theirs = attention(
+            blocks, whole, tables, [in_sum, branch_sum], seq_rows, sizes
         )
-        did(result)
-        total_qkv = place(None, qkv_mine, (owned, 3 * width), part_h, here, 3)
-        vectors = did(then(dense_mine)[part_h:].astype(F32))
-        total_qkv = place(total_qkv, qkv_other, (owned, 3 * width), part_h, there, 3)
-        total_dense = place(None, dense_four, (owned, width), part_h, lambda slot, shard: slot, 0)
-        shard = lax.axis_index("shard")
-
-        def own_part(first, count):
-            piece = vectors[first : first + count].reshape(-1)
-            return lax.dynamic_slice_in_dim(piece, shard * (piece.shape[0] // 2), piece.shape[0] // 2, 0)
-
-        hidden_rows = hidden // width
-        out_sum = own_part(4, 1)
+        did(joint_a)
+        got = line_permute(out_all, [(0, 1), (3, 2)])
+        half = part_f // 2
+        state = {"oa": (out_all[:half], got[:half]), "ob": (out_all[half:], got[half:])}
+        state |= {"ia": in_mine, "ib": in_other, "ja": joint_a}
+        state["jb"] = swap_shard(joint_theirs)
+        for token in ORDER:
+            what, name = token[0], token[1:]
+            held = state.get(name)
+            if what == "t":
+                state[name] = then(held)
+            elif what == "m":
+                state[name] = added(then(held[0]), held[1]) if name[0] == "o" else meet(held)
+            elif what == "c":
+                state[name] = cross(held)
+            elif what == "p":
+                state[name] = spread(held)
+            elif what == "x":
+                state[name] = [held, swap_rep(then(held), 2)]
+            elif what == "s":
+                state[name] = held + [swap_rep(then(v), 1) for v in held]
+            elif what == "l" and name in goes:
+                kind, *how = goes[name]
+                totals[kind] = did(placed(totals[kind], [then(held[0])] + held[1:], *how))
+            elif token == "lja":
+                total_qkv, total_dense = call(
+                    joint_kernel,
+                    "place_joint",
+                    [(then(held[0]), ANY)] + [(a, ANY) for a in held[1:]],
+                    [(shaped((owned, 3 * width), F32), ANY), (shaped((owned, width), F32), ANY)],
+                    [
+                        pltpu.VMEM((4, owned, held[0].shape[1]), BF16),
+                        pltpu.VMEM((4, owned, held[0].shape[1]), F32),
+                        pltpu.SemaphoreType.DMA((4 * (4 + owned // part_h),)),
+                    ],
+                )
+                did(total_dense)
+            elif token == "far":
+                far = swap_rep(then(far), 1)
+            elif token == "fold":
+                give = swap_rep(did(fold(then(near), far, 2 * seq_rows)), 2)
+            elif token == "keep":
+                keep, give = keep_sum(then(near), far, give)
+                did(keep)
+                give = swap_shard(give)
+            elif token == "end":
+                result, grad_tokens = call(
+                    finish_kernel,
+                    "finish",
+                    [(then(lengths), SCALAR)]
+                    + [(a, WHOLE) for a in (tokens, cotangent, keep, give, params)],
+                    [(shaped((seq_rows, width)), WHOLE)] * 2,
+                )
+                did(result)
+        total_out, total_in = totals["out"], totals["in"]
+        joint_a, joint_b = state["ja"], state["jb"]
+        sizes = [3 * owned, hidden // 2] + 6 * [owned]
+        total_qkv, *vectors = pl.pallas_call(
+            other_kernel,
+            out_shape=[shaped(total_qkv.shape, F32)] + [shaped((n,), F32) for n in sizes],
+            in_specs=[ANY] * 9,
+            out_specs=[ANY] + [WHOLE] * 8,
+            scratch_shapes=[
+                pltpu.VMEM((4, owned + VECTORS, wide), BF16),
+                pltpu.VMEM((4, owned + VECTORS, wide), F32),
+                pltpu.VMEM((4, VECTORS, wide), BF16),
+                pltpu.VMEM((1, width), F32),
+                pltpu.VMEM((3, width), F32),
+                pltpu.VMEM((1, hidden // 2), F32),
+                pltpu.SemaphoreType.DMA((20,)),
+            ],
+            input_output_aliases={8: 0},
+            compiler_params=pltpu.CompilerParams(vmem_limit_bytes=LIMIT),
+            cost_estimate=SMALL,
+            name="place_other",
+        )(*joint_a, *joint_b, total_qkv)
+        qkv_b, in_b, out_b, dense_b, g1, b1, g2, b2 = vectors
         return (
-            result,
-            grad_tokens,
-            total_qkv,
-            own_part(5 + hidden_rows, 3),
-            total_dense,
-            out_sum,
-            total_in,
-            own_part(5, hidden_rows),
-            total_out,
-            out_sum,
-            own_part(0, 1),
-            own_part(1, 1),
-            own_part(2, 1),
-            own_part(3, 1),
+            result, grad_tokens, total_qkv, qkv_b, total_dense, dense_b, total_in, in_b, total_out, out_b,
+            g1, b1, g2, b2,
         )
 
     return on_device

time: 251 us -> 230 us (0.916)
  starting transfers between devices: 101 us -> 79.2 us
  local copies, waits for them, and re-layouts: 24.4 us -> 3.77 us
  waiting for transfers between devices: 54.9 us -> 65.4 us
  other arithmetic: 8.81 us -> 17.3 us
  Pallas kernels: 58 us -> 61 us
    unnamed x69 -> x20, local copies, waits for them, and re-layouts: 18.7 us -> 2.5 us
    pallas_call x3 -> x6, Pallas kernels: 13.3 us -> 27.4 us  [call(): pl.pallas_call(kernel, out_shape=[shape for shape, _ in outs], in_specs=[...]
    ppermute x31 -> x26, waiting for transfers between devices: 25.7 us -> 37.4 us  [swap_rep(): return lax.ppermute(values, 'rep', [(i, i ^ bit) for i in range(reps)])]
    pallas_call x9 -> x6, Pallas kernels: 44.7 us -> 33.6 us  [the longest x1 20 us: attention(): pl.pallas_call(attention_kernel, grid=(steps,), out_shape=[half, half, sh...]
    ppermute x21 -> x17, starting transfers between devices: 49.5 us -> 38.5 us  [line_permute(): return lax.ppermute(values, 'rep', pairs)]
    ppermute x31 -> x26, starting transfers between devices: 45.7 us -> 35.7 us  [swap_rep(): return lax.ppermute(values, 'rep', [(i, i ^ bit) for i in range(reps)])]
    ppermute x7 -> x6, waiting for transfers between devices: 18.8 us -> 9.85 us  [swap_shard(): return lax.ppermute(values, 'shard', [(0, 1), (1, 0)])]
    ppermute x21 -> x17, waiting for transfers between devices: 10.4 us -> 18.1 us  [line_permute(): return lax.ppermute(values, 'rep', pairs)]
  transfers between devices with their start and end apart: 59 -> 49, of which waited for: 14 -> 18; matrix products, arithmetic and copies ran while one was open for 6% -> 8% of each run, Pallas kernels for 22% -> 24%
where the time goes in v1:
time: 230 us; the launch traced here: 229 us
  starting transfers between devices  79.2 us (34%)
  waiting for transfers between devices  65.4 us (28%)
  Pallas kernels  61 us (27%)
  other arithmetic  17.3 us (8%)
  local copies, waits for them, and re-layouts  3.77 us (2%)
    ppermute x17, starting transfers between devices, line_permute(): return lax.ppermute(values, 'rep', pairs)  38.5 us
    ppermute x26, waiting for transfers between devices, swap_rep(): return lax.ppermute(values, 'rep', [(i, i ^ bit) for i in range(reps)])  37.4 us
    ppermute x26, starting transfers between devices, swap_rep(): return lax.ppermute(values, 'rep', [(i, i ^ bit) for i in range(reps)])  35.7 us
    pallas_call x6, Pallas kernels, call(): pl.pallas_call(kernel, out_shape=[shape for shape, _ in outs], in_specs=[...  27.4 us
    pallas_call x1, Pallas kernels, attention(): pl.pallas_call(attention_kernel, grid=(steps,), out_shape=[half, half, sh...  20 us
    ppermute x17, waiting for transfers between devices, line_permute(): return lax.ppermute(values, 'rep', pairs)  18.1 us
    convert_element_type x12, other arithmetic, added(): total = (left.astype(F32) + right.astype(F32)).astype(BF16)  13.3 us
    pallas_call x4, Pallas kernels, placed(): pl.pallas_call(kernel, in_specs=[pl.BlockSpec(memory_space=pl.ANY)] * len...  10.1 us
  transfers between devices with their start and end apart: 49, of which 18 were waited for; matrix products, arithmetic and copies ran while one was open for 8% of the time, Pallas kernels for 24%

profile of v1, /device:TPU:9, one launch (start us, length us, event | category | flops | bytes accessed | tf_op | source)
XLA Modules:
  0.0 228.6 jit_solution(17561125479298199751)
XLA Ops:
  6.5 11.3 %collective-permute-done.1.refs_2_ = bf16[272,1024]{1,0:T(8,128)(2,1)S(1)} collective-permute-done((bf16[272,1024]{1,0:T(8,128)(2,1)}, bf16[272,1024]{1,0:T(8,128)(2,1)S(1)}, u32[]{:S(2)}, u32[]{:S(2)}) %collective-permute-start.1) | collective-permute-done | bytes 557088 | tf_op jit(solution)/shard_map/ppermute | solution.py:899
  23.1 7.6 %collective-permute-done.3.refs_9_.in_got = bf16[512,512]{1,0:T(8,128)(2,1)S(1)} collective-permute-done((bf16[512,512]{1,0:T(8,128)(2,1)}, bf16[512,512]{1,0:T(8,128)(2,1)S(1)}, u32[]{:S(2)}, u32[]{:S(2)}) %collective-permute-start.3) | collective-permute-done | bytes 524320 | tf_op jit(solution)/shard_map/ppermute | solution.py:902
  31.4 2.9 %collective-permute-start.7 = (bf16[272,1024]{1,0:T(8,128)(2,1)S(1)}, bf16[272,1024]{1,0:T(8,128)(2,1)S(1)}, u32[]{:S(2)}, u32[]{:S(2)}) collective-permute-start(bf16[272,1024]{1,0:T(8,128)(2,1)S(1)} %collective-permute-done.2.refs_3_), channel_id=1, source_target_pairs={{0,2},{2,0},{4,6},{6,4},{8,10},{10,8},{12,14},{14,12},{16,18},{18,... | collective-permute-start | bytes 1671176 | tf_op jit(solution)/shard_map/ppermute | solution.py:899
  37.7 12.3 %hidden.1 = (bf16[1024,1024]{1,0:T(8,128)(2,1)}, bf16[1024,1024]{1,0:T(8,128)(2,1)}, bf16[1024,512]{1,0:T(8,128)(2,1)}, bf16[1024,512]{1,0:T(8,128)(2,1)}, bf16[...) custom-call(bf16[272,1024]{1,0:T(8,128)(2,1)} %get-tuple-element.98., ...), custom_call_target="tpu_custom_call" | custom-call | flops 999999995904 | bytes 1000000000 | tf_op jit(solution)/shard_map/hidden/pallas_call | solution.py:360
  51.2 20.0 %attention.1 = (bf16[512,2048]{1,0:T(8,128)(2,1)}, bf16[512,2048]{1,0:T(8,128)(2,1)}, bf16[544,640]{1,0:T(8,128)(2,1)}, bf16[544,384]{1,0:T(8,128)(2,1)}) custom-call(bf16[1024,1024]{1,0:T(8,128)(2,1)} %get-tuple-element.105.normed, bf16[1024,1024]{1,0:T(8,128)(2,1)} %get-tuple-element.106.branch, bf16[1024,512]{1,0:T(8,128)(2,1)} %get-tuple-element.107.active, ...), custom_call_target="tpu_custom_call" | custom-call | flops 999999995904 | bytes 1000000000 | tf_op jit(solution)/shard_map/attention/pallas_call | solution.py:684
  73.3 3.2 %collective-permute-done.10 = bf16[512,1024]{1,0:T(8,128)(2,1)} collective-permute-done((bf16[512,1024]{1,0:T(8,128)(2,1)}, bf16[512,1024]{1,0:T(8,128)(2,1)}, u32[]{:S(2)}, u32[]{:S(2)}) %collective-permute-start.10) | collective-permute-done | bytes 1048608 | tf_op jit(solution)/shard_map/ppermute | solution.py:906
  79.0 3.2 %collective-permute-start.11 = (bf16[256,1024]{1,0:T(8,128)(2,1)S(1)}, bf16[256,1024]{1,0:T(8,128)(2,1)S(1)}, u32[]{:S(2)}, u32[]{:S(2)}) collective-permute-start(bf16[256,1024]{1,0:T(8,128)(2,1)S(1)} %add_convert_fusion.8), channel_id=1, source_target_pairs={{8,16},{10,18},{12,20},{14,22},{16,8},{18,10},{20,12},{22,14},{9,1... | collective-permute-start | bytes 1572872 | tf_op jit(solution)/shard_map/ppermute | solution.py:906
  86.6 6.6 %collective-permute-done.11 = bf16[256,1024]{1,0:T(8,128)(2,1)S(1)} collective-permute-done((bf16[256,1024]{1,0:T(8,128)(2,1)S(1)}, bf16[256,1024]{1,0:T(8,128)(2,1)S(1)}, u32[]{:S(2)}, u32[]{:S(2)}) %collective-permute-start.11) | collective-permute-done | bytes 524320 | tf_op jit(solution)/shard_map/ppermute | solution.py:906
  93.2 3.2 %collective-permute-start.15 = (bf16[256,1024]{1,0:T(8,128)(2,1)S(1)}, bf16[256,1024]{1,0:T(8,128)(2,1)}, u32[]{:S(2)}, u32[]{:S(2)}) collective-permute-start(bf16[256,1024]{1,0:T(8,128)(2,1)S(1)} %add_convert_fusion.9), channel_id=1, source_target_pairs={{8,16},{10,18},{12,20},{14,22},{16,8},{18,10},{20,12},{22,14},{9,1... | collective-permute-start | bytes 1572872 | tf_op jit(solution)/shard_map/ppermute | solution.py:906
  99.5 2.8 %fold.1 = bf16[256,2048]{1,0:T(8,128)(2,1)} custom-call(bf16[512,2048]{1,0:T(8,128)(2,1)} %get-tuple-element.130.a, bf16[512,2048]{1,0:T(8,128)(2,1)} %collective-permute-done.12.b), custom_call_target="tpu_custom_call" | custom-call | flops 1000000 | tf_op jit(solution)/shard_map/fold/pallas_call | solution.py:360
  122.0 5.4 %collective-permute-start.23 = (bf16[512,512]{1,0:T(8,128)(2,1)}, bf16[512,512]{1,0:T(8,128)(2,1)}, u32[]{:S(2)}, u32[]{:S(2)}) collective-permute-start(bf16[512,512]{1,0:T(8,128)(2,1)} %add_convert_fusion.3), channel_id=1, source_target_pairs={{8,0},{10,2},{12,4},{14,6},{16,24},{18,26},{20,28},{22,30},{9,1},{... | collective-permute-start | bytes 1572872 | tf_op jit(solution)/shard_map/ppermute | solution.py:906
  131.5 3.2 %keep.1 = (f32[128,2048]{1,0:T(8,128)}, bf16[128,2048]{1,0:T(8,128)(2,1)}) custom-call(bf16[512,2048]{1,0:T(8,128)(2,1)} %get-tuple-element.130.a, bf16[512,2048]{1,0:T(8,128)(2,1)} %collective-permute-done.12.b, bf16[256,2048]{1,0:T(8,128)(2,1)} %collective-permute-done.19.c), custom_call_target="tpu_custom_call" | custom-call | flops 1000000 | tf_op jit(solution)/shard_map/keep/pallas_call | solution.py:360
  136.0 4.8 %collective-permute-start.25 = (bf16[512,512]{1,0:T(8,128)(2,1)S(1)}, bf16[512,512]{1,0:T(8,128)(2,1)S(1)}, u32[]{:S(2)}, u32[]{:S(2)}) collective-permute-start(bf16[512,512]{1,0:T(8,128)(2,1)S(1)} %add_convert_fusion.2), channel_id=1, source_target_pairs={{8,0},{10,2},{12,4},{14,6},{16,24},{18,26},{20,28},{22,30},{9,1},{... | collective-permute-start | bytes 1572872 | tf_op jit(solution)/shard_map/ppermute | solution.py:906
  145.5 7.1 %collective-permute-start.27 = (bf16[256,1024]{1,0:T(8,128)(2,1)}, bf16[256,1024]{1,0:T(8,128)(2,1)S(1)}, u32[]{:S(2)}, u32[]{:S(2)}) collective-permute-start(bf16[256,1024]{1,0:T(8,128)(2,1)} %broadcast_select_fusion.2.refs_0_), channel_id=1, source_target_pairs={{0,2},{2,0},{4,6},{6,4},{8,10},{10,8},{12,14},{14,12},{16,18},{18,... | collective-permute-start | bytes 1572872 | tf_op jit(solution)/shard_map/ppermute | solution.py:899
  155.2 3.2 %place.4.refs_4_ = f32[2048,1024]{1,0:T(8,128)} custom-call(bf16[256,1024]{1,0:T(8,128)(2,1)} %broadcast_select_fusion.2.refs_0_, bf16[256,1024]{1,0:T(8,128)(2,1)} %collective-permute-done.26.refs_1_, bf16[256,1024]{1,0:T(8,128)(2,1)S(1)} %collective-permute-done.27.refs_2_, bf16[256,1024]{1,0:T(8,128)(2,1)S(1)} %collective-permute-done.28.refs_3_), custom_call_target="tpu_custom_call" | custom-call | flops 1000000 | tf_op jit(solution)/shard_map/place/pallas_call | solution.py:725
  159.9 3.9 %collective-permute-start.31 = (bf16[256,1024]{1,0:T(8,128)(2,1)S(1)}, bf16[256,1024]{1,0:T(8,128)(2,1)S(1)}, u32[]{:S(2)}, u32[]{:S(2)}) collective-permute-start(bf16[256,1024]{1,0:T(8,128)(2,1)S(1)} %broadcast_select_fusion.1.refs_0_), channel_id=1, source_target_pairs={{0,2},{2,0},{4,6},{6,4},{8,10},{10,8},{12,14},{14,12},{16,18},{18,... | collective-permute-start | bytes 1572872 | tf_op jit(solution)/shard_map/ppermute | solution.py:899
  163.8 3.2 %collective-permute-done.30.refs_1_ = bf16[256,1024]{1,0:T(8,128)(2,1)S(1)} collective-permute-done((bf16[256,1024]{1,0:T(8,128)(2,1)S(1)}, bf16[256,1024]{1,0:T(8,128)(2,1)S(1)}, u32[]{:S(2)}, u32[]{:S(2)}) %collective-permute-start.30) | collective-permute-done | bytes 524320 | tf_op jit(solution)/shard_map/ppermute | solution.py:899
  168.3 3.2 %collective-permute-start.34 = (bf16[544,384]{1,0:T(8,128)(2,1)S(1)}, bf16[544,384]{1,0:T(8,128)(2,1)S(1)}, u32[]{:S(2)}, u32[]{:S(2)}) collective-permute-start(bf16[544,384]{1,0:T(8,128)(2,1)S(1)} %add_convert_fusion.11), channel_id=1, source_target_pairs={{8,16},{10,18},{12,20},{14,22},{16,8},{18,10},{20,12},{22,14},{9,1... | collective-permute-start | bytes 1253384 | tf_op jit(solution)/shard_map/ppermute | solution.py:906
  176.2 5.2 %collective-permute-done.34 = bf16[544,384]{1,0:T(8,128)(2,1)S(1)} collective-permute-done((bf16[544,384]{1,0:T(8,128)(2,1)S(1)}, bf16[544,384]{1,0:T(8,128)(2,1)S(1)}, u32[]{:S(2)}, u32[]{:S(2)}) %collective-permute-start.34) | collective-permute-done | bytes 417824 | tf_op jit(solution)/shard_map/ppermute | solution.py:906
  186.6 9.4 %collective-permute-done.39.refs_1_ = bf16[512,512]{1,0:T(8,128)(2,1)S(1)} collective-permute-done((bf16[512,512]{1,0:T(8,128)(2,1)S(1)}, bf16[512,512]{1,0:T(8,128)(2,1)S(1)}, u32[]{:S(2)}, u32[]{:S(2)}) %collective-permute-start.39) | collective-permute-done | bytes 524320 | tf_op jit(solution)/shard_map/ppermute | solution.py:899
  205.8 5.2 %collective-permute-done.43.refs_1_ = bf16[544,640]{1,0:T(8,128)(2,1)} collective-permute-done((bf16[544,640]{1,0:T(8,128)(2,1)S(1)}, bf16[544,640]{1,0:T(8,128)(2,1)}, u32[]{:S(2)}, u32[]{:S(2)}) %collective-permute-start.43) | collective-permute-done | bytes 696352 | tf_op jit(solution)/shard_map/ppermute | solution.py:899
  215.5 4.4 %collective-permute-done.46.refs_5_ = bf16[544,384]{1,0:T(8,128)(2,1)} collective-permute-done((bf16[544,384]{1,0:T(8,128)(2,1)}, bf16[544,384]{1,0:T(8,128)(2,1)}, u32[]{:S(2)}, u32[]{:S(2)}) %collective-permute-start.46) | collective-permute-done | bytes 417824 | tf_op jit(solution)/shard_map/ppermute | solution.py:899
  221.1 3.8 %place_joint.1 = (f32[512,3072]{1,0:T(8,128)}, f32[512,1024]{1,0:T(8,128)}) custom-call(bf16[544,640]{1,0:T(8,128)(2,1)} %copy-done, bf16[544,640]{1,0:T(8,128)(2,1)} %collective-permute-done.43.refs_1_, bf16[544,640]{1,0:T(8,128)(2,1)} %collective-permute-done.44.refs_2_, bf16[544,640]{1,0:T(8,128)(2,1)} %collective-permute-done.45.refs_3_), custom_call_target="tpu_custom_call" | custom-call | flops 1000000 | tf_op jit(solution)/shard_map/place_joint/pallas_call | solution.py:360
  224.9 3.6 %place_other.1 = (f32[512,3072]{1,0:T(8,128)}, f32[1536]{0:T(1024)}, f32[2048]{0:T(1024)}, f32[512]{0:T(512)}, f32[512]{0:T(512)}, /*index=5*/f32[512]{0:T(512)}, f32[512]{0:T(512)}, f32[512]{0:T(512)}, f32[512]{0:T(512)}) custom-call(bf16[544,640]{1,0:T(8,128)(2,1)} %copy-done, ...), custom_call_target="tpu_custom_call", output_to_operand_aliasing={{0}: (8, {})} | custom-call | flops 1000000 | tf_op jit(solution)/shard_map/place_other/pallas_call | solution.py:1084
  (125 shorter events, 88.2 us)
Async XLA Ops:
  20.3 15.4 %collective-permute-start.4 = (bf16[272,1024]{1,0:T(8,128)(2,1)}, bf16[272,1024]{1,0:T(8,128)(2,1)S(1)}, u32[]{:S(2)}, u32[]{:S(2)}) collective-permute-start(bf16[272,1024]{1,0:T(8,128)(2,1)} %get-tuple-element.98.refs_0_), channel_id=1, source_target_pairs={{0,2},{2,0},{4,6},{6,4},{8,10},{10,8},{12,14},{14,12},{16,18},{18,... | collective-permute-start | bytes 1671176 | tf_op jit(solution)/shard_map/ppermute | solution.py:899
  34.4 16.8 %collective-permute-start.9 = (bf16[512,384]{1,0:T(8,128)(2,1)}, bf16[512,384]{1,0:T(8,128)(2,1)}, u32[]{:S(2)}, u32[]{:S(2)}) collective-permute-start(bf16[512,384]{1,0:T(8,128)(2,1)} %get-tuple-element.111), channel_id=1, source_target_pairs={{0,1},{1,0},{2,3},{3,2},{4,5},{5,4},{6,7},{7,6},{8,9},{9,8},{10,11... | collective-permute-start | bytes 1179656 | tf_op jit(solution)/shard_map/ppermute | solution.py:902
  49.9 26.6 %collective-permute-start.10 = (bf16[512,1024]{1,0:T(8,128)(2,1)}, bf16[512,1024]{1,0:T(8,128)(2,1)}, u32[]{:S(2)}, u32[]{:S(2)}) collective-permute-start(bf16[512,1024]{1,0:T(8,128)(2,1)} %get-tuple-element.116), channel_id=1, source_target_pairs={{0,8},{2,10},{4,12},{6,14},{24,16},{26,18},{28,20},{30,22},{1,9},{... | collective-permute-start | bytes 3145736 | tf_op jit(solution)/shard_map/ppermute | solution.py:906
  71.2 26.2 %collective-permute-start.12 = (bf16[512,2048]{1,0:T(8,128)(2,1)}, bf16[512,2048]{1,0:T(8,128)(2,1)}, u32[]{:S(2)}, u32[]{:S(2)}) collective-permute-start(bf16[512,2048]{1,0:T(8,128)(2,1)} %get-tuple-element.123), channel_id=1, source_target_pairs={{0,2},{2,0},{4,6},{6,4},{8,10},{10,8},{12,14},{14,12},{16,18},{18,... | collective-permute-start | bytes 6291464 | tf_op jit(solution)/shard_map/ppermute | solution.py:899
  82.2 20.1 %collective-permute-start.13 = (bf16[512,512]{1,0:T(8,128)(2,1)}, bf16[512,512]{1,0:T(8,128)(2,1)}, u32[]{:S(2)}, u32[]{:S(2)}) collective-permute-start(bf16[512,512]{1,0:T(8,128)(2,1)} %get-tuple-element.124), channel_id=1, source_target_pairs={{0,8},{2,10},{4,12},{6,14},{24,16},{26,18},{28,20},{30,22},{1,9},{... | collective-permute-start | bytes 1572872 | tf_op jit(solution)/shard_map/ppermute | solution.py:906
  83.5 37.1 %collective-permute-start.21 = (bf16[544,384]{1,0:T(8,128)(2,1)}, bf16[544,384]{1,0:T(8,128)(2,1)S(1)}, u32[]{:S(2)}, u32[]{:S(2)}) collective-permute-start(bf16[544,384]{1,0:T(8,128)(2,1)} %get-tuple-element.133), channel_id=1, source_target_pairs={{0,1},{1,0},{2,3},{3,2},{4,5},{5,4},{6,7},{7,6},{8,9},{9,8},{10,11... | collective-permute-start | bytes 1253384 | tf_op jit(solution)/shard_map/ppermute | solution.py:902
  85.3 22.3 %collective-permute-start.14 = (bf16[512,512]{1,0:T(8,128)(2,1)}, bf16[512,512]{1,0:T(8,128)(2,1)}, u32[]{:S(2)}, u32[]{:S(2)}) collective-permute-start(bf16[512,512]{1,0:T(8,128)(2,1)} %collective-permute-done.8), channel_id=1, source_target_pairs={{0,8},{2,10},{4,12},{6,14},{24,16},{26,18},{28,20},{30,22},{1,9},{... | collective-permute-start | bytes 1572872 | tf_op jit(solution)/shard_map/ppermute | solution.py:906
  93.2 17.6 %collective-permute-start.15 = (bf16[256,1024]{1,0:T(8,128)(2,1)S(1)}, bf16[256,1024]{1,0:T(8,128)(2,1)}, u32[]{:S(2)}, u32[]{:S(2)}) collective-permute-start(bf16[256,1024]{1,0:T(8,128)(2,1)S(1)} %add_convert_fusion.9), channel_id=1, source_target_pairs={{8,16},{10,18},{12,20},{14,22},{16,8},{18,10},{20,12},{22,14},{9,1... | collective-permute-start | bytes 1572872 | tf_op jit(solution)/shard_map/ppermute | solution.py:906
  97.4 16.0 %collective-permute-start.16 = (bf16[256,1024]{1,0:T(8,128)(2,1)}, bf16[256,1024]{1,0:T(8,128)(2,1)}, u32[]{:S(2)}, u32[]{:S(2)}) collective-permute-start(bf16[256,1024]{1,0:T(8,128)(2,1)} %add_convert_fusion.7), channel_id=1, source_target_pairs={{8,0},{10,2},{12,4},{14,6},{16,24},{18,26},{20,28},{22,30},{9,1},{... | collective-permute-start | bytes 1572872 | tf_op jit(solution)/shard_map/ppermute | solution.py:906
  107.6 22.6 %collective-permute-start.19 = (bf16[256,2048]{1,0:T(8,128)(2,1)}, bf16[256,2048]{1,0:T(8,128)(2,1)}, u32[]{:S(2)}, u32[]{:S(2)}) collective-permute-start(bf16[256,2048]{1,0:T(8,128)(2,1)} %fold.1), channel_id=1, source_target_pairs={{0,4},{2,6},{4,0},{6,2},{8,12},{10,14},{12,8},{14,10},{16,20},{18,... | collective-permute-start | bytes 3145736 | tf_op jit(solution)/shard_map/ppermute | solution.py:899
  115.3 19.4 %collective-permute-start.20 = (bf16[512,512]{1,0:T(8,128)(2,1)}, bf16[512,512]{1,0:T(8,128)(2,1)}, u32[]{:S(2)}, u32[]{:S(2)}) collective-permute-start(bf16[512,512]{1,0:T(8,128)(2,1)} %add_convert_fusion.5), channel_id=1, source_target_pairs={{8,16},{10,18},{12,20},{14,22},{16,8},{18,10},{20,12},{22,14},{9,1... | collective-permute-start | bytes 1572872 | tf_op jit(solution)/shard_map/ppermute | solution.py:906
  118.4 22.4 %collective-permute-start.22 = (bf16[544,640]{1,0:T(8,128)(2,1)}, bf16[544,640]{1,0:T(8,128)(2,1)}, u32[]{:S(2)}, u32[]{:S(2)}) collective-permute-start(bf16[544,640]{1,0:T(8,128)(2,1)} %get-tuple-element.136), channel_id=1, source_target_pairs={{0,8},{2,10},{4,12},{6,14},{24,16},{26,18},{28,20},{30,22},{1,9},{... | collective-permute-start | bytes 2088968 | tf_op jit(solution)/shard_map/ppermute | solution.py:906
  120.6 25.0 %collective-permute-start.26 = (bf16[256,1024]{1,0:T(8,128)(2,1)}, bf16[256,1024]{1,0:T(8,128)(2,1)}, u32[]{:S(2)}, u32[]{:S(2)}) collective-permute-start(bf16[256,1024]{1,0:T(8,128)(2,1)} %broadcast_select_fusion.2.refs_0_), channel_id=1, source_target_pairs={{0,4},{2,6},{4,0},{6,2},{8,12},{10,14},{12,8},{14,10},{16,20},{18,... | collective-permute-start | bytes 1572872 | tf_op jit(solution)/shard_map/ppermute | solution.py:899
  122.0 22.4 %collective-permute-start.23 = (bf16[512,512]{1,0:T(8,128)(2,1)}, bf16[512,512]{1,0:T(8,128)(2,1)}, u32[]{:S(2)}, u32[]{:S(2)}) collective-permute-start(bf16[512,512]{1,0:T(8,128)(2,1)} %add_convert_fusion.3), channel_id=1, source_target_pairs={{8,0},{10,2},{12,4},{14,6},{16,24},{18,26},{20,28},{22,30},{9,1},{... | collective-permute-start | bytes 1572872 | tf_op jit(solution)/shard_map/ppermute | solution.py:906
  130.2 22.6 %collective-permute-start.24 = (bf16[544,384]{1,0:T(8,128)(2,1)S(1)}, bf16[544,384]{1,0:T(8,128)(2,1)}, u32[]{:S(2)}, u32[]{:S(2)}) collective-permute-start(bf16[544,384]{1,0:T(8,128)(2,1)S(1)} %collective-permute-done.21), channel_id=1, source_target_pairs={{0,8},{2,10},{4,12},{6,14},{24,16},{26,18},{28,20},{30,22},{1,9},{... | collective-permute-start | bytes 1253384 | tf_op jit(solution)/shard_map/ppermute | solution.py:906
  136.0 19.0 %collective-permute-start.25 = (bf16[512,512]{1,0:T(8,128)(2,1)S(1)}, bf16[512,512]{1,0:T(8,128)(2,1)S(1)}, u32[]{:S(2)}, u32[]{:S(2)}) collective-permute-start(bf16[512,512]{1,0:T(8,128)(2,1)S(1)} %add_convert_fusion.2), channel_id=1, source_target_pairs={{8,0},{10,2},{12,4},{14,6},{16,24},{18,26},{20,28},{22,30},{9,1},{... | collective-permute-start | bytes 1572872 | tf_op jit(solution)/shard_map/ppermute | solution.py:906
  142.3 16.1 %collective-permute-start.29 = (bf16[544,640]{1,0:T(8,128)(2,1)S(1)}, bf16[544,640]{1,0:T(8,128)(2,1)S(1)}, u32[]{:S(2)}, u32[]{:S(2)}) collective-permute-start(bf16[544,640]{1,0:T(8,128)(2,1)S(1)} %add_convert_fusion.1), channel_id=1, source_target_pairs={{8,16},{10,18},{12,20},{14,22},{16,8},{18,10},{20,12},{22,14},{9,1... | collective-permute-start | bytes 2088968 | tf_op jit(solution)/shard_map/ppermute | solution.py:906
  158.5 17.6 %collective-permute-start.33 = (bf16[544,640]{1,0:T(8,128)(2,1)S(1)}, bf16[544,640]{1,0:T(8,128)(2,1)S(1)}, u32[]{:S(2)}, u32[]{:S(2)}) collective-permute-start(bf16[544,640]{1,0:T(8,128)(2,1)S(1)} %add_convert_fusion), channel_id=1, source_target_pairs={{8,0},{10,2},{12,4},{14,6},{16,24},{18,26},{20,28},{22,30},{9,1},{... | collective-permute-start | bytes 2088968 | tf_op jit(solution)/shard_map/ppermute | solution.py:906
  172.6 23.4 %collective-permute-start.39 = (bf16[512,512]{1,0:T(8,128)(2,1)S(1)}, bf16[512,512]{1,0:T(8,128)(2,1)S(1)}, u32[]{:S(2)}, u32[]{:S(2)}) collective-permute-start(bf16[512,512]{1,0:T(8,128)(2,1)S(1)} %broadcast_select_fusion.3.refs_0_), channel_id=1, source_target_pairs={{0,4},{2,6},{4,0},{6,2},{8,12},{10,14},{12,8},{14,10},{16,20},{18,... | collective-permute-start | bytes 1572872 | tf_op jit(solution)/shard_map/ppermute | solution.py:899
  173.0 24.8 %collective-permute-start.37 = (bf16[512,512]{1,0:T(8,128)(2,1)S(1)}, bf16[512,512]{1,0:T(8,128)(2,1)S(1)}, u32[]{:S(2)}, u32[]{:S(2)}) collective-permute-start(bf16[512,512]{1,0:T(8,128)(2,1)S(1)} %broadcast_select_fusion.4.refs_0_), channel_id=1, source_target_pairs={{0,2},{2,0},{4,6},{6,4},{8,10},{10,8},{12,14},{14,12},{16,18},{18,... | collective-permute-start | bytes 1572872 | tf_op jit(solution)/shard_map/ppermute | solution.py:899
  181.5 16.3 %collective-permute-start.35 = (bf16[544,384]{1,0:T(8,128)(2,1)S(1)}, bf16[544,384]{1,0:T(8,128)(2,1)S(1)}, u32[]{:S(2)}, u32[]{:S(2)}) collective-permute-start(bf16[544,384]{1,0:T(8,128)(2,1)S(1)} %add_convert_fusion.10), channel_id=1, source_target_pairs={{8,0},{10,2},{12,4},{14,6},{16,24},{18,26},{20,28},{22,30},{9,1},{... | collective-permute-start | bytes 1253384 | tf_op jit(solution)/shard_map/ppermute | solution.py:906
  182.8 28.2 %collective-permute-start.43 = (bf16[544,640]{1,0:T(8,128)(2,1)S(1)}, bf16[544,640]{1,0:T(8,128)(2,1)}, u32[]{:S(2)}, u32[]{:S(2)}) collective-permute-start(bf16[544,640]{1,0:T(8,128)(2,1)S(1)} %broadcast_select_fusion.refs_0_), channel_id=1, source_target_pairs={{0,4},{2,6},{4,0},{6,2},{8,12},{10,14},{12,8},{14,10},{16,20},{18,... | collective-permute-start | bytes 2088968 | tf_op jit(solution)/shard_map/ppermute | solution.py:899
  199.0 20.9 %collective-permute-start.46 = (bf16[544,384]{1,0:T(8,128)(2,1)}, bf16[544,384]{1,0:T(8,128)(2,1)}, u32[]{:S(2)}, u32[]{:S(2)}) collective-permute-start(bf16[544,384]{1,0:T(8,128)(2,1)} %broadcast_select_fusion.5.refs_4_), channel_id=1, source_target_pairs={{0,4},{2,6},{4,0},{6,2},{8,12},{10,14},{12,8},{14,10},{16,20},{18,... | collective-permute-start | bytes 1253384 | tf_op jit(solution)/shard_map/ppermute | solution.py:899
  204.8 16.3 %collective-permute-start.44 = (bf16[544,640]{1,0:T(8,128)(2,1)S(1)}, bf16[544,640]{1,0:T(8,128)(2,1)}, u32[]{:S(2)}, u32[]{:S(2)}) collective-permute-start(bf16[544,640]{1,0:T(8,128)(2,1)S(1)} %broadcast_select_fusion.refs_0_), channel_id=1, source_target_pairs={{0,2},{2,0},{4,6},{6,4},{8,10},{10,8},{12,14},{14,12},{16,18},{18,... | collective-permute-start | bytes 2088968 | tf_op jit(solution)/shard_map/ppermute | solution.py:899
  (35 other events, 365.7 us)

commit v2 on v1

--- a/solution.py
+++ b/solution.py
@@ -345,6 +345,7 @@
 TAIL = 16
 VECTORS = 32
 ANY = pl.BlockSpec(memory_space=pltpu.HBM)
+FREE = pl.BlockSpec(memory_space=pl.ANY)
 SCALAR = pl.BlockSpec(memory_space=pltpu.SMEM)
 WHOLE = pl.BlockSpec(memory_space=pltpu.VMEM)
 LIMIT = 63 * 2**20
@@ -363,7 +364,7 @@
         in_specs=[spec for _, spec in ins],
         out_specs=[spec for _, spec in outs],
         scratch_shapes=list(scratch),
-        compiler_params=pltpu.CompilerParams(vmem_limit_bytes=LIMIT),
+        compiler_params=pltpu.CompilerParams(vmem_limit_bytes=LIMIT if name in ("pack", "hidden") else LIMIT // 3),
         cost_estimate=COST if name == "hidden" else SMALL,
         name=name,
     )(*[array for array, _ in ins])
@@ -678,7 +679,7 @@
     half = shaped((2 * rows, 2 * width))
     args = [*blocks, *whole, *tables, *small]
     specs = [block(a, h) for a, h in zip(blocks, [rows] * 5 + [16])]
-    specs += [ANY] * 6 + [full(a.shape) for a in [whole[6], *tables, *small]]
+    specs += [ANY, FREE, ANY, ANY, ANY, FREE] + [full(a.shape) for a in [whole[6], *tables, *small]]
     sums = [(width, wide), (part, width), (8, width), (1, wide), (VECTORS, wide)]
     weights = [(width, wide), (part, width), (hidden, width), (width, hidden)]
     return pl.pallas_call(
@@ -753,7 +754,7 @@
         copies.start(a_v, out).wait()
 
     scratch = [pltpu.VMEM(shape, BF16)] * 2 + [pltpu.SemaphoreType.DMA((3,))]
-    return call(kernel, name, [(left, ANY), (right, ANY)], [(shaped(shape), ANY)], scratch)[0]
+    return call(kernel, name, [(left, FREE), (right, FREE)], [(shaped(shape), FREE)], scratch)[0]
 
 
 def keep_sum(near, far, got):
@@ -775,7 +776,7 @@
     return call(
         kernel,
         "keep",
-        [(near, ANY), (far, ANY), (got, ANY)],
+        [(near, FREE), (far, FREE), (got, FREE)],
         [(shaped((count, width), F32), ANY), (shaped((count, width)), ANY)],
         scratch + [pltpu.SemaphoreType.DMA((5,))],
     )
@@ -884,11 +885,10 @@
 
 
 ORDER = (
-    "far", "mob", "moa", "coa", "fold", "tja", "mia", "mib", "cob", "poa",
-    "xoa", "cia", "tjb", "pob", "keep", "xob", "cib", "mja", "pia", "xia",
-    "sob", "soa", "mjb", "pib", "xib", "loa", "cja", "sia", "lob", "pja",
-    "cjb", "xja", "sib", "pjb", "xjb", "lia", "lib", "sja", "end", "sjb",
-    "lja",
+    "far", "moa", "mob", "coa", "mia", "fold", "poa", "mib", "xoa", "cob",
+    "tjb", "cia", "pob", "xob", "keep", "soa", "cib", "mja", "pia", "xia",
+    "mjb", "pib", "loa", "sob", "sia", "cja", "xib", "lob", "cjb", "pja",
+    "sib", "xja", "lia", "pjb", "lib", "sja", "xjb", "end", "sjb", "lja",
 )
 
 
@@ -945,8 +945,8 @@
         normed, xhat, active, grad_before, branch, out_all, in_mine, in_theirs, params, lens, in_sum = call(
             hidden_kernel,
             "hidden",
-            [(p, ANY) for p in pieces]
-            + [(in_weight, ANY), (in_got, ANY), (out_weight, ANY), (in_b, WHOLE)],
+            [(p, FREE) for p in pieces]
+            + [(in_weight, ANY), (in_got, FREE), (out_weight, ANY), (in_b, WHOLE)],
             [
                 (shaped((rows, width)), ANY),
                 (shaped((rows, width)), ANY),
@@ -1026,6 +1026,7 @@
         )
         did(joint_a)
         got = line_permute(out_all, [(0, 1), (3, 2)])
+        got = after(got, in_other)
         half = part_f // 2
         state = {"oa": (out_all[:half], got[:half]), "ob": (out_all[half:], got[half:])}
         state |= {"ia": in_mine, "ib": in_other, "ja": joint_a}
@@ -1052,7 +1053,7 @@
                 total_qkv, total_dense = call(
                     joint_kernel,
                     "place_joint",
-                    [(then(held[0]), ANY)] + [(a, ANY) for a in held[1:]],
+                    [(then(held[0]), FREE)] + [(a, FREE) for a in held[1:]],
                     [(shaped((owned, 3 * width), F32), ANY), (shaped((owned, width), F32), ANY)],
                     [
                         pltpu.VMEM((4, owned, held[0].shape[1]), BF16),
@@ -1084,8 +1085,8 @@
         total_qkv, *vectors = pl.pallas_call(
             other_kernel,
             out_shape=[shaped(total_qkv.shape, F32)] + [shaped((n,), F32) for n in sizes],
-            in_specs=[ANY] * 9,
-            out_specs=[ANY] + [WHOLE] * 8,
+            in_specs=[FREE] * 9,
+            out_specs=[FREE] + [WHOLE] * 8,
             scratch_shapes=[
                 pltpu.VMEM((4, owned + VECTORS, wide), BF16),
                 pltpu.VMEM((4, owned + VECTORS, wide), F32),
@@ -1096,7 +1097,7 @@
                 pltpu.SemaphoreType.DMA((20,)),
             ],
             input_output_aliases={8: 0},
-            compiler_params=pltpu.CompilerParams(vmem_limit_bytes=LIMIT),
+            compiler_params=pltpu.CompilerParams(vmem_limit_bytes=LIMIT // 3),
             cost_estimate=SMALL,
             name="place_other",
         )(*joint_a, *joint_b, total_qkv)

time: 230 us -> 211 us (0.917)
  other arithmetic: 17.3 us -> 6.68 us
  Pallas kernels: 61 us -> 55.6 us
  waiting for transfers between devices: 65.4 us -> 62.6 us
    ppermute x26, waiting for transfers between devices: 37.4 us -> 27.4 us  [swap_rep(): return lax.ppermute(values, 'rep', [(i, i ^ bit) for i in range(reps)])]
    ppermute x17, waiting for transfers between devices: 18.1 us -> 26.7 us  [line_permute(): return lax.ppermute(values, 'rep', pairs)]
    convert_element_type x12, other arithmetic: 13.3 us -> 6.32 us  [added(): total = (left.astype(F32) + right.astype(F32)).astype(BF16)]
    pallas_call x6, Pallas kernels: 27.4 us -> 23 us  [call(): pl.pallas_call(kernel, out_shape=[shape for shape, _ in outs], in_specs=[...]
    select_n x6, other arithmetic: 4.02 us -> 0.36 us  [spread(): return did(jnp.where(inner_line, then(both), got))]
    ppermute x17, starting transfers between devices: 38.5 us -> 35 us  [line_permute(): return lax.ppermute(values, 'rep', pairs)]
  transfers between devices with their start and end apart: 49 -> 49, of which waited for: 18 -> 18; matrix products, arithmetic and copies ran while one was open for 8% -> 4% of each run, Pallas kernels for 24% -> 24%
where the time goes in v2:
time: 211 us; the launch traced here: 209 us
  starting transfers between devices  77.8 us (37%)
  waiting for transfers between devices  62.6 us (30%)
  Pallas kernels  55.6 us (26%)
  other arithmetic  6.68 us (3%)
  local copies, waits for them, and re-layouts  3.85 us (2%)
    ppermute x26, starting transfers between devices, swap_rep(): return lax.ppermute(values, 'rep', [(i, i ^ bit) for i in range(reps)])  36.1 us
    ppermute x17, starting transfers between devices, line_permute(): return lax.ppermute(values, 'rep', pairs)  35 us
    ppermute x26, waiting for transfers between devices, swap_rep(): return lax.ppermute(values, 'rep', [(i, i ^ bit) for i in range(reps)])  27.4 us
    ppermute x17, waiting for transfers between devices, line_permute(): return lax.ppermute(values, 'rep', pairs)  26.7 us
    pallas_call x6, Pallas kernels, call(): pl.pallas_call(kernel, out_shape=[shape for shape, _ in outs], in_specs=[...  23 us
    pallas_call x1, Pallas kernels, attention(): pl.pallas_call(attention_kernel, grid=(steps,), out_shape=[half, half, sh...  20 us
    pallas_call x4, Pallas kernels, placed(): pl.pallas_call(kernel, in_specs=[pl.BlockSpec(memory_space=pl.ANY)] * len...  9.16 us
    ppermute x6, waiting for transfers between devices, swap_shard(): return lax.ppermute(values, 'shard', [(0, 1), (1, 0)])  8.46 us
  transfers between devices with their start and end apart: 49, of which 18 were waited for; matrix products, arithmetic and copies ran while one was open for 4% of the time, Pallas kernels for 24%

profile of v2, /device:TPU:9, one launch (start us, length us, event | category | flops | bytes accessed | tf_op | source)
XLA Modules:
  0.0 208.6 jit_solution(7060052367129349569)
XLA Ops:
  1.3 2.7 %pack.1 = (bf16[272,1024]{1,0:T(8,128)(2,1)}, f32[1,1024]{1,0:T(1,128)}, f32[1,512]{1,0:T(1,128)}, bf16[512,512]{1,0:T(8,128)(2,1)}, bf16[512,384]{1,0:T(8,128)(2,1)}) custom-call(s32[1]{0:T(128)S(6)} %copy.38.length, bf16[128,1024]{1,0:T(8,128)(2,1)} %tok.3, bf16[128,1024]{1,0:T(8,128)(2,1)} %cot.3, bf16[2048]{0:T(1024)(128)(2,1)} %in_bias.1, ...), custom_call_target="tpu_custom_call" | custom-call | flops 1000000 | tf_op jit(solution)/shard_map/pack/pallas_call | solution.py:361
  6.5 11.3 %collective-permute-done.1.refs_2_ = bf16[272,1024]{1,0:T(8,128)(2,1)S(1)} collective-permute-done((bf16[272,1024]{1,0:T(8,128)(2,1)}, bf16[272,1024]{1,0:T(8,128)(2,1)S(1)}, u32[]{:S(2)}, u32[]{:S(2)}) %collective-permute-start.1) | collective-permute-done | bytes 557088 | tf_op jit(solution)/shard_map/ppermute | solution.py:899
  23.1 7.6 %collective-permute-done.3.refs_9_.in_got = bf16[512,512]{1,0:T(8,128)(2,1)S(1)} collective-permute-done((bf16[512,512]{1,0:T(8,128)(2,1)}, bf16[512,512]{1,0:T(8,128)(2,1)S(1)}, u32[]{:S(2)}, u32[]{:S(2)}) %collective-permute-start.3) | collective-permute-done | bytes 524320 | tf_op jit(solution)/shard_map/ppermute | solution.py:902
  31.4 2.9 %collective-permute-start.7 = (bf16[272,1024]{1,0:T(8,128)(2,1)S(1)}, bf16[272,1024]{1,0:T(8,128)(2,1)S(1)}, u32[]{:S(2)}, u32[]{:S(2)}) collective-permute-start(bf16[272,1024]{1,0:T(8,128)(2,1)S(1)} %collective-permute-done.2.refs_3_), channel_id=1, source_target_pairs={{0,2},{2,0},{4,6},{6,4},{8,10},{10,8},{12,14},{14,12},{16,18},{18,... | collective-permute-start | bytes 1671176 | tf_op jit(solution)/shard_map/ppermute | solution.py:899
  37.7 12.3 %hidden.1 = (bf16[1024,1024]{1,0:T(8,128)(2,1)}, bf16[1024,1024]{1,0:T(8,128)(2,1)}, bf16[1024,512]{1,0:T(8,128)(2,1)}, bf16[1024,512]{1,0:T(8,128)(2,1)}, bf16[...) custom-call(bf16[272,1024]{1,0:T(8,128)(2,1)} %get-tuple-element.98., ...), custom_call_target="tpu_custom_call" | custom-call | flops 999999995904 | bytes 1000000000 | tf_op jit(solution)/shard_map/hidden/pallas_call | solution.py:361
  51.6 20.0 %attention.1 = (bf16[512,2048]{1,0:T(8,128)(2,1)}, bf16[512,2048]{1,0:T(8,128)(2,1)}, bf16[544,640]{1,0:T(8,128)(2,1)}, bf16[544,384]{1,0:T(8,128)(2,1)}) custom-call(bf16[1024,1024]{1,0:T(8,128)(2,1)} %get-tuple-element.105.normed, bf16[1024,1024]{1,0:T(8,128)(2,1)} %get-tuple-element.106.branch, bf16[1024,512]{1,0:T(8,128)(2,1)} %get-tuple-element.107.active, ...), custom_call_target="tpu_custom_call" | custom-call | flops 999999995904 | bytes 1000000000 | tf_op jit(solution)/shard_map/attention/pallas_call | solution.py:685
  73.6 3.0 %collective-permute-done.10 = bf16[512,1024]{1,0:T(8,128)(2,1)} collective-permute-done((bf16[512,1024]{1,0:T(8,128)(2,1)}, bf16[512,1024]{1,0:T(8,128)(2,1)}, u32[]{:S(2)}, u32[]{:S(2)}) %collective-permute-start.10) | collective-permute-done | bytes 1048608 | tf_op jit(solution)/shard_map/ppermute | solution.py:906
  77.8 3.2 %collective-permute-start.11 = (bf16[256,1024]{1,0:T(8,128)(2,1)S(1)}, bf16[256,1024]{1,0:T(8,128)(2,1)S(1)}, u32[]{:S(2)}, u32[]{:S(2)}) collective-permute-start(bf16[256,1024]{1,0:T(8,128)(2,1)S(1)} %add_convert_fusion.9), channel_id=1, source_target_pairs={{8,16},{10,18},{12,20},{14,22},{16,8},{18,10},{20,12},{22,14},{9,1... | collective-permute-start | bytes 1572872 | tf_op jit(solution)/shard_map/ppermute | solution.py:906
  83.7 8.0 %collective-permute-done.11 = bf16[256,1024]{1,0:T(8,128)(2,1)S(1)} collective-permute-done((bf16[256,1024]{1,0:T(8,128)(2,1)S(1)}, bf16[256,1024]{1,0:T(8,128)(2,1)S(1)}, u32[]{:S(2)}, u32[]{:S(2)}) %collective-permute-start.11) | collective-permute-done | bytes 524320 | tf_op jit(solution)/shard_map/ppermute | solution.py:906
  95.3 3.2 %collective-permute-start.16 = (bf16[256,1024]{1,0:T(8,128)(2,1)S(1)}, bf16[256,1024]{1,0:T(8,128)(2,1)S(1)}, u32[]{:S(2)}, u32[]{:S(2)}) collective-permute-start(bf16[256,1024]{1,0:T(8,128)(2,1)S(1)} %add_convert_fusion.8), channel_id=1, source_target_pairs={{8,16},{10,18},{12,20},{14,22},{16,8},{18,10},{20,12},{22,14},{9,1... | collective-permute-start | bytes 1572872 | tf_op jit(solution)/shard_map/ppermute | solution.py:906
  112.5 7.0 %collective-permute-done.17 = bf16[512,512]{1,0:T(8,128)(2,1)S(1)} collective-permute-done((bf16[512,512]{1,0:T(8,128)(2,1)S(1)}, bf16[512,512]{1,0:T(8,128)(2,1)S(1)}, u32[]{:S(2)}, u32[]{:S(2)}) %collective-permute-start.17) | collective-permute-done | bytes 524320 | tf_op jit(solution)/shard_map/ppermute | solution.py:906
  119.5 3.2 %collective-permute-start.20 = (bf16[512,512]{1,0:T(8,128)(2,1)S(1)}, bf16[512,512]{1,0:T(8,128)(2,1)S(1)}, u32[]{:S(2)}, u32[]{:S(2)}) collective-permute-start(bf16[512,512]{1,0:T(8,128)(2,1)S(1)} %add_convert_fusion.5), channel_id=1, source_target_pairs={{8,16},{10,18},{12,20},{14,22},{16,8},{18,10},{20,12},{22,14},{9,1... | collective-permute-start | bytes 1572872 | tf_op jit(solution)/shard_map/ppermute | solution.py:906
  128.5 3.0 %collective-permute-done.20 = bf16[512,512]{1,0:T(8,128)(2,1)S(1)} collective-permute-done((bf16[512,512]{1,0:T(8,128)(2,1)S(1)}, bf16[512,512]{1,0:T(8,128)(2,1)S(1)}, u32[]{:S(2)}, u32[]{:S(2)}) %collective-permute-start.20) | collective-permute-done | bytes 524320 | tf_op jit(solution)/shard_map/ppermute | solution.py:906
  136.0 3.2 %collective-permute-start.29 = (bf16[544,640]{1,0:T(8,128)(2,1)S(1)}, bf16[544,640]{1,0:T(8,128)(2,1)S(1)}, u32[]{:S(2)}, u32[]{:S(2)}) collective-permute-start(bf16[544,640]{1,0:T(8,128)(2,1)S(1)} %add_convert_fusion.1), channel_id=1, source_target_pairs={{8,16},{10,18},{12,20},{14,22},{16,8},{18,10},{20,12},{22,14},{9,1... | collective-permute-start | bytes 2088968 | tf_op jit(solution)/shard_map/ppermute | solution.py:906
  139.2 9.3 %collective-permute-start.27 = (bf16[256,1024]{1,0:T(8,128)(2,1)S(1)}, bf16[256,1024]{1,0:T(8,128)(2,1)S(1)}, u32[]{:S(2)}, u32[]{:S(2)}) collective-permute-start(bf16[256,1024]{1,0:T(8,128)(2,1)S(1)} %broadcast_select_fusion.2.refs_0_), channel_id=1, source_target_pairs={{0,2},{2,0},{4,6},{6,4},{8,10},{10,8},{12,14},{14,12},{16,18},{18,... | collective-permute-start | bytes 1572872 | tf_op jit(solution)/shard_map/ppermute | solution.py:899
  153.8 4.1 %collective-permute-start.34 = (bf16[544,640]{1,0:T(8,128)(2,1)S(1)}, bf16[544,640]{1,0:T(8,128)(2,1)S(1)}, u32[]{:S(2)}, u32[]{:S(2)}) collective-permute-start(bf16[544,640]{1,0:T(8,128)(2,1)S(1)} %add_convert_fusion), channel_id=1, source_target_pairs={{8,0},{10,2},{12,4},{14,6},{16,24},{18,26},{20,28},{22,30},{9,1},{... | collective-permute-start | bytes 2088968 | tf_op jit(solution)/shard_map/ppermute | solution.py:906
  166.6 3.0 %collective-permute-done.33 = bf16[544,384]{1,0:T(8,128)(2,1)S(1)} collective-permute-done((bf16[544,384]{1,0:T(8,128)(2,1)S(1)}, bf16[544,384]{1,0:T(8,128)(2,1)S(1)}, u32[]{:S(2)}, u32[]{:S(2)}) %collective-permute-start.33) | collective-permute-done | bytes 417824 | tf_op jit(solution)/shard_map/ppermute | solution.py:906
  173.1 3.2 %collective-permute-done.39.refs_1_ = bf16[512,512]{1,0:T(8,128)(2,1)S(1)} collective-permute-done((bf16[512,512]{1,0:T(8,128)(2,1)S(1)}, bf16[512,512]{1,0:T(8,128)(2,1)S(1)}, u32[]{:S(2)}, u32[]{:S(2)}) %collective-permute-start.39) | collective-permute-done | bytes 524320 | tf_op jit(solution)/shard_map/ppermute | solution.py:899
  182.2 2.3 %place.7 = f32[512,4096]{1,0:T(8,128)} custom-call(bf16[512,512]{1,0:T(8,128)(2,1)S(1)} %broadcast_select_fusion.3.refs_0_, bf16[512,512]{1,0:T(8,128)(2,1)S(1)} %collective-permute-done.39.refs_1_, bf16[512,512]{1,0:T(8,128)(2,1)S(1)} %collective-permute-done.40.refs_2_, ...), custom_call_target="tpu_custom_call", output_to_operand_aliasing={{}: (4, {})} | custom-call | flops 1000000 | tf_op jit(solution)/shard_map/place/pallas_call | solution.py:726
  186.7 3.9 %collective-permute-done.43.refs_1_ = bf16[544,640]{1,0:T(8,128)(2,1)S(1)} collective-permute-done((bf16[544,640]{1,0:T(8,128)(2,1)S(1)}, bf16[544,640]{1,0:T(8,128)(2,1)S(1)}, u32[]{:S(2)}, u32[]{:S(2)}) %collective-permute-start.43) | collective-permute-done | bytes 696352 | tf_op jit(solution)/shard_map/ppermute | solution.py:899
  190.6 3.5 %collective-permute-start.45 = (bf16[544,640]{1,0:T(8,128)(2,1)S(1)}, bf16[544,640]{1,0:T(8,128)(2,1)S(1)}, u32[]{:S(2)}, u32[]{:S(2)}) collective-permute-start(bf16[544,640]{1,0:T(8,128)(2,1)S(1)} %collective-permute-done.43.refs_1_), channel_id=1, source_target_pairs={{0,2},{2,0},{4,6},{6,4},{8,10},{10,8},{12,14},{14,12},{16,18},{18,... | collective-permute-start | bytes 2088968 | tf_op jit(solution)/shard_map/ppermute | solution.py:899
  195.3 4.2 %collective-permute-done.46.refs_5_ = bf16[544,384]{1,0:T(8,128)(2,1)S(1)} collective-permute-done((bf16[544,384]{1,0:T(8,128)(2,1)S(1)}, bf16[544,384]{1,0:T(8,128)(2,1)S(1)}, u32[]{:S(2)}, u32[]{:S(2)}) %collective-permute-start.46) | collective-permute-done | bytes 417824 | tf_op jit(solution)/shard_map/ppermute | solution.py:899
  201.5 3.5 %place_joint.1 = (f32[512,3072]{1,0:T(8,128)}, f32[512,1024]{1,0:T(8,128)}) custom-call(bf16[544,640]{1,0:T(8,128)(2,1)S(1)} %broadcast_select_fusion.refs_0_, bf16[544,640]{1,0:T(8,128)(2,1)S(1)} %collective-permute-done.43.refs_1_, bf16[544,640]{1,0:T(8,128)(2,1)S(1)} %collective-permute-done.44.refs_2_, bf16[544,640]{1,0:T(8,128)(2,1)S(1)} %collective-permute-done.45.refs_3_), custom_call_target="tpu_custom_call" | custom-call | flops 1000000 | tf_op jit(solution)/shard_map/place_joint/pallas_call | solution.py:361
  205.0 3.4 %place_other.1 = (f32[512,3072]{1,0:T(8,128)}, f32[1536]{0:T(1024)}, f32[2048]{0:T(1024)}, f32[512]{0:T(512)}, f32[512]{0:T(512)}, /*index=5*/f32[512]{0:T(512)}, f32[512]{0:T(512)}, f32[512]{0:T(512)}, f32[512]{0:T(512)}) custom-call(bf16[544,640]{1,0:T(8,128)(2,1)S(1)} %broadcast_select_fusion.refs_0_, ...), custom_call_target="tpu_custom_call", output_to_operand_aliasing={{0}: (8, {})} | custom-call | flops 1000000 | tf_op jit(solution)/shard_map/place_other/pallas_call | solution.py:1085
  (133 shorter events, 75.7 us)
Async XLA Ops:
  4.0 13.8 %collective-permute-start.1 = (bf16[272,1024]{1,0:T(8,128)(2,1)}, bf16[272,1024]{1,0:T(8,128)(2,1)S(1)}, u32[]{:S(2)}, u32[]{:S(2)}) collective-permute-start(bf16[272,1024]{1,0:T(8,128)(2,1)} %get-tuple-element.98.refs_0_), channel_id=1, source_target_pairs={{0,4},{2,6},{4,0},{6,2},{8,12},{10,14},{12,8},{14,10},{16,20},{18,... | collective-permute-start | bytes 1671176 | tf_op jit(solution)/shard_map/ppermute | solution.py:899
  20.3 15.4 %collective-permute-start.4 = (bf16[272,1024]{1,0:T(8,128)(2,1)}, bf16[272,1024]{1,0:T(8,128)(2,1)S(1)}, u32[]{:S(2)}, u32[]{:S(2)}) collective-permute-start(bf16[272,1024]{1,0:T(8,128)(2,1)} %get-tuple-element.98.refs_0_), channel_id=1, source_target_pairs={{0,2},{2,0},{4,6},{6,4},{8,10},{10,8},{12,14},{14,12},{16,18},{18,... | collective-permute-start | bytes 1671176 | tf_op jit(solution)/shard_map/ppermute | solution.py:899
  34.4 17.2 %collective-permute-start.9 = (bf16[512,384]{1,0:T(8,128)(2,1)}, bf16[512,384]{1,0:T(8,128)(2,1)}, u32[]{:S(2)}, u32[]{:S(2)}) collective-permute-start(bf16[512,384]{1,0:T(8,128)(2,1)} %get-tuple-element.111), channel_id=1, source_target_pairs={{0,1},{1,0},{2,3},{3,2},{4,5},{5,4},{6,7},{7,6},{8,9},{9,8},{10,11... | collective-permute-start | bytes 1179656 | tf_op jit(solution)/shard_map/ppermute | solution.py:902
  50.0 23.6 %collective-permute-start.8 = (bf16[512,512]{1,0:T(8,128)(2,1)}, bf16[512,512]{1,0:T(8,128)(2,1)}, u32[]{:S(2)}, u32[]{:S(2)}) collective-permute-start(bf16[512,512]{1,0:T(8,128)(2,1)} %get-tuple-element.103), channel_id=1, source_target_pairs={{0,1},{1,0},{2,3},{3,2},{4,5},{5,4},{6,7},{7,6},{8,9},{9,8},{10,11... | collective-permute-start | bytes 1572872 | tf_op jit(solution)/shard_map/ppermute | solution.py:902
  50.3 26.2 %collective-permute-start.10 = (bf16[512,1024]{1,0:T(8,128)(2,1)}, bf16[512,1024]{1,0:T(8,128)(2,1)}, u32[]{:S(2)}, u32[]{:S(2)}) collective-permute-start(bf16[512,1024]{1,0:T(8,128)(2,1)} %get-tuple-element.104), channel_id=1, source_target_pairs={{0,8},{2,10},{4,12},{6,14},{24,16},{26,18},{28,20},{30,22},{1,9},{... | collective-permute-start | bytes 3145736 | tf_op jit(solution)/shard_map/ppermute | solution.py:906
  71.6 30.5 %collective-permute-start.13 = (bf16[512,2048]{1,0:T(8,128)(2,1)}, bf16[512,2048]{1,0:T(8,128)(2,1)}, u32[]{:S(2)}, u32[]{:S(2)}) collective-permute-start(bf16[512,2048]{1,0:T(8,128)(2,1)} %get-tuple-element.125), channel_id=1, source_target_pairs={{0,2},{2,0},{4,6},{6,4},{8,10},{10,8},{12,14},{14,12},{16,18},{18,... | collective-permute-start | bytes 6291464 | tf_op jit(solution)/shard_map/ppermute | solution.py:899
  77.8 13.9 %collective-permute-start.11 = (bf16[256,1024]{1,0:T(8,128)(2,1)S(1)}, bf16[256,1024]{1,0:T(8,128)(2,1)S(1)}, u32[]{:S(2)}, u32[]{:S(2)}) collective-permute-start(bf16[256,1024]{1,0:T(8,128)(2,1)S(1)} %add_convert_fusion.9), channel_id=1, source_target_pairs={{8,16},{10,18},{12,20},{14,22},{16,8},{18,10},{20,12},{22,14},{9,1... | collective-permute-start | bytes 1572872 | tf_op jit(solution)/shard_map/ppermute | solution.py:906
  81.0 17.5 %collective-permute-start.12 = (bf16[512,512]{1,0:T(8,128)(2,1)}, bf16[512,512]{1,0:T(8,128)(2,1)}, u32[]{:S(2)}, u32[]{:S(2)}) collective-permute-start(bf16[512,512]{1,0:T(8,128)(2,1)} %get-tuple-element.122), channel_id=1, source_target_pairs={{0,8},{2,10},{4,12},{6,14},{24,16},{26,18},{28,20},{30,22},{1,9},{... | collective-permute-start | bytes 1572872 | tf_op jit(solution)/shard_map/ppermute | solution.py:906
  99.8 19.7 %collective-permute-start.17 = (bf16[512,512]{1,0:T(8,128)(2,1)S(1)}, bf16[512,512]{1,0:T(8,128)(2,1)S(1)}, u32[]{:S(2)}, u32[]{:S(2)}) collective-permute-start(bf16[512,512]{1,0:T(8,128)(2,1)S(1)} %add_convert_fusion.6), channel_id=1, source_target_pairs={{8,16},{10,18},{12,20},{14,22},{16,8},{18,10},{20,12},{22,14},{9,1... | collective-permute-start | bytes 1572872 | tf_op jit(solution)/shard_map/ppermute | solution.py:906
  103.8 21.8 %collective-permute-start.19 = (bf16[256,2048]{1,0:T(8,128)(2,1)S(1)}, bf16[256,2048]{1,0:T(8,128)(2,1)S(1)}, u32[]{:S(2)}, u32[]{:S(2)}) collective-permute-start(bf16[256,2048]{1,0:T(8,128)(2,1)S(1)} %fold.1), channel_id=1, source_target_pairs={{0,4},{2,6},{4,0},{6,2},{8,12},{10,14},{12,8},{14,10},{16,20},{18,... | collective-permute-start | bytes 3145736 | tf_op jit(solution)/shard_map/ppermute | solution.py:899
  108.5 15.6 %collective-permute-start.18 = (bf16[256,1024]{1,0:T(8,128)(2,1)S(1)}, bf16[256,1024]{1,0:T(8,128)(2,1)S(1)}, u32[]{:S(2)}, u32[]{:S(2)}) collective-permute-start(bf16[256,1024]{1,0:T(8,128)(2,1)S(1)} %add_convert_fusion.4), channel_id=1, source_target_pairs={{8,0},{10,2},{12,4},{14,6},{16,24},{18,26},{20,28},{22,30},{9,1},{... | collective-permute-start | bytes 1572872 | tf_op jit(solution)/shard_map/ppermute | solution.py:906
  111.2 21.5 %collective-permute-start.22 = (bf16[544,640]{1,0:T(8,128)(2,1)S(1)}, bf16[544,640]{1,0:T(8,128)(2,1)S(1)}, u32[]{:S(2)}, u32[]{:S(2)}) collective-permute-start(bf16[544,640]{1,0:T(8,128)(2,1)S(1)} %copy-done.4), channel_id=1, source_target_pairs={{0,8},{2,10},{4,12},{6,14},{24,16},{26,18},{28,20},{30,22},{1,9},{... | collective-permute-start | bytes 2088968 | tf_op jit(solution)/shard_map/ppermute | solution.py:906
  122.8 25.7 %collective-permute-start.23 = (bf16[512,512]{1,0:T(8,128)(2,1)S(1)}, bf16[512,512]{1,0:T(8,128)(2,1)S(1)}, u32[]{:S(2)}, u32[]{:S(2)}) collective-permute-start(bf16[512,512]{1,0:T(8,128)(2,1)S(1)} %add_convert_fusion.3), channel_id=1, source_target_pairs={{8,0},{10,2},{12,4},{14,6},{16,24},{18,26},{20,28},{22,30},{9,1},{... | collective-permute-start | bytes 1572872 | tf_op jit(solution)/shard_map/ppermute | solution.py:906
  124.1 15.0 %collective-permute-start.24 = (bf16[544,384]{1,0:T(8,128)(2,1)S(1)}, bf16[544,384]{1,0:T(8,128)(2,1)S(1)}, u32[]{:S(2)}, u32[]{:S(2)}) collective-permute-start(bf16[544,384]{1,0:T(8,128)(2,1)S(1)} %collective-permute-done.21), channel_id=1, source_target_pairs={{0,8},{2,10},{4,12},{6,14},{24,16},{26,18},{28,20},{30,22},{1,9},{... | collective-permute-start | bytes 1253384 | tf_op jit(solution)/shard_map/ppermute | solution.py:906
  131.5 21.6 %collective-permute-start.30 = (bf16[256,1024]{1,0:T(8,128)(2,1)S(1)}, bf16[256,1024]{1,0:T(8,128)(2,1)S(1)}, u32[]{:S(2)}, u32[]{:S(2)}) collective-permute-start(bf16[256,1024]{1,0:T(8,128)(2,1)S(1)} %broadcast_select_fusion.1.refs_0_), channel_id=1, source_target_pairs={{0,4},{2,6},{4,0},{6,2},{8,12},{10,14},{12,8},{14,10},{16,20},{18,... | collective-permute-start | bytes 1572872 | tf_op jit(solution)/shard_map/ppermute | solution.py:899
  132.7 16.1 %collective-permute-start.25 = (bf16[512,512]{1,0:T(8,128)(2,1)S(1)}, bf16[512,512]{1,0:T(8,128)(2,1)S(1)}, u32[]{:S(2)}, u32[]{:S(2)}) collective-permute-start(bf16[512,512]{1,0:T(8,128)(2,1)S(1)} %add_convert_fusion.2), channel_id=1, source_target_pairs={{8,0},{10,2},{12,4},{14,6},{16,24},{18,26},{20,28},{22,30},{9,1},{... | collective-permute-start | bytes 1572872 | tf_op jit(solution)/shard_map/ppermute | solution.py:906
  136.0 17.7 %collective-permute-start.29 = (bf16[544,640]{1,0:T(8,128)(2,1)S(1)}, bf16[544,640]{1,0:T(8,128)(2,1)S(1)}, u32[]{:S(2)}, u32[]{:S(2)}) collective-permute-start(bf16[544,640]{1,0:T(8,128)(2,1)S(1)} %add_convert_fusion.1), channel_id=1, source_target_pairs={{8,16},{10,18},{12,20},{14,22},{16,8},{18,10},{20,12},{22,14},{9,1... | collective-permute-start | bytes 2088968 | tf_op jit(solution)/shard_map/ppermute | solution.py:906
  153.8 17.9 %collective-permute-start.34 = (bf16[544,640]{1,0:T(8,128)(2,1)S(1)}, bf16[544,640]{1,0:T(8,128)(2,1)S(1)}, u32[]{:S(2)}, u32[]{:S(2)}) collective-permute-start(bf16[544,640]{1,0:T(8,128)(2,1)S(1)} %add_convert_fusion), channel_id=1, source_target_pairs={{8,0},{10,2},{12,4},{14,6},{16,24},{18,26},{20,28},{22,30},{9,1},{... | collective-permute-start | bytes 2088968 | tf_op jit(solution)/shard_map/ppermute | solution.py:906
  161.9 16.6 %collective-permute-start.36 = (bf16[512,512]{1,0:T(8,128)(2,1)S(1)}, bf16[512,512]{1,0:T(8,128)(2,1)S(1)}, u32[]{:S(2)}, u32[]{:S(2)}) collective-permute-start(bf16[512,512]{1,0:T(8,128)(2,1)S(1)} %broadcast_select_fusion.4.refs_0_), channel_id=1, source_target_pairs={{0,2},{2,0},{4,6},{6,4},{8,10},{10,8},{12,14},{14,12},{16,18},{18,... | collective-permute-start | bytes 1572872 | tf_op jit(solution)/shard_map/ppermute | solution.py:899
  163.2 15.3 %collective-permute-start.37 = (bf16[512,512]{1,0:T(8,128)(2,1)S(1)}, bf16[512,512]{1,0:T(8,128)(2,1)S(1)}, u32[]{:S(2)}, u32[]{:S(2)}) collective-permute-start(bf16[512,512]{1,0:T(8,128)(2,1)S(1)} %collective-permute-done.35.refs_1_), channel_id=1, source_target_pairs={{0,2},{2,0},{4,6},{6,4},{8,10},{10,8},{12,14},{14,12},{16,18},{18,... | collective-permute-start | bytes 1572872 | tf_op jit(solution)/shard_map/ppermute | solution.py:899
  171.8 18.8 %collective-permute-start.43 = (bf16[544,640]{1,0:T(8,128)(2,1)S(1)}, bf16[544,640]{1,0:T(8,128)(2,1)S(1)}, u32[]{:S(2)}, u32[]{:S(2)}) collective-permute-start(bf16[544,640]{1,0:T(8,128)(2,1)S(1)} %broadcast_select_fusion.refs_0_), channel_id=1, source_target_pairs={{0,4},{2,6},{4,0},{6,2},{8,12},{10,14},{12,8},{14,10},{16,20},{18,... | collective-permute-start | bytes 2088968 | tf_op jit(solution)/shard_map/ppermute | solution.py:899
  178.5 15.6 %collective-permute-start.42 = (bf16[128,2048]{1,0:T(8,128)(2,1)S(1)}, bf16[128,2048]{1,0:T(8,128)(2,1)S(1)}, u32[]{:S(2)}, u32[]{:S(2)}) collective-permute-start(bf16[128,2048]{1,0:T(8,128)(2,1)S(1)} %get-tuple-element.161), channel_id=1, source_target_pairs={{0,1},{1,0},{2,3},{3,2},{4,5},{5,4},{6,7},{7,6},{8,9},{9,8},{10,11... | collective-permute-start | bytes 1572872 | tf_op jit(solution)/shard_map/ppermute | solution.py:902
  184.5 15.0 %collective-permute-start.46 = (bf16[544,384]{1,0:T(8,128)(2,1)S(1)}, bf16[544,384]{1,0:T(8,128)(2,1)S(1)}, u32[]{:S(2)}, u32[]{:S(2)}) collective-permute-start(bf16[544,384]{1,0:T(8,128)(2,1)S(1)} %broadcast_select_fusion.5.refs_4_), channel_id=1, source_target_pairs={{0,4},{2,6},{4,0},{6,2},{8,12},{10,14},{12,8},{14,10},{16,20},{18,... | collective-permute-start | bytes 1253384 | tf_op jit(solution)/shard_map/ppermute | solution.py:899
  185.7 15.8 %collective-permute-start.44 = (bf16[544,640]{1,0:T(8,128)(2,1)S(1)}, bf16[544,640]{1,0:T(8,128)(2,1)S(1)}, u32[]{:S(2)}, u32[]{:S(2)}) collective-permute-start(bf16[544,640]{1,0:T(8,128)(2,1)S(1)} %broadcast_select_fusion.refs_0_), channel_id=1, source_target_pairs={{0,2},{2,0},{4,6},{6,4},{8,10},{10,8},{12,14},{14,12},{16,18},{18,... | collective-permute-start | bytes 2088968 | tf_op jit(solution)/shard_map/ppermute | solution.py:899
  (39 other events, 376.9 us)

commit v3 on v2

--- a/solution.py
+++ b/solution.py
@@ -364,7 +364,9 @@
         in_specs=[spec for _, spec in ins],
         out_specs=[spec for _, spec in outs],
         scratch_shapes=list(scratch),
-        compiler_params=pltpu.CompilerParams(vmem_limit_bytes=LIMIT if name in ("pack", "hidden") else LIMIT // 3),
+        compiler_params=pltpu.CompilerParams(
+            vmem_limit_bytes=LIMIT if name in ("pack", "hidden") else LIMIT // 3
+        ),
         cost_estimate=COST if name == "hidden" else SMALL,
         name=name,
     )(*[array for array, _ in ins])
@@ -885,10 +887,10 @@
 
 
 ORDER = (
-    "far", "moa", "mob", "coa", "mia", "fold", "poa", "mib", "xoa", "cob",
-    "tjb", "cia", "pob", "xob", "keep", "soa", "cib", "mja", "pia", "xia",
-    "mjb", "pib", "loa", "sob", "sia", "cja", "xib", "lob", "cjb", "pja",
-    "sib", "xja", "lia", "pjb", "lib", "sja", "xjb", "end", "sjb", "lja",
+    "far", "moa", "mob", "coa", "mia", "fold", "poa", "mib", "cob", "tjb",
+    "cia", "pob", "xoa", "xob", "keep", "soa", "cib", "mja", "pia", "xia",
+    "pib", "loa", "sob", "cja", "sia", "mjb", "xib", "sib", "lob", "cjb",
+    "pja", "xja", "lia", "pjb", "sja", "lib", "xjb", "end", "sjb", "lja",
 )
 
 
@@ -1028,8 +1030,7 @@
         got = line_permute(out_all, [(0, 1), (3, 2)])
         got = after(got, in_other)
         half = part_f // 2
-        state = {"oa": (out_all[:half], got[:half]), "ob": (out_all[half:], got[half:])}
-        state |= {"ia": in_mine, "ib": in_other, "ja": joint_a}
+        state = {"oa": slice(0, half), "ob": slice(half, part_f), "ia": in_mine, "ib": in_other, "ja": joint_a}
         state["jb"] = swap_shard(joint_theirs)
         for token in ORDER:
             what, name = token[0], token[1:]
@@ -1037,7 +1038,8 @@
             if what == "t":
                 state[name] = then(held)
             elif what == "m":
-                state[name] = added(then(held[0]), held[1]) if name[0] == "o" else meet(held)
+                whole = name[0] == "o"
+                state[name] = added(then(out_all)[held], got[held]) if whole else meet(held)
             elif what == "c":
                 state[name] = cross(held)
             elif what == "p":

time: 211 us -> 210 us (level)
  waiting for transfers between devices: 62.6 us -> 58 us
  starting transfers between devices: 77.8 us -> 81.1 us
    ppermute x26, waiting for transfers between devices: 27.4 us -> 17.4 us  [swap_rep(): return lax.ppermute(values, 'rep', [(i, i ^ bit) for i in range(reps)])]
    ppermute x17, waiting for transfers between devices: 26.7 us -> 32.2 us  [line_permute(): return lax.ppermute(values, 'rep', pairs)]
    ppermute x26, starting transfers between devices: 36.1 us -> 40.6 us  [swap_rep(): return lax.ppermute(values, 'rep', [(i, i ^ bit) for i in range(reps)])]
  transfers between devices with their start and end apart: 49 -> 49, of which waited for: 18 -> 17; matrix products, arithmetic and copies ran while one was open for 4% -> 3% of each run, Pallas kernels for 24% -> 24%
where the time goes in v3:
time: 210 us; the launch traced here: 206 us
  starting transfers between devices  81.1 us (39%)
  waiting for transfers between devices  58 us (28%)
  Pallas kernels  55.5 us (26%)
  other arithmetic  6.88 us (3%)
  local copies, waits for them, and re-layouts  2.57 us (1%)
    ppermute x26, starting transfers between devices, swap_rep(): return lax.ppermute(values, 'rep', [(i, i ^ bit) for i in range(reps)])  40.6 us
    ppermute x17, starting transfers between devices, line_permute(): return lax.ppermute(values, 'rep', pairs)  33.8 us
    ppermute x17, waiting for transfers between devices, line_permute(): return lax.ppermute(values, 'rep', pairs)  32.2 us
    pallas_call x6, Pallas kernels, call(): pl.pallas_call(kernel, out_shape=[shape for shape, _ in outs], in_specs=[...  23 us
    pallas_call x1, Pallas kernels, attention(): pl.pallas_call(attention_kernel, grid=(steps,), out_shape=[half, half, sh...  20 us
    ppermute x26, waiting for transfers between devices, swap_rep(): return lax.ppermute(values, 'rep', [(i, i ^ bit) for i in range(reps)])  17.4 us
    pallas_call x4, Pallas kernels, placed(): pl.pallas_call(kernel, in_specs=[pl.BlockSpec(memory_space=pl.ANY)] * len...  9.16 us
    ppermute x6, waiting for transfers between devices, swap_shard(): return lax.ppermute(values, 'shard', [(0, 1), (1, 0)])  8.46 us
  transfers between devices with their start and end apart: 49, of which 17 were waited for; matrix products, arithmetic and copies ran while one was open for 3% of the time, Pallas kernels for 24%

profile of v3, /device:TPU:9, one launch (start us, length us, event | category | flops | bytes accessed | tf_op | source)
XLA Modules:
  0.0 206.1 jit_solution(18287526714872780956)
XLA Ops:
  1.3 2.6 %pack.1 = (bf16[272,1024]{1,0:T(8,128)(2,1)}, f32[1,1024]{1,0:T(1,128)}, f32[1,512]{1,0:T(1,128)}, bf16[512,512]{1,0:T(8,128)(2,1)}, bf16[512,384]{1,0:T(8,128)(2,1)}) custom-call(s32[1]{0:T(128)S(6)} %copy.38.length, bf16[128,1024]{1,0:T(8,128)(2,1)} %tok.3, bf16[128,1024]{1,0:T(8,128)(2,1)} %cot.3, bf16[2048]{0:T(1024)(128)(2,1)} %in_bias.1, ...), custom_call_target="tpu_custom_call" | custom-call | flops 1000000 | tf_op jit(solution)/shard_map/pack/pallas_call | solution.py:361
  6.5 11.3 %collective-permute-done.1.refs_2_ = bf16[272,1024]{1,0:T(8,128)(2,1)S(1)} collective-permute-done((bf16[272,1024]{1,0:T(8,128)(2,1)}, bf16[272,1024]{1,0:T(8,128)(2,1)S(1)}, u32[]{:S(2)}, u32[]{:S(2)}) %collective-permute-start.1) | collective-permute-done | bytes 557088 | tf_op jit(solution)/shard_map/ppermute | solution.py:901
  23.0 7.6 %collective-permute-done.3.refs_9_.in_got = bf16[512,512]{1,0:T(8,128)(2,1)S(1)} collective-permute-done((bf16[512,512]{1,0:T(8,128)(2,1)}, bf16[512,512]{1,0:T(8,128)(2,1)S(1)}, u32[]{:S(2)}, u32[]{:S(2)}) %collective-permute-start.3) | collective-permute-done | bytes 524320 | tf_op jit(solution)/shard_map/ppermute | solution.py:904
  31.4 2.9 %collective-permute-start.7 = (bf16[272,1024]{1,0:T(8,128)(2,1)S(1)}, bf16[272,1024]{1,0:T(8,128)(2,1)S(1)}, u32[]{:S(2)}, u32[]{:S(2)}) collective-permute-start(bf16[272,1024]{1,0:T(8,128)(2,1)S(1)} %collective-permute-done.2.refs_3_), channel_id=1, source_target_pairs={{0,2},{2,0},{4,6},{6,4},{8,10},{10,8},{12,14},{14,12},{16,18},{18,... | collective-permute-start | bytes 1671176 | tf_op jit(solution)/shard_map/ppermute | solution.py:901
  37.7 12.3 %hidden.1 = (bf16[1024,1024]{1,0:T(8,128)(2,1)}, bf16[1024,1024]{1,0:T(8,128)(2,1)}, bf16[1024,512]{1,0:T(8,128)(2,1)}, bf16[1024,512]{1,0:T(8,128)(2,1)}, bf16[...) custom-call(bf16[272,1024]{1,0:T(8,128)(2,1)} %get-tuple-element.97., ...), custom_call_target="tpu_custom_call" | custom-call | flops 999999995904 | bytes 1000000000 | tf_op jit(solution)/shard_map/hidden/pallas_call | solution.py:361
  51.6 20.0 %attention.1 = (bf16[512,2048]{1,0:T(8,128)(2,1)}, bf16[512,2048]{1,0:T(8,128)(2,1)}, bf16[544,640]{1,0:T(8,128)(2,1)}, bf16[544,384]{1,0:T(8,128)(2,1)}) custom-call(bf16[1024,1024]{1,0:T(8,128)(2,1)} %get-tuple-element.104.normed, bf16[1024,1024]{1,0:T(8,128)(2,1)} %get-tuple-element.105.branch, bf16[1024,512]{1,0:T(8,128)(2,1)} %get-tuple-element.106.active, ...), custom_call_target="tpu_custom_call" | custom-call | flops 999999995904 | bytes 1000000000 | tf_op jit(solution)/shard_map/attention/pallas_call | solution.py:687
  72.3 4.2 %collective-permute-done.10 = bf16[512,1024]{1,0:T(8,128)(2,1)} collective-permute-done((bf16[512,1024]{1,0:T(8,128)(2,1)}, bf16[512,1024]{1,0:T(8,128)(2,1)}, u32[]{:S(2)}, u32[]{:S(2)}) %collective-permute-start.10) | collective-permute-done | bytes 1048608 | tf_op jit(solution)/shard_map/ppermute | solution.py:908
  77.9 3.2 %collective-permute-start.11 = (bf16[256,1024]{1,0:T(8,128)(2,1)S(1)}, bf16[256,1024]{1,0:T(8,128)(2,1)S(1)}, u32[]{:S(2)}, u32[]{:S(2)}) collective-permute-start(bf16[256,1024]{1,0:T(8,128)(2,1)S(1)} %add_convert_fusion.9), channel_id=1, source_target_pairs={{8,16},{10,18},{12,20},{14,22},{16,8},{18,10},{20,12},{22,14},{9,1... | collective-permute-start | bytes 1572872 | tf_op jit(solution)/shard_map/ppermute | solution.py:908
  84.0 7.8 %collective-permute-done.11 = bf16[256,1024]{1,0:T(8,128)(2,1)S(1)} collective-permute-done((bf16[256,1024]{1,0:T(8,128)(2,1)S(1)}, bf16[256,1024]{1,0:T(8,128)(2,1)S(1)}, u32[]{:S(2)}, u32[]{:S(2)}) %collective-permute-start.11) | collective-permute-done | bytes 524320 | tf_op jit(solution)/shard_map/ppermute | solution.py:908
  95.4 3.2 %collective-permute-start.16 = (bf16[256,1024]{1,0:T(8,128)(2,1)S(1)}, bf16[256,1024]{1,0:T(8,128)(2,1)S(1)}, u32[]{:S(2)}, u32[]{:S(2)}) collective-permute-start(bf16[256,1024]{1,0:T(8,128)(2,1)S(1)} %add_convert_fusion.8), channel_id=1, source_target_pairs={{8,16},{10,18},{12,20},{14,22},{16,8},{18,10},{20,12},{22,14},{9,1... | collective-permute-start | bytes 1572872 | tf_op jit(solution)/shard_map/ppermute | solution.py:908
  112.7 6.9 %collective-permute-done.17 = bf16[512,512]{1,0:T(8,128)(2,1)S(1)} collective-permute-done((bf16[512,512]{1,0:T(8,128)(2,1)S(1)}, bf16[512,512]{1,0:T(8,128)(2,1)S(1)}, u32[]{:S(2)}, u32[]{:S(2)}) %collective-permute-start.17) | collective-permute-done | bytes 524320 | tf_op jit(solution)/shard_map/ppermute | solution.py:908
  119.6 3.2 %collective-permute-start.20 = (bf16[512,512]{1,0:T(8,128)(2,1)S(1)}, bf16[512,512]{1,0:T(8,128)(2,1)S(1)}, u32[]{:S(2)}, u32[]{:S(2)}) collective-permute-start(bf16[512,512]{1,0:T(8,128)(2,1)S(1)} %add_convert_fusion.5), channel_id=1, source_target_pairs={{8,16},{10,18},{12,20},{14,22},{16,8},{18,10},{20,12},{22,14},{9,1... | collective-permute-start | bytes 1572872 | tf_op jit(solution)/shard_map/ppermute | solution.py:908
  128.6 3.0 %collective-permute-done.20 = bf16[512,512]{1,0:T(8,128)(2,1)S(1)} collective-permute-done((bf16[512,512]{1,0:T(8,128)(2,1)S(1)}, bf16[512,512]{1,0:T(8,128)(2,1)S(1)}, u32[]{:S(2)}, u32[]{:S(2)}) %collective-permute-start.20) | collective-permute-done | bytes 524320 | tf_op jit(solution)/shard_map/ppermute | solution.py:908
  133.2 3.2 %collective-permute-start.28 = (bf16[544,640]{1,0:T(8,128)(2,1)S(1)}, bf16[544,640]{1,0:T(8,128)(2,1)S(1)}, u32[]{:S(2)}, u32[]{:S(2)}) collective-permute-start(bf16[544,640]{1,0:T(8,128)(2,1)S(1)} %add_convert_fusion.1), channel_id=1, source_target_pairs={{8,16},{10,18},{12,20},{14,22},{16,8},{18,10},{20,12},{22,14},{9,1... | collective-permute-start | bytes 2088968 | tf_op jit(solution)/shard_map/ppermute | solution.py:908
  137.7 4.7 %collective-permute-start.26 = (bf16[256,1024]{1,0:T(8,128)(2,1)S(1)}, bf16[256,1024]{1,0:T(8,128)(2,1)S(1)}, u32[]{:S(2)}, u32[]{:S(2)}) collective-permute-start(bf16[256,1024]{1,0:T(8,128)(2,1)S(1)} %broadcast_select_fusion.2.refs_0_), channel_id=1, source_target_pairs={{0,2},{2,0},{4,6},{6,4},{8,10},{10,8},{12,14},{14,12},{16,18},{18,... | collective-permute-start | bytes 1572872 | tf_op jit(solution)/shard_map/ppermute | solution.py:901
  149.6 5.0 %collective-permute-start.31 = (bf16[256,1024]{1,0:T(8,128)(2,1)S(1)}, bf16[256,1024]{1,0:T(8,128)(2,1)S(1)}, u32[]{:S(2)}, u32[]{:S(2)}) collective-permute-start(bf16[256,1024]{1,0:T(8,128)(2,1)S(1)} %broadcast_select_fusion.1.refs_0_), channel_id=1, source_target_pairs={{0,2},{2,0},{4,6},{6,4},{8,10},{10,8},{12,14},{14,12},{16,18},{18,... | collective-permute-start | bytes 1572872 | tf_op jit(solution)/shard_map/ppermute | solution.py:901
  154.8 2.6 %collective-permute-start.34 = (bf16[544,640]{1,0:T(8,128)(2,1)S(1)}, bf16[544,640]{1,0:T(8,128)(2,1)S(1)}, u32[]{:S(2)}, u32[]{:S(2)}) collective-permute-start(bf16[544,640]{1,0:T(8,128)(2,1)S(1)} %add_convert_fusion), channel_id=1, source_target_pairs={{8,0},{10,2},{12,4},{14,6},{16,24},{18,26},{20,28},{22,30},{9,1},{... | collective-permute-start | bytes 2088968 | tf_op jit(solution)/shard_map/ppermute | solution.py:908
  161.3 3.3 %collective-permute-start.36 = (bf16[512,512]{1,0:T(8,128)(2,1)S(1)}, bf16[512,512]{1,0:T(8,128)(2,1)S(1)}, u32[]{:S(2)}, u32[]{:S(2)}) collective-permute-start(bf16[512,512]{1,0:T(8,128)(2,1)S(1)} %broadcast_select_fusion.4.refs_0_), channel_id=1, source_target_pairs={{0,2},{2,0},{4,6},{6,4},{8,10},{10,8},{12,14},{14,12},{16,18},{18,... | collective-permute-start | bytes 1572872 | tf_op jit(solution)/shard_map/ppermute | solution.py:901
  172.4 2.4 %collective-permute-start.40 = (bf16[512,512]{1,0:T(8,128)(2,1)S(1)}, bf16[512,512]{1,0:T(8,128)(2,1)S(1)}, u32[]{:S(2)}, u32[]{:S(2)}) collective-permute-start(bf16[512,512]{1,0:T(8,128)(2,1)S(1)} %broadcast_select_fusion.3.refs_0_), channel_id=1, source_target_pairs={{0,2},{2,0},{4,6},{6,4},{8,10},{10,8},{12,14},{14,12},{16,18},{18,... | collective-permute-start | bytes 1572872 | tf_op jit(solution)/shard_map/ppermute | solution.py:901
  178.4 2.4 %collective-permute-done.38 = bf16[544,384]{1,0:T(8,128)(2,1)S(1)} collective-permute-done((bf16[544,384]{1,0:T(8,128)(2,1)S(1)}, bf16[544,384]{1,0:T(8,128)(2,1)S(1)}, u32[]{:S(2)}, u32[]{:S(2)}) %collective-permute-start.38) | collective-permute-done | bytes 417824 | tf_op jit(solution)/shard_map/ppermute | solution.py:908
  187.0 5.7 %collective-permute-start.45 = (bf16[544,640]{1,0:T(8,128)(2,1)S(1)}, bf16[544,640]{1,0:T(8,128)(2,1)S(1)}, u32[]{:S(2)}, u32[]{:S(2)}) collective-permute-start(bf16[544,640]{1,0:T(8,128)(2,1)S(1)} %collective-permute-done.43.refs_1_), channel_id=1, source_target_pairs={{0,2},{2,0},{4,6},{6,4},{8,10},{10,8},{12,14},{14,12},{16,18},{18,... | collective-permute-start | bytes 2088968 | tf_op jit(solution)/shard_map/ppermute | solution.py:901
  196.0 3.1 %collective-permute-start.48 = (bf16[544,384]{1,0:T(8,128)(2,1)S(1)}, bf16[544,384]{1,0:T(8,128)(2,1)S(1)}, u32[]{:S(2)}, u32[]{:S(2)}) collective-permute-start(bf16[544,384]{1,0:T(8,128)(2,1)S(1)} %collective-permute-done.46.refs_5_), channel_id=1, source_target_pairs={{0,2},{2,0},{4,6},{6,4},{8,10},{10,8},{12,14},{14,12},{16,18},{18,... | collective-permute-start | bytes 1253384 | tf_op jit(solution)/shard_map/ppermute | solution.py:901
  199.1 3.5 %place_joint.1 = (f32[512,3072]{1,0:T(8,128)}, f32[512,1024]{1,0:T(8,128)}) custom-call(bf16[544,640]{1,0:T(8,128)(2,1)S(1)} %broadcast_select_fusion.refs_0_, bf16[544,640]{1,0:T(8,128)(2,1)S(1)} %collective-permute-done.43.refs_1_, bf16[544,640]{1,0:T(8,128)(2,1)S(1)} %collective-permute-done.44.refs_2_, bf16[544,640]{1,0:T(8,128)(2,1)S(1)} %collective-permute-done.45.refs_3_), custom_call_target="tpu_custom_call" | custom-call | flops 1000000 | tf_op jit(solution)/shard_map/place_joint/pallas_call | solution.py:361
  202.6 3.4 %place_other.1 = (f32[512,3072]{1,0:T(8,128)}, f32[1536]{0:T(1024)}, f32[2048]{0:T(1024)}, f32[512]{0:T(512)}, f32[512]{0:T(512)}, /*index=5*/f32[512]{0:T(512)}, f32[512]{0:T(512)}, f32[512]{0:T(512)}, f32[512]{0:T(512)}) custom-call(bf16[544,640]{1,0:T(8,128)(2,1)S(1)} %broadcast_select_fusion.refs_0_, ...), custom_call_target="tpu_custom_call", output_to_operand_aliasing={{0}: (8, {})} | custom-call | flops 1000000 | tf_op jit(solution)/shard_map/place_other/pallas_call | solution.py:1087
  (132 shorter events, 76.5 us)
Async XLA Ops:
  4.0 13.8 %collective-permute-start.1 = (bf16[272,1024]{1,0:T(8,128)(2,1)}, bf16[272,1024]{1,0:T(8,128)(2,1)S(1)}, u32[]{:S(2)}, u32[]{:S(2)}) collective-permute-start(bf16[272,1024]{1,0:T(8,128)(2,1)} %get-tuple-element.97.refs_0_), channel_id=1, source_target_pairs={{0,4},{2,6},{4,0},{6,2},{8,12},{10,14},{12,8},{14,10},{16,20},{18,... | collective-permute-start | bytes 1671176 | tf_op jit(solution)/shard_map/ppermute | solution.py:901
  5.2 13.4 %collective-permute-start = (bf16[272,1024]{1,0:T(8,128)(2,1)}, bf16[272,1024]{1,0:T(8,128)(2,1)S(1)}, u32[]{:S(2)}, u32[]{:S(2)}) collective-permute-start(bf16[272,1024]{1,0:T(8,128)(2,1)} %get-tuple-element.97.refs_0_), channel_id=1, source_target_pairs={{0,1},{1,0},{2,3},{3,2},{4,5},{5,4},{6,7},{7,6},{8,9},{9,8},{10,11... | collective-permute-start | bytes 1671176 | tf_op jit(solution)/shard_map/ppermute | solution.py:904
  20.2 15.4 %collective-permute-start.4 = (bf16[272,1024]{1,0:T(8,128)(2,1)}, bf16[272,1024]{1,0:T(8,128)(2,1)S(1)}, u32[]{:S(2)}, u32[]{:S(2)}) collective-permute-start(bf16[272,1024]{1,0:T(8,128)(2,1)} %get-tuple-element.97.refs_0_), channel_id=1, source_target_pairs={{0,2},{2,0},{4,6},{6,4},{8,10},{10,8},{12,14},{14,12},{16,18},{18,... | collective-permute-start | bytes 1671176 | tf_op jit(solution)/shard_map/ppermute | solution.py:901
  34.4 17.2 %collective-permute-start.9 = (bf16[512,384]{1,0:T(8,128)(2,1)}, bf16[512,384]{1,0:T(8,128)(2,1)}, u32[]{:S(2)}, u32[]{:S(2)}) collective-permute-start(bf16[512,384]{1,0:T(8,128)(2,1)} %get-tuple-element.110), channel_id=1, source_target_pairs={{0,1},{1,0},{2,3},{3,2},{4,5},{5,4},{6,7},{7,6},{8,9},{9,8},{10,11... | collective-permute-start | bytes 1179656 | tf_op jit(solution)/shard_map/ppermute | solution.py:904
  49.9 22.4 %collective-permute-start.8 = (bf16[512,512]{1,0:T(8,128)(2,1)}, bf16[512,512]{1,0:T(8,128)(2,1)}, u32[]{:S(2)}, u32[]{:S(2)}) collective-permute-start(bf16[512,512]{1,0:T(8,128)(2,1)} %get-tuple-element.102), channel_id=1, source_target_pairs={{0,1},{1,0},{2,3},{3,2},{4,5},{5,4},{6,7},{7,6},{8,9},{9,8},{10,11... | collective-permute-start | bytes 1572872 | tf_op jit(solution)/shard_map/ppermute | solution.py:904
  50.3 26.2 %collective-permute-start.10 = (bf16[512,1024]{1,0:T(8,128)(2,1)}, bf16[512,1024]{1,0:T(8,128)(2,1)}, u32[]{:S(2)}, u32[]{:S(2)}) collective-permute-start(bf16[512,1024]{1,0:T(8,128)(2,1)} %get-tuple-element.117), channel_id=1, source_target_pairs={{0,8},{2,10},{4,12},{6,14},{24,16},{26,18},{28,20},{30,22},{1,9},{... | collective-permute-start | bytes 3145736 | tf_op jit(solution)/shard_map/ppermute | solution.py:908
  71.6 30.6 %collective-permute-start.13 = (bf16[512,2048]{1,0:T(8,128)(2,1)}, bf16[512,2048]{1,0:T(8,128)(2,1)}, u32[]{:S(2)}, u32[]{:S(2)}) collective-permute-start(bf16[512,2048]{1,0:T(8,128)(2,1)} %get-tuple-element.124), channel_id=1, source_target_pairs={{0,2},{2,0},{4,6},{6,4},{8,10},{10,8},{12,14},{14,12},{16,18},{18,... | collective-permute-start | bytes 6291464 | tf_op jit(solution)/shard_map/ppermute | solution.py:901
  77.9 13.9 %collective-permute-start.11 = (bf16[256,1024]{1,0:T(8,128)(2,1)S(1)}, bf16[256,1024]{1,0:T(8,128)(2,1)S(1)}, u32[]{:S(2)}, u32[]{:S(2)}) collective-permute-start(bf16[256,1024]{1,0:T(8,128)(2,1)S(1)} %add_convert_fusion.9), channel_id=1, source_target_pairs={{8,16},{10,18},{12,20},{14,22},{16,8},{18,10},{20,12},{22,14},{9,1... | collective-permute-start | bytes 1572872 | tf_op jit(solution)/shard_map/ppermute | solution.py:908
  81.2 17.5 %collective-permute-start.12 = (bf16[512,512]{1,0:T(8,128)(2,1)}, bf16[512,512]{1,0:T(8,128)(2,1)}, u32[]{:S(2)}, u32[]{:S(2)}) collective-permute-start(bf16[512,512]{1,0:T(8,128)(2,1)} %get-tuple-element.121), channel_id=1, source_target_pairs={{0,8},{2,10},{4,12},{6,14},{24,16},{26,18},{28,20},{30,22},{1,9},{... | collective-permute-start | bytes 1572872 | tf_op jit(solution)/shard_map/ppermute | solution.py:908
  94.1 13.2 %collective-permute-start.15 = (bf16[512,512]{1,0:T(8,128)(2,1)}, bf16[512,512]{1,0:T(8,128)(2,1)S(1)}, u32[]{:S(2)}, u32[]{:S(2)}) collective-permute-start(bf16[512,512]{1,0:T(8,128)(2,1)} %collective-permute-done.8), channel_id=1, source_target_pairs={{0,8},{2,10},{4,12},{6,14},{24,16},{26,18},{28,20},{30,22},{1,9},{... | collective-permute-start | bytes 1572872 | tf_op jit(solution)/shard_map/ppermute | solution.py:908
  100.0 19.6 %collective-permute-start.17 = (bf16[512,512]{1,0:T(8,128)(2,1)S(1)}, bf16[512,512]{1,0:T(8,128)(2,1)S(1)}, u32[]{:S(2)}, u32[]{:S(2)}) collective-permute-start(bf16[512,512]{1,0:T(8,128)(2,1)S(1)} %add_convert_fusion.6), channel_id=1, source_target_pairs={{8,16},{10,18},{12,20},{14,22},{16,8},{18,10},{20,12},{22,14},{9,1... | collective-permute-start | bytes 1572872 | tf_op jit(solution)/shard_map/ppermute | solution.py:908
  103.9 21.8 %collective-permute-start.19 = (bf16[256,2048]{1,0:T(8,128)(2,1)S(1)}, bf16[256,2048]{1,0:T(8,128)(2,1)S(1)}, u32[]{:S(2)}, u32[]{:S(2)}) collective-permute-start(bf16[256,2048]{1,0:T(8,128)(2,1)S(1)} %fold.1), channel_id=1, source_target_pairs={{0,4},{2,6},{4,0},{6,2},{8,12},{10,14},{12,8},{14,10},{16,20},{18,... | collective-permute-start | bytes 3145736 | tf_op jit(solution)/shard_map/ppermute | solution.py:901
  108.6 14.3 %collective-permute-start.18 = (bf16[256,1024]{1,0:T(8,128)(2,1)S(1)}, bf16[256,1024]{1,0:T(8,128)(2,1)S(1)}, u32[]{:S(2)}, u32[]{:S(2)}) collective-permute-start(bf16[256,1024]{1,0:T(8,128)(2,1)S(1)} %add_convert_fusion.4), channel_id=1, source_target_pairs={{8,0},{10,2},{12,4},{14,6},{16,24},{18,26},{20,28},{22,30},{9,1},{... | collective-permute-start | bytes 1572872 | tf_op jit(solution)/shard_map/ppermute | solution.py:908
  110.0 23.1 %collective-permute-start.21 = (bf16[544,640]{1,0:T(8,128)(2,1)S(1)}, bf16[544,640]{1,0:T(8,128)(2,1)S(1)}, u32[]{:S(2)}, u32[]{:S(2)}) collective-permute-start(bf16[544,640]{1,0:T(8,128)(2,1)S(1)} %copy-done.4), channel_id=1, source_target_pairs={{0,8},{2,10},{4,12},{6,14},{24,16},{26,18},{28,20},{30,22},{1,9},{... | collective-permute-start | bytes 2088968 | tf_op jit(solution)/shard_map/ppermute | solution.py:908
  111.3 25.2 %collective-permute-start.24 = (bf16[544,384]{1,0:T(8,128)(2,1)S(1)}, bf16[544,384]{1,0:T(8,128)(2,1)S(1)}, u32[]{:S(2)}, u32[]{:S(2)}) collective-permute-start(bf16[544,384]{1,0:T(8,128)(2,1)S(1)} %copy-done.13), channel_id=1, source_target_pairs={{0,1},{1,0},{2,3},{3,2},{4,5},{5,4},{6,7},{7,6},{8,9},{9,8},{10,11... | collective-permute-start | bytes 1253384 | tf_op jit(solution)/shard_map/ppermute | solution.py:904
  123.0 19.5 %collective-permute-start.22 = (bf16[512,512]{1,0:T(8,128)(2,1)S(1)}, bf16[512,512]{1,0:T(8,128)(2,1)S(1)}, u32[]{:S(2)}, u32[]{:S(2)}) collective-permute-start(bf16[512,512]{1,0:T(8,128)(2,1)S(1)} %add_convert_fusion.3), channel_id=1, source_target_pairs={{8,0},{10,2},{12,4},{14,6},{16,24},{18,26},{20,28},{22,30},{9,1},{... | collective-permute-start | bytes 1572872 | tf_op jit(solution)/shard_map/ppermute | solution.py:908
  133.2 21.4 %collective-permute-start.28 = (bf16[544,640]{1,0:T(8,128)(2,1)S(1)}, bf16[544,640]{1,0:T(8,128)(2,1)S(1)}, u32[]{:S(2)}, u32[]{:S(2)}) collective-permute-start(bf16[544,640]{1,0:T(8,128)(2,1)S(1)} %add_convert_fusion.1), channel_id=1, source_target_pairs={{8,16},{10,18},{12,20},{14,22},{16,8},{18,10},{20,12},{22,14},{9,1... | collective-permute-start | bytes 2088968 | tf_op jit(solution)/shard_map/ppermute | solution.py:908
  136.5 13.1 %collective-permute-start.30 = (bf16[256,1024]{1,0:T(8,128)(2,1)S(1)}, bf16[256,1024]{1,0:T(8,128)(2,1)S(1)}, u32[]{:S(2)}, u32[]{:S(2)}) collective-permute-start(bf16[256,1024]{1,0:T(8,128)(2,1)S(1)} %broadcast_select_fusion.1.refs_0_), channel_id=1, source_target_pairs={{0,4},{2,6},{4,0},{6,2},{8,12},{10,14},{12,8},{14,10},{16,20},{18,... | collective-permute-start | bytes 1572872 | tf_op jit(solution)/shard_map/ppermute | solution.py:901
  146.2 14.1 %collective-permute-start.35 = (bf16[512,512]{1,0:T(8,128)(2,1)S(1)}, bf16[512,512]{1,0:T(8,128)(2,1)S(1)}, u32[]{:S(2)}, u32[]{:S(2)}) collective-permute-start(bf16[512,512]{1,0:T(8,128)(2,1)S(1)} %broadcast_select_fusion.4.refs_0_), channel_id=1, source_target_pairs={{0,4},{2,6},{4,0},{6,2},{8,12},{10,14},{12,8},{14,10},{16,20},{18,... | collective-permute-start | bytes 1572872 | tf_op jit(solution)/shard_map/ppermute | solution.py:901
  154.8 17.1 %collective-permute-start.34 = (bf16[544,640]{1,0:T(8,128)(2,1)S(1)}, bf16[544,640]{1,0:T(8,128)(2,1)S(1)}, u32[]{:S(2)}, u32[]{:S(2)}) collective-permute-start(bf16[544,640]{1,0:T(8,128)(2,1)S(1)} %add_convert_fusion), channel_id=1, source_target_pairs={{8,0},{10,2},{12,4},{14,6},{16,24},{18,26},{20,28},{22,30},{9,1},{... | collective-permute-start | bytes 2088968 | tf_op jit(solution)/shard_map/ppermute | solution.py:908
  161.3 13.5 %collective-permute-start.36 = (bf16[512,512]{1,0:T(8,128)(2,1)S(1)}, bf16[512,512]{1,0:T(8,128)(2,1)S(1)}, u32[]{:S(2)}, u32[]{:S(2)}) collective-permute-start(bf16[512,512]{1,0:T(8,128)(2,1)S(1)} %broadcast_select_fusion.4.refs_0_), channel_id=1, source_target_pairs={{0,2},{2,0},{4,6},{6,4},{8,10},{10,8},{12,14},{14,12},{16,18},{18,... | collective-permute-start | bytes 1572872 | tf_op jit(solution)/shard_map/ppermute | solution.py:901
  172.0 15.0 %collective-permute-start.43 = (bf16[544,640]{1,0:T(8,128)(2,1)S(1)}, bf16[544,640]{1,0:T(8,128)(2,1)S(1)}, u32[]{:S(2)}, u32[]{:S(2)}) collective-permute-start(bf16[544,640]{1,0:T(8,128)(2,1)S(1)} %broadcast_select_fusion.refs_0_), channel_id=1, source_target_pairs={{0,4},{2,6},{4,0},{6,2},{8,12},{10,14},{12,8},{14,10},{16,20},{18,... | collective-permute-start | bytes 2088968 | tf_op jit(solution)/shard_map/ppermute | solution.py:901
  174.9 17.8 %collective-permute-start.42 = (bf16[128,2048]{1,0:T(8,128)(2,1)S(1)}, bf16[128,2048]{1,0:T(8,128)(2,1)S(1)}, u32[]{:S(2)}, u32[]{:S(2)}) collective-permute-start(bf16[128,2048]{1,0:T(8,128)(2,1)S(1)} %get-tuple-element.159), channel_id=1, source_target_pairs={{0,1},{1,0},{2,3},{3,2},{4,5},{5,4},{6,7},{7,6},{8,9},{9,8},{10,11... | collective-permute-start | bytes 1572872 | tf_op jit(solution)/shard_map/ppermute | solution.py:904
  183.7 15.3 %collective-permute-start.44 = (bf16[544,640]{1,0:T(8,128)(2,1)S(1)}, bf16[544,640]{1,0:T(8,128)(2,1)S(1)}, u32[]{:S(2)}, u32[]{:S(2)}) collective-permute-start(bf16[544,640]{1,0:T(8,128)(2,1)S(1)} %broadcast_select_fusion.refs_0_), channel_id=1, source_target_pairs={{0,2},{2,0},{4,6},{6,4},{8,10},{10,8},{12,14},{14,12},{16,18},{18,... | collective-permute-start | bytes 2088968 | tf_op jit(solution)/shard_map/ppermute | solution.py:901
  (39 other events, 382.1 us)

commit v4 on v3

--- a/solution.py
+++ b/solution.py
@@ -890,7 +890,7 @@
     "far", "moa", "mob", "coa", "mia", "fold", "poa", "mib", "cob", "tjb",
     "cia", "pob", "xoa", "xob", "keep", "soa", "cib", "mja", "pia", "xia",
     "pib", "loa", "sob", "cja", "sia", "mjb", "xib", "sib", "lob", "cjb",
-    "pja", "xja", "lia", "pjb", "sja", "lib", "xjb", "end", "sjb", "lja",
+    "pja", "xja", "end", "lia", "pjb", "sja", "lib", "xjb", "sjb", "lja",
 )
 
 

time: 210 us -> 211 us (level); the launches traced: 206 us -> 210 us
  starting transfers between devices: 81.1 us -> 85 us
    ppermute x26, waiting for transfers between devices: 17.4 us -> 20.8 us  [swap_rep(): return lax.ppermute(values, 'rep', [(i, i ^ bit) for i in range(reps)])]
    ppermute x17, waiting for transfers between devices: 32.2 us -> 29 us  [line_permute(): return lax.ppermute(values, 'rep', pairs)]
    ppermute x17, starting transfers between devices: 33.8 us -> 36.6 us  [line_permute(): return lax.ppermute(values, 'rep', pairs)]
where the time goes in v4:
time: 211 us; the launch traced here: 210 us
  starting transfers between devices  85 us (40%)
  waiting for transfers between devices  58.3 us (28%)
  Pallas kernels  55.5 us (26%)
  other arithmetic  6.87 us (3%)
  local copies, waits for them, and re-layouts  2.57 us (1%)
    ppermute x26, starting transfers between devices, swap_rep(): return lax.ppermute(values, 'rep', [(i, i ^ bit) for i in range(reps)])  41.6 us
    ppermute x17, starting transfers between devices, line_permute(): return lax.ppermute(values, 'rep', pairs)  36.6 us
    ppermute x17, waiting for transfers between devices, line_permute(): return lax.ppermute(values, 'rep', pairs)  29 us
    pallas_call x6, Pallas kernels, call(): pl.pallas_call(kernel, out_shape=[shape for shape, _ in outs], in_specs=[...  23 us
    ppermute x26, waiting for transfers between devices, swap_rep(): return lax.ppermute(values, 'rep', [(i, i ^ bit) for i in range(reps)])  20.8 us
    pallas_call x1, Pallas kernels, attention(): pl.pallas_call(attention_kernel, grid=(steps,), out_shape=[half, half, sh...  20 us
    pallas_call x4, Pallas kernels, placed(): pl.pallas_call(kernel, in_specs=[pl.BlockSpec(memory_space=pl.ANY)] * len...  9.16 us
    ppermute x6, waiting for transfers between devices, swap_shard(): return lax.ppermute(values, 'shard', [(0, 1), (1, 0)])  8.46 us
  transfers between devices with their start and end apart: 49, of which 17 were waited for; matrix products, arithmetic and copies ran while one was open for 3% of the time, Pallas kernels for 24%

profile of v4, /device:TPU:9, one launch (start us, length us, event | category | flops | bytes accessed | tf_op | source)
XLA Modules:
  0.0 210.3 jit_solution(13789871106407132171)
XLA Ops:
  1.3 2.6 %pack.1 = (bf16[272,1024]{1,0:T(8,128)(2,1)}, f32[1,1024]{1,0:T(1,128)}, f32[1,512]{1,0:T(1,128)}, bf16[512,512]{1,0:T(8,128)(2,1)}, bf16[512,384]{1,0:T(8,128)(2,1)}) custom-call(s32[1]{0:T(128)S(6)} %copy.38.length, bf16[128,1024]{1,0:T(8,128)(2,1)} %tok.3, bf16[128,1024]{1,0:T(8,128)(2,1)} %cot.3, bf16[2048]{0:T(1024)(128)(2,1)} %in_bias.1, ...), custom_call_target="tpu_custom_call" | custom-call | flops 1000000 | tf_op jit(solution)/shard_map/pack/pallas_call | solution.py:361
  6.5 11.3 %collective-permute-done.1.refs_2_ = bf16[272,1024]{1,0:T(8,128)(2,1)S(1)} collective-permute-done((bf16[272,1024]{1,0:T(8,128)(2,1)}, bf16[272,1024]{1,0:T(8,128)(2,1)S(1)}, u32[]{:S(2)}, u32[]{:S(2)}) %collective-permute-start.1) | collective-permute-done | bytes 557088 | tf_op jit(solution)/shard_map/ppermute | solution.py:901
  23.0 7.6 %collective-permute-done.3.refs_9_.in_got = bf16[512,512]{1,0:T(8,128)(2,1)S(1)} collective-permute-done((bf16[512,512]{1,0:T(8,128)(2,1)}, bf16[512,512]{1,0:T(8,128)(2,1)S(1)}, u32[]{:S(2)}, u32[]{:S(2)}) %collective-permute-start.3) | collective-permute-done | bytes 524320 | tf_op jit(solution)/shard_map/ppermute | solution.py:904
  31.4 2.9 %collective-permute-start.7 = (bf16[272,1024]{1,0:T(8,128)(2,1)S(1)}, bf16[272,1024]{1,0:T(8,128)(2,1)S(1)}, u32[]{:S(2)}, u32[]{:S(2)}) collective-permute-start(bf16[272,1024]{1,0:T(8,128)(2,1)S(1)} %collective-permute-done.2.refs_3_), channel_id=1, source_target_pairs={{0,2},{2,0},{4,6},{6,4},{8,10},{10,8},{12,14},{14,12},{16,18},{18,... | collective-permute-start | bytes 1671176 | tf_op jit(solution)/shard_map/ppermute | solution.py:901
  37.7 12.3 %hidden.1 = (bf16[1024,1024]{1,0:T(8,128)(2,1)}, bf16[1024,1024]{1,0:T(8,128)(2,1)}, bf16[1024,512]{1,0:T(8,128)(2,1)}, bf16[1024,512]{1,0:T(8,128)(2,1)}, bf16[...) custom-call(bf16[272,1024]{1,0:T(8,128)(2,1)} %get-tuple-element.96., ...), custom_call_target="tpu_custom_call" | custom-call | flops 999999995904 | bytes 1000000000 | tf_op jit(solution)/shard_map/hidden/pallas_call | solution.py:361
  51.6 20.0 %attention.1 = (bf16[512,2048]{1,0:T(8,128)(2,1)}, bf16[512,2048]{1,0:T(8,128)(2,1)}, bf16[544,640]{1,0:T(8,128)(2,1)}, bf16[544,384]{1,0:T(8,128)(2,1)}) custom-call(bf16[1024,1024]{1,0:T(8,128)(2,1)} %get-tuple-element.101.normed, bf16[1024,1024]{1,0:T(8,128)(2,1)} %get-tuple-element.102.branch, bf16[1024,512]{1,0:T(8,128)(2,1)} %get-tuple-element.103.active, ...), custom_call_target="tpu_custom_call" | custom-call | flops 999999995904 | bytes 1000000000 | tf_op jit(solution)/shard_map/attention/pallas_call | solution.py:687
  72.3 4.2 %collective-permute-done.10 = bf16[512,1024]{1,0:T(8,128)(2,1)} collective-permute-done((bf16[512,1024]{1,0:T(8,128)(2,1)}, bf16[512,1024]{1,0:T(8,128)(2,1)}, u32[]{:S(2)}, u32[]{:S(2)}) %collective-permute-start.10) | collective-permute-done | bytes 1048608 | tf_op jit(solution)/shard_map/ppermute | solution.py:908
  77.9 3.2 %collective-permute-start.11 = (bf16[256,1024]{1,0:T(8,128)(2,1)S(1)}, bf16[256,1024]{1,0:T(8,128)(2,1)S(1)}, u32[]{:S(2)}, u32[]{:S(2)}) collective-permute-start(bf16[256,1024]{1,0:T(8,128)(2,1)S(1)} %add_convert_fusion.9), channel_id=1, source_target_pairs={{8,16},{10,18},{12,20},{14,22},{16,8},{18,10},{20,12},{22,14},{9,1... | collective-permute-start | bytes 1572872 | tf_op jit(solution)/shard_map/ppermute | solution.py:908
  84.0 7.8 %collective-permute-done.11 = bf16[256,1024]{1,0:T(8,128)(2,1)S(1)} collective-permute-done((bf16[256,1024]{1,0:T(8,128)(2,1)S(1)}, bf16[256,1024]{1,0:T(8,128)(2,1)S(1)}, u32[]{:S(2)}, u32[]{:S(2)}) %collective-permute-start.11) | collective-permute-done | bytes 524320 | tf_op jit(solution)/shard_map/ppermute | solution.py:908
  95.4 3.2 %collective-permute-start.16 = (bf16[256,1024]{1,0:T(8,128)(2,1)S(1)}, bf16[256,1024]{1,0:T(8,128)(2,1)S(1)}, u32[]{:S(2)}, u32[]{:S(2)}) collective-permute-start(bf16[256,1024]{1,0:T(8,128)(2,1)S(1)} %add_convert_fusion.8), channel_id=1, source_target_pairs={{8,16},{10,18},{12,20},{14,22},{16,8},{18,10},{20,12},{22,14},{9,1... | collective-permute-start | bytes 1572872 | tf_op jit(solution)/shard_map/ppermute | solution.py:908
  112.7 6.9 %collective-permute-done.17 = bf16[512,512]{1,0:T(8,128)(2,1)S(1)} collective-permute-done((bf16[512,512]{1,0:T(8,128)(2,1)S(1)}, bf16[512,512]{1,0:T(8,128)(2,1)S(1)}, u32[]{:S(2)}, u32[]{:S(2)}) %collective-permute-start.17) | collective-permute-done | bytes 524320 | tf_op jit(solution)/shard_map/ppermute | solution.py:908
  119.6 3.2 %collective-permute-start.20 = (bf16[512,512]{1,0:T(8,128)(2,1)S(1)}, bf16[512,512]{1,0:T(8,128)(2,1)S(1)}, u32[]{:S(2)}, u32[]{:S(2)}) collective-permute-start(bf16[512,512]{1,0:T(8,128)(2,1)S(1)} %add_convert_fusion.5), channel_id=1, source_target_pairs={{8,16},{10,18},{12,20},{14,22},{16,8},{18,10},{20,12},{22,14},{9,1... | collective-permute-start | bytes 1572872 | tf_op jit(solution)/shard_map/ppermute | solution.py:908
  128.6 3.0 %collective-permute-done.20 = bf16[512,512]{1,0:T(8,128)(2,1)S(1)} collective-permute-done((bf16[512,512]{1,0:T(8,128)(2,1)S(1)}, bf16[512,512]{1,0:T(8,128)(2,1)S(1)}, u32[]{:S(2)}, u32[]{:S(2)}) %collective-permute-start.20) | collective-permute-done | bytes 524320 | tf_op jit(solution)/shard_map/ppermute | solution.py:908
  133.2 3.2 %collective-permute-start.27 = (bf16[544,640]{1,0:T(8,128)(2,1)S(1)}, bf16[544,640]{1,0:T(8,128)(2,1)S(1)}, u32[]{:S(2)}, u32[]{:S(2)}) collective-permute-start(bf16[544,640]{1,0:T(8,128)(2,1)S(1)} %add_convert_fusion.1), channel_id=1, source_target_pairs={{8,16},{10,18},{12,20},{14,22},{16,8},{18,10},{20,12},{22,14},{9,1... | collective-permute-start | bytes 2088968 | tf_op jit(solution)/shard_map/ppermute | solution.py:908
  137.7 4.7 %collective-permute-start.25 = (bf16[256,1024]{1,0:T(8,128)(2,1)S(1)}, bf16[256,1024]{1,0:T(8,128)(2,1)S(1)}, u32[]{:S(2)}, u32[]{:S(2)}) collective-permute-start(bf16[256,1024]{1,0:T(8,128)(2,1)S(1)} %broadcast_select_fusion.4.refs_0_), channel_id=1, source_target_pairs={{0,2},{2,0},{4,6},{6,4},{8,10},{10,8},{12,14},{14,12},{16,18},{18,... | collective-permute-start | bytes 1572872 | tf_op jit(solution)/shard_map/ppermute | solution.py:901
  149.6 5.0 %collective-permute-start.31 = (bf16[256,1024]{1,0:T(8,128)(2,1)S(1)}, bf16[256,1024]{1,0:T(8,128)(2,1)S(1)}, u32[]{:S(2)}, u32[]{:S(2)}) collective-permute-start(bf16[256,1024]{1,0:T(8,128)(2,1)S(1)} %broadcast_select_fusion.3.refs_0_), channel_id=1, source_target_pairs={{0,2},{2,0},{4,6},{6,4},{8,10},{10,8},{12,14},{14,12},{16,18},{18,... | collective-permute-start | bytes 1572872 | tf_op jit(solution)/shard_map/ppermute | solution.py:901
  154.8 2.6 %collective-permute-start.34 = (bf16[544,640]{1,0:T(8,128)(2,1)S(1)}, bf16[544,640]{1,0:T(8,128)(2,1)S(1)}, u32[]{:S(2)}, u32[]{:S(2)}) collective-permute-start(bf16[544,640]{1,0:T(8,128)(2,1)S(1)} %add_convert_fusion), channel_id=1, source_target_pairs={{8,0},{10,2},{12,4},{14,6},{16,24},{18,26},{20,28},{22,30},{9,1},{... | collective-permute-start | bytes 2088968 | tf_op jit(solution)/shard_map/ppermute | solution.py:908
  162.7 3.5 %collective-permute-start.38 = (bf16[512,512]{1,0:T(8,128)(2,1)S(1)}, bf16[512,512]{1,0:T(8,128)(2,1)S(1)}, u32[]{:S(2)}, u32[]{:S(2)}) collective-permute-start(bf16[512,512]{1,0:T(8,128)(2,1)S(1)} %broadcast_select_fusion.2.refs_0_), channel_id=1, source_target_pairs={{0,2},{2,0},{4,6},{6,4},{8,10},{10,8},{12,14},{14,12},{16,18},{18,... | collective-permute-start | bytes 1572872 | tf_op jit(solution)/shard_map/ppermute | solution.py:901
  171.9 4.1 %collective-permute-start.40 = (bf16[544,384]{1,0:T(8,128)(2,1)S(1)}, bf16[544,384]{1,0:T(8,128)(2,1)S(1)}, u32[]{:S(2)}, u32[]{:S(2)}) collective-permute-start(bf16[544,384]{1,0:T(8,128)(2,1)S(1)} %add_convert_fusion.10), channel_id=1, source_target_pairs={{8,0},{10,2},{12,4},{14,6},{16,24},{18,26},{20,28},{22,30},{9,1},{... | collective-permute-start | bytes 1253384 | tf_op jit(solution)/shard_map/ppermute | solution.py:908
  188.9 2.8 %collective-permute-done.36.refs_1_ = bf16[544,640]{1,0:T(8,128)(2,1)S(1)} collective-permute-done((bf16[544,640]{1,0:T(8,128)(2,1)S(1)}, bf16[544,640]{1,0:T(8,128)(2,1)S(1)}, u32[]{:S(2)}, u32[]{:S(2)}) %collective-permute-start.36) | collective-permute-done | bytes 696352 | tf_op jit(solution)/shard_map/ppermute | solution.py:901
  191.8 4.5 %collective-permute-start.42 = (bf16[544,640]{1,0:T(8,128)(2,1)S(1)}, bf16[544,640]{1,0:T(8,128)(2,1)S(1)}, u32[]{:S(2)}, u32[]{:S(2)}) collective-permute-start(bf16[544,640]{1,0:T(8,128)(2,1)S(1)} %collective-permute-done.36.refs_1_), channel_id=1, source_target_pairs={{0,2},{2,0},{4,6},{6,4},{8,10},{10,8},{12,14},{14,12},{16,18},{18,... | collective-permute-start | bytes 2088968 | tf_op jit(solution)/shard_map/ppermute | solution.py:901
  196.3 4.4 %collective-permute-done.46.refs_5_ = bf16[544,384]{1,0:T(8,128)(2,1)S(1)} collective-permute-done((bf16[544,384]{1,0:T(8,128)(2,1)S(1)}, bf16[544,384]{1,0:T(8,128)(2,1)S(1)}, u32[]{:S(2)}, u32[]{:S(2)}) %collective-permute-start.46) | collective-permute-done | bytes 417824 | tf_op jit(solution)/shard_map/ppermute | solution.py:901
  203.2 3.5 %place_joint.1 = (f32[512,3072]{1,0:T(8,128)}, f32[512,1024]{1,0:T(8,128)}) custom-call(bf16[544,640]{1,0:T(8,128)(2,1)S(1)} %broadcast_select_fusion.refs_0_, bf16[544,640]{1,0:T(8,128)(2,1)S(1)} %collective-permute-done.36.refs_1_, bf16[544,640]{1,0:T(8,128)(2,1)S(1)} %collective-permute-done.41.refs_2_, bf16[544,640]{1,0:T(8,128)(2,1)S(1)} %collective-permute-done.42.refs_3_), custom_call_target="tpu_custom_call" | custom-call | flops 1000000 | tf_op jit(solution)/shard_map/place_joint/pallas_call | solution.py:361
  206.7 3.4 %place_other.1 = (f32[512,3072]{1,0:T(8,128)}, f32[1536]{0:T(1024)}, f32[2048]{0:T(1024)}, f32[512]{0:T(512)}, f32[512]{0:T(512)}, /*index=5*/f32[512]{0:T(512)}, f32[512]{0:T(512)}, f32[512]{0:T(512)}, f32[512]{0:T(512)}) custom-call(bf16[544,640]{1,0:T(8,128)(2,1)S(1)} %broadcast_select_fusion.refs_0_, ...), custom_call_target="tpu_custom_call", output_to_operand_aliasing={{0}: (8, {})} | custom-call | flops 1000000 | tf_op jit(solution)/shard_map/place_other/pallas_call | solution.py:1087
  (132 shorter events, 78.2 us)
Async XLA Ops:
  4.0 13.8 %collective-permute-start.1 = (bf16[272,1024]{1,0:T(8,128)(2,1)}, bf16[272,1024]{1,0:T(8,128)(2,1)S(1)}, u32[]{:S(2)}, u32[]{:S(2)}) collective-permute-start(bf16[272,1024]{1,0:T(8,128)(2,1)} %get-tuple-element.96.refs_0_), channel_id=1, source_target_pairs={{0,4},{2,6},{4,0},{6,2},{8,12},{10,14},{12,8},{14,10},{16,20},{18,... | collective-permute-start | bytes 1671176 | tf_op jit(solution)/shard_map/ppermute | solution.py:901
  5.2 13.4 %collective-permute-start = (bf16[272,1024]{1,0:T(8,128)(2,1)}, bf16[272,1024]{1,0:T(8,128)(2,1)S(1)}, u32[]{:S(2)}, u32[]{:S(2)}) collective-permute-start(bf16[272,1024]{1,0:T(8,128)(2,1)} %get-tuple-element.96.refs_0_), channel_id=1, source_target_pairs={{0,1},{1,0},{2,3},{3,2},{4,5},{5,4},{6,7},{7,6},{8,9},{9,8},{10,11... | collective-permute-start | bytes 1671176 | tf_op jit(solution)/shard_map/ppermute | solution.py:904
  20.2 15.4 %collective-permute-start.4 = (bf16[272,1024]{1,0:T(8,128)(2,1)}, bf16[272,1024]{1,0:T(8,128)(2,1)S(1)}, u32[]{:S(2)}, u32[]{:S(2)}) collective-permute-start(bf16[272,1024]{1,0:T(8,128)(2,1)} %get-tuple-element.96.refs_0_), channel_id=1, source_target_pairs={{0,2},{2,0},{4,6},{6,4},{8,10},{10,8},{12,14},{14,12},{16,18},{18,... | collective-permute-start | bytes 1671176 | tf_op jit(solution)/shard_map/ppermute | solution.py:901
  34.4 17.2 %collective-permute-start.8 = (bf16[512,384]{1,0:T(8,128)(2,1)}, bf16[512,384]{1,0:T(8,128)(2,1)}, u32[]{:S(2)}, u32[]{:S(2)}) collective-permute-start(bf16[512,384]{1,0:T(8,128)(2,1)} %get-tuple-element.107), channel_id=1, source_target_pairs={{0,1},{1,0},{2,3},{3,2},{4,5},{5,4},{6,7},{7,6},{8,9},{9,8},{10,11... | collective-permute-start | bytes 1179656 | tf_op jit(solution)/shard_map/ppermute | solution.py:904
  49.9 22.4 %collective-permute-start.9 = (bf16[512,512]{1,0:T(8,128)(2,1)}, bf16[512,512]{1,0:T(8,128)(2,1)}, u32[]{:S(2)}, u32[]{:S(2)}) collective-permute-start(bf16[512,512]{1,0:T(8,128)(2,1)} %get-tuple-element.112), channel_id=1, source_target_pairs={{0,1},{1,0},{2,3},{3,2},{4,5},{5,4},{6,7},{7,6},{8,9},{9,8},{10,11... | collective-permute-start | bytes 1572872 | tf_op jit(solution)/shard_map/ppermute | solution.py:904
  50.3 26.2 %collective-permute-start.10 = (bf16[512,1024]{1,0:T(8,128)(2,1)}, bf16[512,1024]{1,0:T(8,128)(2,1)}, u32[]{:S(2)}, u32[]{:S(2)}) collective-permute-start(bf16[512,1024]{1,0:T(8,128)(2,1)} %get-tuple-element.116), channel_id=1, source_target_pairs={{0,8},{2,10},{4,12},{6,14},{24,16},{26,18},{28,20},{30,22},{1,9},{... | collective-permute-start | bytes 3145736 | tf_op jit(solution)/shard_map/ppermute | solution.py:908
  71.6 30.6 %collective-permute-start.13 = (bf16[512,2048]{1,0:T(8,128)(2,1)}, bf16[512,2048]{1,0:T(8,128)(2,1)}, u32[]{:S(2)}, u32[]{:S(2)}) collective-permute-start(bf16[512,2048]{1,0:T(8,128)(2,1)} %get-tuple-element.123), channel_id=1, source_target_pairs={{0,2},{2,0},{4,6},{6,4},{8,10},{10,8},{12,14},{14,12},{16,18},{18,... | collective-permute-start | bytes 6291464 | tf_op jit(solution)/shard_map/ppermute | solution.py:901
  77.9 13.9 %collective-permute-start.11 = (bf16[256,1024]{1,0:T(8,128)(2,1)S(1)}, bf16[256,1024]{1,0:T(8,128)(2,1)S(1)}, u32[]{:S(2)}, u32[]{:S(2)}) collective-permute-start(bf16[256,1024]{1,0:T(8,128)(2,1)S(1)} %add_convert_fusion.9), channel_id=1, source_target_pairs={{8,16},{10,18},{12,20},{14,22},{16,8},{18,10},{20,12},{22,14},{9,1... | collective-permute-start | bytes 1572872 | tf_op jit(solution)/shard_map/ppermute | solution.py:908
  81.2 17.5 %collective-permute-start.12 = (bf16[512,512]{1,0:T(8,128)(2,1)}, bf16[512,512]{1,0:T(8,128)(2,1)}, u32[]{:S(2)}, u32[]{:S(2)}) collective-permute-start(bf16[512,512]{1,0:T(8,128)(2,1)} %get-tuple-element.120), channel_id=1, source_target_pairs={{0,8},{2,10},{4,12},{6,14},{24,16},{26,18},{28,20},{30,22},{1,9},{... | collective-permute-start | bytes 1572872 | tf_op jit(solution)/shard_map/ppermute | solution.py:908
  100.0 19.6 %collective-permute-start.17 = (bf16[512,512]{1,0:T(8,128)(2,1)S(1)}, bf16[512,512]{1,0:T(8,128)(2,1)S(1)}, u32[]{:S(2)}, u32[]{:S(2)}) collective-permute-start(bf16[512,512]{1,0:T(8,128)(2,1)S(1)} %add_convert_fusion.6), channel_id=1, source_target_pairs={{8,16},{10,18},{12,20},{14,22},{16,8},{18,10},{20,12},{22,14},{9,1... | collective-permute-start | bytes 1572872 | tf_op jit(solution)/shard_map/ppermute | solution.py:908
  103.9 21.8 %collective-permute-start.19 = (bf16[256,2048]{1,0:T(8,128)(2,1)S(1)}, bf16[256,2048]{1,0:T(8,128)(2,1)S(1)}, u32[]{:S(2)}, u32[]{:S(2)}) collective-permute-start(bf16[256,2048]{1,0:T(8,128)(2,1)S(1)} %fold.1), channel_id=1, source_target_pairs={{0,4},{2,6},{4,0},{6,2},{8,12},{10,14},{12,8},{14,10},{16,20},{18,... | collective-permute-start | bytes 3145736 | tf_op jit(solution)/shard_map/ppermute | solution.py:901
  108.6 14.3 %collective-permute-start.18 = (bf16[256,1024]{1,0:T(8,128)(2,1)S(1)}, bf16[256,1024]{1,0:T(8,128)(2,1)S(1)}, u32[]{:S(2)}, u32[]{:S(2)}) collective-permute-start(bf16[256,1024]{1,0:T(8,128)(2,1)S(1)} %add_convert_fusion.4), channel_id=1, source_target_pairs={{8,0},{10,2},{12,4},{14,6},{16,24},{18,26},{20,28},{22,30},{9,1},{... | collective-permute-start | bytes 1572872 | tf_op jit(solution)/shard_map/ppermute | solution.py:908
  110.0 23.1 %collective-permute-start.21 = (bf16[544,640]{1,0:T(8,128)(2,1)S(1)}, bf16[544,640]{1,0:T(8,128)(2,1)S(1)}, u32[]{:S(2)}, u32[]{:S(2)}) collective-permute-start(bf16[544,640]{1,0:T(8,128)(2,1)S(1)} %copy-done.4), channel_id=1, source_target_pairs={{0,8},{2,10},{4,12},{6,14},{24,16},{26,18},{28,20},{30,22},{1,9},{... | collective-permute-start | bytes 2088968 | tf_op jit(solution)/shard_map/ppermute | solution.py:908
  111.3 25.2 %collective-permute-start.28 = (bf16[544,384]{1,0:T(8,128)(2,1)S(1)}, bf16[544,384]{1,0:T(8,128)(2,1)S(1)}, u32[]{:S(2)}, u32[]{:S(2)}) collective-permute-start(bf16[544,384]{1,0:T(8,128)(2,1)S(1)} %copy-done.13), channel_id=1, source_target_pairs={{0,1},{1,0},{2,3},{3,2},{4,5},{5,4},{6,7},{7,6},{8,9},{9,8},{10,11... | collective-permute-start | bytes 1253384 | tf_op jit(solution)/shard_map/ppermute | solution.py:904
  123.0 19.5 %collective-permute-start.22 = (bf16[512,512]{1,0:T(8,128)(2,1)S(1)}, bf16[512,512]{1,0:T(8,128)(2,1)S(1)}, u32[]{:S(2)}, u32[]{:S(2)}) collective-permute-start(bf16[512,512]{1,0:T(8,128)(2,1)S(1)} %add_convert_fusion.3), channel_id=1, source_target_pairs={{8,0},{10,2},{12,4},{14,6},{16,24},{18,26},{20,28},{22,30},{9,1},{... | collective-permute-start | bytes 1572872 | tf_op jit(solution)/shard_map/ppermute | solution.py:908
  133.2 21.4 %collective-permute-start.27 = (bf16[544,640]{1,0:T(8,128)(2,1)S(1)}, bf16[544,640]{1,0:T(8,128)(2,1)S(1)}, u32[]{:S(2)}, u32[]{:S(2)}) collective-permute-start(bf16[544,640]{1,0:T(8,128)(2,1)S(1)} %add_convert_fusion.1), channel_id=1, source_target_pairs={{8,16},{10,18},{12,20},{14,22},{16,8},{18,10},{20,12},{22,14},{9,1... | collective-permute-start | bytes 2088968 | tf_op jit(solution)/shard_map/ppermute | solution.py:908
  146.2 14.1 %collective-permute-start.37 = (bf16[512,512]{1,0:T(8,128)(2,1)S(1)}, bf16[512,512]{1,0:T(8,128)(2,1)S(1)}, u32[]{:S(2)}, u32[]{:S(2)}) collective-permute-start(bf16[512,512]{1,0:T(8,128)(2,1)S(1)} %broadcast_select_fusion.2.refs_0_), channel_id=1, source_target_pairs={{0,4},{2,6},{4,0},{6,2},{8,12},{10,14},{12,8},{14,10},{16,20},{18,... | collective-permute-start | bytes 1572872 | tf_op jit(solution)/shard_map/ppermute | solution.py:901
  154.8 17.1 %collective-permute-start.34 = (bf16[544,640]{1,0:T(8,128)(2,1)S(1)}, bf16[544,640]{1,0:T(8,128)(2,1)S(1)}, u32[]{:S(2)}, u32[]{:S(2)}) collective-permute-start(bf16[544,640]{1,0:T(8,128)(2,1)S(1)} %add_convert_fusion), channel_id=1, source_target_pairs={{8,0},{10,2},{12,4},{14,6},{16,24},{18,26},{20,28},{22,30},{9,1},{... | collective-permute-start | bytes 2088968 | tf_op jit(solution)/shard_map/ppermute | solution.py:908
  160.2 16.3 %collective-permute-start.35 = (bf16[128,2048]{1,0:T(8,128)(2,1)S(1)}, bf16[128,2048]{1,0:T(8,128)(2,1)S(1)}, u32[]{:S(2)}, u32[]{:S(2)}) collective-permute-start(bf16[128,2048]{1,0:T(8,128)(2,1)S(1)} %get-tuple-element.150), channel_id=1, source_target_pairs={{0,1},{1,0},{2,3},{3,2},{4,5},{5,4},{6,7},{7,6},{8,9},{9,8},{10,11... | collective-permute-start | bytes 1572872 | tf_op jit(solution)/shard_map/ppermute | solution.py:904
  161.6 14.5 %collective-permute-start.43 = (bf16[512,512]{1,0:T(8,128)(2,1)S(1)}, bf16[512,512]{1,0:T(8,128)(2,1)S(1)}, u32[]{:S(2)}, u32[]{:S(2)}) collective-permute-start(bf16[512,512]{1,0:T(8,128)(2,1)S(1)} %broadcast_select_fusion.1.refs_0_), channel_id=1, source_target_pairs={{0,4},{2,6},{4,0},{6,2},{8,12},{10,14},{12,8},{14,10},{16,20},{18,... | collective-permute-start | bytes 1572872 | tf_op jit(solution)/shard_map/ppermute | solution.py:901
  162.7 15.7 %collective-permute-start.38 = (bf16[512,512]{1,0:T(8,128)(2,1)S(1)}, bf16[512,512]{1,0:T(8,128)(2,1)S(1)}, u32[]{:S(2)}, u32[]{:S(2)}) collective-permute-start(bf16[512,512]{1,0:T(8,128)(2,1)S(1)} %broadcast_select_fusion.2.refs_0_), channel_id=1, source_target_pairs={{0,2},{2,0},{4,6},{6,4},{8,10},{10,8},{12,14},{14,12},{16,18},{18,... | collective-permute-start | bytes 1572872 | tf_op jit(solution)/shard_map/ppermute | solution.py:901
  176.1 15.6 %collective-permute-start.36 = (bf16[544,640]{1,0:T(8,128)(2,1)S(1)}, bf16[544,640]{1,0:T(8,128)(2,1)S(1)}, u32[]{:S(2)}, u32[]{:S(2)}) collective-permute-start(bf16[544,640]{1,0:T(8,128)(2,1)S(1)} %broadcast_select_fusion.refs_0_), channel_id=1, source_target_pairs={{0,4},{2,6},{4,0},{6,2},{8,12},{10,14},{12,8},{14,10},{16,20},{18,... | collective-permute-start | bytes 2088968 | tf_op jit(solution)/shard_map/ppermute | solution.py:901
  186.0 14.7 %collective-permute-start.46 = (bf16[544,384]{1,0:T(8,128)(2,1)S(1)}, bf16[544,384]{1,0:T(8,128)(2,1)S(1)}, u32[]{:S(2)}, u32[]{:S(2)}) collective-permute-start(bf16[544,384]{1,0:T(8,128)(2,1)S(1)} %broadcast_select_fusion.5.refs_4_), channel_id=1, source_target_pairs={{0,4},{2,6},{4,0},{6,2},{8,12},{10,14},{12,8},{14,10},{16,20},{18,... | collective-permute-start | bytes 1253384 | tf_op jit(solution)/shard_map/ppermute | solution.py:901
  186.4 16.7 %collective-permute-start.41 = (bf16[544,640]{1,0:T(8,128)(2,1)S(1)}, bf16[544,640]{1,0:T(8,128)(2,1)S(1)}, u32[]{:S(2)}, u32[]{:S(2)}) collective-permute-start(bf16[544,640]{1,0:T(8,128)(2,1)S(1)} %broadcast_select_fusion.refs_0_), channel_id=1, source_target_pairs={{0,2},{2,0},{4,6},{6,4},{8,10},{10,8},{12,14},{14,12},{16,18},{18,... | collective-permute-start | bytes 2088968 | tf_op jit(solution)/shard_map/ppermute | solution.py:901
  (39 other events, 375.1 us)
